TPU v7x, 32 devices: a whole 2x2x4 slice. The times are simulated.
32 devices in a mesh: node: 16 (over z, y, core), rep: 2 (over x).
Axes of the slice: x: 2, y: 2, z: 4, core: 2. Of those that a mesh axis runs over, the one named last changes fastest.
Arguments:
- node_feats: bfloat16 [4096, 256], P(('node', 'rep')), may hold values from -6 to 6
- tile_vals: bfloat16 [16, 2, 16, 2, 128, 128], P('node', 'rep'), may hold values from -0.125 to 0.125
- tile_rows: int32 [16, 2, 16, 2], P('node', 'rep'), may hold values from 0 to 1
- tile_count: int32 [16, 2, 16], P('node', 'rep'), may hold values from 0 to 2, as said below
- w_self: bfloat16 [256, 256], replicated, may hold values from -0.375 to 0.375
- w_neigh: bfloat16 [256, 256], replicated, may hold values from -0.375 to 0.375
- out_grad: bfloat16 [4096, 256], P(('node', 'rep')), may hold values from -0.09375 to 0.09375
Outputs:
- layer_out: bfloat16 [4096, 256], P(('node', 'rep'))
- grad_self: float32 [256, 256], replicated
- grad_neigh: float32 [256, 256], replicated
Inputs may be any that keep to these rules, and one draw needn't show every extreme that they name: `tile_count`: number of live slots of a column block in one device's tile list; every device has a column block with 2 live slots.
All inputs are finite; a program needn't handle non-finite values.
Results may differ from a plain program's by a relative error of at most 0.0055.
Values may be sent and summed in bfloat16 or wider, within the bound.
No kernel may reach another device: no remote copies, remote signals or barrier semaphores. Data moves between devices by JAX's collectives and lax.ppermute only.
A program may use at most 64 MiB of HBM per device.

v0:
```python
import math

import jax
import jax.numpy as jnp
from jax import lax
from jax.sharding import PartitionSpec as P


def column_terms(tile_collection, row_ids, live_count, columns, panel_tiles):
    ncols = tile_collection.shape[0]
    slot_total = tile_collection.shape[1]
    group = math.gcd(ncols, 8)
    nsteps = ncols // group
    tile_grp = tile_collection.reshape((nsteps, group) + tile_collection.shape[1:])
    row_grp = row_ids.reshape((nsteps, group) + row_ids.shape[1:])
    count_grp = live_count.reshape((nsteps, group))
    col_grp = columns.reshape((nsteps, group) + columns.shape[1:])
    slot_position = jnp.arange(slot_total, dtype=jnp.int32)

    def one_group(running, inputs):
        tile_block, row_blk, count_blk, column_block = inputs
        product_terms = jnp.einsum(
            "lhjz,lzd->lhjd", tile_block, column_block, preferred_element_type=jnp.float32
        )
        live = jnp.where(slot_position[None, :] < count_blk[:, None], 1.0, 0.0).astype(jnp.float32)
        masked = product_terms * live[:, :, None, None]
        flat_rows = row_blk.reshape(-1)
        flat_terms = masked.reshape((-1,) + masked.shape[2:])
        return (running.at[flat_rows].add(flat_terms), None)

    start_sum = jnp.zeros((panel_tiles, tile_collection.shape[2], columns.shape[2]), jnp.float32)
    running, unused = lax.scan(one_group, start_sum, (tile_grp, row_grp, count_grp, col_grp))
    return running


def local(node_feats, tile_vals, tile_rows, tile_count, w_self, w_neigh, out_grad):
    tile_collection = tile_vals[0, 0]
    row_ids = tile_rows[0, 0]
    live_count = tile_count[0, 0]
    block_rows = node_feats.shape[0]
    panel_tiles = lax.axis_size("rep")
    width = node_feats.shape[1]
    shard_rows = lax.all_gather(node_feats, "node", axis=0, tiled=True)
    ncols = shard_rows.shape[0] // block_rows
    columns = shard_rows.reshape(ncols, block_rows, width)
    panel = column_terms(tile_collection, row_ids, live_count, columns, panel_tiles)
    aggregate = lax.psum_scatter(
        panel.reshape(panel_tiles * block_rows, width), "rep", scatter_dimension=0, tiled=True
    ).astype(jnp.bfloat16)
    pre = jnp.dot(node_feats, w_self, preferred_element_type=jnp.float32) + jnp.dot(
        aggregate, w_neigh, preferred_element_type=jnp.float32
    )
    sigma = jax.nn.sigmoid(pre)
    layer_out = (pre * sigma).astype(jnp.bfloat16)
    delta = (out_grad.astype(jnp.float32) * sigma * (1.0 + pre * (1.0 - sigma))).astype(
        jnp.bfloat16
    )
    local_self = lax.dot_general(
        node_feats, delta, (((0,), (0,)), ((), ())), preferred_element_type=jnp.float32
    )
    local_neigh = lax.dot_general(
        aggregate, delta, (((0,), (0,)), ((), ())), preferred_element_type=jnp.float32
    )
    grad_self, grad_neigh = lax.psum((local_self, local_neigh), ("node", "rep"))
    return (layer_out, grad_self, grad_neigh)


def solution(mesh):
    placed = (
        P(("node", "rep"), None),
        P("node", "rep", None, None, None, None),
        P("node", "rep", None, None),
        P("node", "rep", None),
        P(),
        P(),
        P(("node", "rep"), None),
    )
    return jax.shard_map(
        local,
        mesh=mesh,
        in_specs=placed,
        out_specs=(P(("node", "rep"), None), P(), P()),
        check_vma=False,
    )
```

profile of v0, /device:TPU:0, one launch (start us, length us, event | category | flops | bytes accessed | tf_op | source)
XLA Modules:
  0.0 215.5 jit_solution(2512210940800126964)
XLA Ops:
  7.2 0.0 copy-start
  7.2 0.0 all-gather.2.cloned.1.call-start
  7.2 0.7 all-gather.2.cloned.1.call-update
  7.9 0.0 reduce-scatter.2.cloned.1.call-start
  8.0 0.5 broadcast.61
  8.5 1.3 reduce.3
  9.8 0.1 reshape_squeeze.11
  9.9 0.8 copy.15
  10.6 40.2 %all-gather.2.cloned.1.call-done = bf16[2048,256]{1,0:T(8,128)(2,1)} async-done(((bf16[128,256]{1,0:T(8,128)(2,1)}), bf16[2048,256]{1,0:T(8,128)(2,1)}) %all-gather.2.cloned.1.call-update) | async-done | bytes 1048592 | tf_op jit(solution)/shard_map/all_gather | solution.py:43
  50.9 0.0 copy-start.2
  50.9 0.0 copy-start.3
  50.9 0.0 copy-start.4
  50.9 8.0 %while.11 = (s32[]{:T(128)}, f32[2,128,256]{2,1,0:T(8,128)S(1)}, s32[2,8,2]{2,1,0:T(8,128)S(1)}, bf16[2,8,2,128,128]{4,3,2,1,0:T(8,128)(2,1)}, bf16[2,8,128,256]...) while((s32[]{:T(128)}, f32[2,128,256]{2,1,0:T(8,128)S(1)}, s32[2,8,2]{2,1,0:T(8,128)S(1)}, ...), condition=%wide.region_2.3_spmd.clone, body=%wide.region_0.2_spmd.clone.sunk | while | flops 135266384 | bytes 9438965 | solution.py:32
  50.9 0.1 fusion.27
  51.0 1.6 convolution_multiply_fusion.2
  52.7 0.1 reshape.105
  52.8 2.2 %scatter_fusion = f32[2,128,256]{2,1,0:T(8,128)S(1)} fusion(f32[2,128,256]{2,1,0:T(8,128)S(1)} %get-tuple-element.134, s32[16]{0:T(128)S(1)} %fusion.25, f32[16,128,256]{2,1,0:T(8,128)S(1)} %bitcast.35), kind=kCustom, calls=%fused_computation.clone.clone.1 | custom fusion | flops 524288 | bytes 6291520 | tf_op jit(solution)/shard_map/while/body/eval_jaxpr/scatter-add | solution.py:29
  55.0 0.1 fusion.27
  55.0 1.6 convolution_multiply_fusion.2
  56.7 0.1 reshape.105
  56.8 2.2 %scatter_fusion = f32[2,128,256]{2,1,0:T(8,128)S(1)} fusion(f32[2,128,256]{2,1,0:T(8,128)S(1)} %get-tuple-element.134, s32[16]{0:T(128)S(1)} %fusion.25, f32[16,128,256]{2,1,0:T(8,128)S(1)} %bitcast.35), kind=kCustom, calls=%fused_computation.clone.clone.1 | custom fusion | flops 524288 | bytes 6291520 | tf_op jit(solution)/shard_map/while/body/eval_jaxpr/scatter-add | solution.py:29
  59.0 0.0 copy-start.1
  59.0 0.7 copy-done.1
  59.7 0.0 reduce-scatter.2.cloned.1.call-update
  59.7 0.0 all-reduce.3.cloned.1.call-start
  59.7 0.0 copy-done.2
  59.8 0.0 copy-done.3
  59.8 0.2 fusion.13
  59.9 10.5 %reduce-scatter.2.cloned.1.call-done = f32[128,256]{1,0:T(8,128)} async-done(((f32[256,256]{1,0:T(8,128)}), f32[128,256]{1,0:T(8,128)}) %reduce-scatter.2.cloned.1.call-update) | async-done | bytes 131088 | tf_op jit(solution)/shard_map/reduce_scatter | solution.py:47
  70.4 0.0 copy-done
  70.4 1.7 multiply_convert_fusion.1
  72.1 0.0 copy-done.4
  72.1 1.0 convolution_bitcast_fusion
  73.1 1.8 fusion.10
  74.9 0.0 all-reduce.3.cloned.1.call-update
  75.0 130.6 %all-reduce.3.cloned.1.call-done = (f32[256,256]{0,1:T(8,128)}, f32[256,256]{1,0:T(8,128)}) async-done(((f32[256,256]{0,1:T(8,128)}, f32[256,256]{1,0:T(8,128)}), (f32[256,256]{0,1:T(8,128)}, f32[256,256]{1,0:T(8,128)})) %all-reduce.3.cloned.1.call-update) | async-done | bytes 524304 | tf_op jit(solution)/shard_map/psum | solution.py:64
  205.6 1.8 copy.13
  207.3 1.7 copy.27
  (7 shorter events, 0.1 us)
Async XLA Ops:
  7.2 63.2 %copy-start = (bf16[256,256]{1,0:T(8,128)(2,1)S(1)}, bf16[256,256]{1,0:T(8,128)(2,1)}, u32[]{:S(2)}) copy-start(bf16[256,256]{1,0:T(8,128)(2,1)} %param.14) | copy-start | bytes 393220
  7.2 43.7 %all-gather.2.cloned.1.call-start = ((), (), s32[]{:S(2)}) async-start(), calls=%async_computation.1 | async-start | bytes 1114112 | tf_op jit(solution)/shard_map/all_gather | solution.py:43
  7.9 62.5 %reduce-scatter.2.cloned.1.call-start = ((), (), s32[]{:S(2)}) async-start(), calls=%async_computation.2 | async-start | bytes 393216 | tf_op jit(solution)/shard_map/reduce_scatter | solution.py:47
  50.9 8.9 %copy-start.2 = (bf16[128,256]{1,0:T(8,128)(2,1)S(1)}, bf16[128,256]{1,0:T(8,128)(2,1)}, u32[]{:S(2)}) copy-start(bf16[128,256]{1,0:T(8,128)(2,1)} %param.9) | copy-start | bytes 196612
  50.9 8.9 %copy-start.3 = (bf16[256,256]{1,0:T(8,128)(2,1)S(1)}, bf16[256,256]{1,0:T(8,128)(2,1)}, u32[]{:S(2)}) copy-start(bf16[256,256]{1,0:T(8,128)(2,1)} %param.13) | copy-start | bytes 393220
  50.9 21.3 %copy-start.4 = (bf16[128,256]{1,0:T(8,128)(2,1)S(1)}, bf16[128,256]{1,0:T(8,128)(2,1)}, u32[]{:S(2)}) copy-start(bf16[128,256]{1,0:T(8,128)(2,1)} %param.15) | copy-start | bytes 196612
  59.0 0.7 copy-start.1
  59.7 145.9 %all-reduce.3.cloned.1.call-start = ((), (), s32[]{:S(2)}) async-start(), calls=%async_computation.3 | async-start | bytes 1048576 | tf_op jit(solution)/shard_map/psum | solution.py:64
Sparse Core Ops, SparseCore 0:
  10.2 40.6 all-gather.1
  59.8 10.5 reduce-scatter.1
  77.4 128.1 all-reduce.2
where the time goes:
time: 216 us
  waiting for transfers between devices  182 us (84%)
  between operations  13.8 us (6%)
  matrix products  7.94 us (4%)
  other arithmetic  5.82 us (3%)
  local copies, waits for them, and re-layouts  5.74 us (3%)
    psum x1, waiting for transfers between devices, local(): grad_self, grad_neigh = lax.psum((local_self, local_neigh), ('node', 'rep'))  131 us
    all_gather x1, waiting for transfers between devices, local(): shard_rows = lax.all_gather(node_feats, 'node', axis=0, tiled=True)  40.2 us
    reduce_scatter x1, waiting for transfers between devices, local(): lax.psum_scatter(panel.reshape(panel_tiles * block_rows, width), 'rep', s...  10.5 us
    unnamed x14, local copies, waits for them, and re-layouts  5.45 us
    scatter-add x2, other arithmetic, one_group(): return (running.at[flat_rows].add(flat_terms), None)  4.35 us
  transfers between devices with their start and end apart: 3, of which 3 were waited for; matrix products, arithmetic and copies ran while one was open for 1% of the time, Pallas kernels for 0%

commit v1 on v0

v1 whole, which is shorter than its diff:
```python
import functools

import jax
import jax.numpy as jnp
from jax import lax
from jax.experimental import pallas as pl
from jax.experimental.pallas import tpu as pltpu
from jax.sharding import PartitionSpec as P

VMEM = pl.BlockSpec(memory_space=pltpu.VMEM)
SMEM = pl.BlockSpec(memory_space=pltpu.SMEM)
F32 = jnp.float32
BF16 = jnp.bfloat16


def bits_below(size):
    return [1 << i for i in reversed(range(size.bit_length() - 1))]


def doubling_masks(bits):
    masks = [0]
    for bit in bits:
        masks = masks + [mask ^ bit for mask in masks]
    return masks


def swap(x, n_node, n_rep, even, odd):
    pairs = []
    for node in range(n_node):
        flip_node, flip_rep = odd if node & 1 else even
        for rep in range(n_rep):
            pairs.append((node * n_rep + rep, (node ^ flip_node) * n_rep + (rep ^ flip_rep)))
    return lax.ppermute(x, ("node", "rep"), pairs)


def tile_sums(masks_even, masks_odd, other_core, seeded, *refs):
    if seeded:
        place, rows, count, tiles, columns, seed, out = refs
    else:
        place, rows, count, tiles, columns, out = refs
    node, rep = place[0], place[1]
    n_blocks = len(masks_even)
    tile = tiles.shape[2]
    panel_tiles = out.shape[0] // tile
    slots = tiles.shape[1]
    core = node & 1
    origin = node ^ 1 if other_core else node
    swapped = core == (1 if not other_core else 0)

    def pair_terms(step, even, odd):
        groups = [origin ^ even, origin ^ odd]
        block = columns[pl.ds(pl.multiple_of(step * 2 * tile, 2 * tile), 2 * tile), :]
        for k in range(panel_tiles):
            target = rep ^ k
            total = None
            for s in range(slots):
                parts = []
                for group in groups:
                    live = jnp.logical_and(s < count[group], rows[group * slots + s] == target)
                    weight = jnp.where(live, 1.0, 0.0).astype(F32)
                    value = tiles[group, s]
                    parts.append(jnp.where(jnp.full(value.shape, weight) > 0.5, value, jnp.zeros_like(value)))
                left = jnp.concatenate(parts, axis=1)
                term = jnp.dot(left, block, preferred_element_type=F32)
                total = term if total is None else total + term
            out[k * tile : (k + 1) * tile, :] += total

    out[...] = seed[...] if seeded else jnp.zeros_like(out)
    for step in range(n_blocks // 2):
        pair = [
            jnp.where(swapped, masks_odd[2 * step + i], masks_even[2 * step + i]) for i in (0, 1)
        ]
        pair_terms(step, pair[0], pair[1])


def update(own, got, feats, w_self, w_neigh, out_grad, layer_out, send):
    aggregate = (own[...] + got[...].astype(F32)).astype(BF16)
    pre = jnp.dot(feats[...], w_self[...], preferred_element_type=F32) + jnp.dot(
        aggregate, w_neigh[...], preferred_element_type=F32
    )
    sigma = jax.nn.sigmoid(pre)
    layer_out[...] = (pre * sigma).astype(BF16)
    delta = (out_grad[...].astype(F32) * sigma * (1.0 + pre * (1.0 - sigma))).astype(BF16)
    rows = feats.shape[0]
    send[:rows, :] = delta
    send[rows:, :] = aggregate


def chip_gradient(place, feats, other_feats, mine, other, out):
    rows = feats.shape[0]
    first = jnp.full(feats.shape, place[0] & 1) == 0
    left = jnp.concatenate(
        [
            jnp.where(first, feats[...], mine[rows:, :]),
            jnp.where(first, other_feats[:rows, :], other[rows:, :]),
        ],
        axis=0,
    )
    delta = jnp.concatenate([mine[:rows, :], other[:rows, :]], axis=0)
    out[...] = lax.dot_general(
        left, delta, (((0,), (0,)), ((), ())), preferred_element_type=F32
    ).astype(out.dtype)


def call(body, out_shape, specs, flops, nbytes):
    return pl.pallas_call(
        body,
        out_shape=out_shape,
        in_specs=specs,
        out_specs=jax.tree.map(lambda _: VMEM, out_shape),
        cost_estimate=pl.CostEstimate(flops=flops, bytes_accessed=nbytes, transcendentals=0),
        compiler_params=pltpu.CompilerParams(vmem_limit_bytes=24 * 1024 * 1024),
    )


def local(n_node, n_rep, node_feats, tile_vals, tile_rows, tile_count, w_self, w_neigh, out_grad):
    tiles = tile_vals[0, 0]
    row_ids = tile_rows[0, 0].reshape(-1)
    live_count = tile_count[0, 0]
    rows, width = node_feats.shape
    place = jnp.stack([lax.axis_index("node"), lax.axis_index("rep")]).astype(jnp.int32)

    chip_bits = bits_below(n_node)[:-1]
    turned = chip_bits[-1:] + chip_bits[:-1]
    rep_bits = bits_below(n_rep)

    held = node_feats
    for even, odd in zip(chip_bits, turned, strict=True):
        held = jnp.concatenate([held, swap(held, n_node, n_rep, (even, 0), (odd, 0))], axis=0)
    other_held = swap(held, n_node, n_rep, (1, 0), (1, 0))

    masks_even, masks_odd = doubling_masks(chip_bits), doubling_masks(turned)
    panel = jax.ShapeDtypeStruct((n_rep * rows, width), F32)
    flops = held.shape[0] * n_rep * rows * width * 4
    nbytes = tiles.size + held.size * 2 + panel.size * 4
    own = call(
        functools.partial(tile_sums, masks_even, masks_odd, False, False),
        panel, [SMEM] * 3 + [VMEM] * 2, flops, nbytes,
    )(place, row_ids, live_count, tiles, held)
    total = call(
        functools.partial(tile_sums, masks_even, masks_odd, True, True),
        panel, [SMEM] * 3 + [VMEM] * 3, flops, nbytes,
    )(place, row_ids, live_count, tiles, other_held, own)

    for bit in rep_bits[:-1]:
        half = bit * rows
        got = swap(total[half:].astype(BF16), n_node, n_rep, (0, bit), (0, bit))
        total = total[:half] + got.astype(F32)
    got = swap(total[rows:].astype(BF16), n_node, n_rep, (0, 1), (0, 1))

    layer_out, mine = call(
        update,
        (jax.ShapeDtypeStruct((rows, width), BF16), jax.ShapeDtypeStruct((2 * rows, width), BF16)),
        [VMEM] * 6, 4 * rows * width * width, 1 << 20,
    )(total[:rows], got, node_feats, w_self, w_neigh, out_grad)
    other = swap(mine, n_node, n_rep, (1, 0), (1, 0))
    grad = call(
        chip_gradient, jax.ShapeDtypeStruct((width, width), BF16),
        [SMEM] + [VMEM] * 4, 4 * rows * width * width, 1 << 20,
    )(place, node_feats, other_held[:rows], mine, other)

    steps = [(0, bit) for bit in rep_bits] + [(bit, 0) for bit in reversed(chip_bits)]
    half = len(rep_bits) + 1
    first, rest = steps[:half], steps[half:]
    order_even = first + rest
    order_odd = first[::-1] + rest[::-1]
    for even, odd in zip(order_even, order_odd, strict=True):
        got = swap(grad.astype(BF16), n_node, n_rep, even, odd)
        grad = grad.astype(BF16).astype(F32) + got.astype(F32)
    other_grad = swap(grad, n_node, n_rep, (1, 0), (1, 0))
    first_core = (place[0] & 1) == 0
    grad_self = jnp.where(first_core, grad, other_grad)
    grad_neigh = jnp.where(first_core, other_grad, grad)
    return (layer_out, grad_self, grad_neigh)


def solution(mesh):
    placed = (
        P(("node", "rep"), None),
        P("node", "rep", None, None, None, None),
        P("node", "rep", None, None),
        P("node", "rep", None),
        P(),
        P(),
        P(("node", "rep"), None),
    )
    return jax.shard_map(
        functools.partial(local, mesh.shape["node"], mesh.shape["rep"]),
        mesh=mesh,
        in_specs=placed,
        out_specs=(P(("node", "rep"), None), P(), P()),
        check_vma=False,
    )
```

time: 216 us -> 55.6 us (0.26)
  waiting for transfers between devices: 182 us -> 28.8 us
  starting transfers between devices: 0.12 us -> 18.1 us
  between operations: 13.8 us -> 0.81 us
  matrix products: 7.94 us -> 0 us
  local copies, waits for them, and re-layouts: 5.74 us -> 1.59 us
  other arithmetic: 5.82 us -> 1.91 us
  Pallas kernels: 0 us -> 3.6 us
    psum x1 -> x0, waiting for transfers between devices: 131 us -> none  [local(): grad_self, grad_neigh = lax.psum((local_self, local_neigh), ('node', 'rep'))]
    all_gather x1 -> x0, waiting for transfers between devices: 40.2 us -> none  [local(): shard_rows = lax.all_gather(node_feats, 'node', axis=0, tiled=True)]
    ppermute x0 -> x11, waiting for transfers between devices: none -> 28.8 us  [swap(): return lax.ppermute(x, ('node', 'rep'), pairs)]
    ppermute x0 -> x11, starting transfers between devices: none -> 18.1 us  [swap(): return lax.ppermute(x, ('node', 'rep'), pairs)]
    reduce_scatter x1 -> x0, waiting for transfers between devices: 10.5 us -> none  [local(): lax.psum_scatter(panel.reshape(panel_tiles * block_rows, width), 'rep', s...]
    dot_general x6 -> x0, matrix products: 7.94 us -> none  [the longest x2 3.26 us: one_group(): jnp.einsum('lhjz,lzd->lhjd', tile_block, column_block, preferred_element_...]
    scatter-add x2 -> x0, other arithmetic: 4.35 us -> none  [one_group(): return (running.at[flat_rows].add(flat_terms), None)]
    unnamed x14 -> x18, local copies, waits for them, and re-layouts: 5.45 us -> 1.46 us
  transfers between devices with their start and end apart: 3 -> 11, of which waited for: 3 -> 10; matrix products, arithmetic and copies ran while one was open for 1% -> 1% of each run, Pallas kernels for 0% -> 2%
where the time goes in v1:
time: 55.6 us; the launch traced here: 54.8 us
  waiting for transfers between devices  28.8 us (52%)
  starting transfers between devices  18.1 us (33%)
  Pallas kernels  3.6 us (6%)
  other arithmetic  1.91 us (3%)
  local copies, waits for them, and re-layouts  1.59 us (3%)
  between operations  0.81 us (1%)
    ppermute x11, waiting for transfers between devices, swap(): return lax.ppermute(x, ('node', 'rep'), pairs)  28.8 us
    ppermute x11, starting transfers between devices, swap(): return lax.ppermute(x, ('node', 'rep'), pairs)  18.1 us
    unnamed x18, local copies, waits for them, and re-layouts  1.46 us
  transfers between devices with their start and end apart: 11, of which 10 were waited for; matrix products, arithmetic and copies ran while one was open for 1% of the time, Pallas kernels for 2%

profile of v1, /device:TPU:0, one launch (start us, length us, event | category | flops | bytes accessed | tf_op | source)
XLA Modules:
  0.0 54.8 jit_solution(17319503824750577250)
XLA Ops:
  0.6 0.0 copy-start.1
  0.6 0.0 copy-start
  0.6 4.1 %collective-permute-start = (bf16[128,256]{1,0:T(8,128)(2,1)}, bf16[128,256]{1,0:T(8,128)(2,1)S(1)}, u32[]{:S(2)}, u32[]{:S(2)}) collective-permute-start(bf16[128,256]{1,0:T(8,128)(2,1)} %feats.3), channel_id=1, source_target_pairs={{0,16},{1,17},{2,6},{3,7},{4,20},{5,21},{6,2},{7,3},{8,24},{9,25},... | collective-permute-start | bytes 196616 | tf_op jit(solution)/shard_map/ppermute | solution.py:33
  4.8 2.5 %collective-permute-done = bf16[128,256]{1,0:T(8,128)(2,1)S(1)} collective-permute-done((bf16[128,256]{1,0:T(8,128)(2,1)}, bf16[128,256]{1,0:T(8,128)(2,1)S(1)}, u32[]{:S(2)}, u32[]{:S(2)}) %collective-permute-start) | collective-permute-done | bytes 65568 | tf_op jit(solution)/shard_map/ppermute | solution.py:33
  7.2 0.8 %pad_maximum_fusion.1 = bf16[256,256]{1,0:T(8,128)(2,1)S(1)} fusion(bf16[128,256]{1,0:T(8,128)(2,1)S(1)} %collective-permute-done, bf16[128,256]{1,0:T(8,128)(2,1)} %feats.3), kind=kLoop, calls=%fused_computation.6 | loop fusion | flops 262144 | bytes 262144 | tf_op jit(solution)/shard_map/concatenate | solution.py:129
  8.1 2.0 %collective-permute-start.1 = (bf16[256,256]{1,0:T(8,128)(2,1)S(1)}, bf16[256,256]{1,0:T(8,128)(2,1)S(1)}, u32[]{:S(2)}, u32[]{:S(2)}) collective-permute-start(bf16[256,256]{1,0:T(8,128)(2,1)S(1)} %pad_maximum_fusion.1), channel_id=1, source_target_pairs={{0,8},{1,9},{2,18},{3,19},{4,12},{5,13},{6,22},{7,23},{8,0},{9,1},... | collective-permute-start | bytes 393224 | tf_op jit(solution)/shard_map/ppermute | solution.py:33
  10.0 3.3 %collective-permute-done.1 = bf16[256,256]{1,0:T(8,128)(2,1)S(1)} collective-permute-done((bf16[256,256]{1,0:T(8,128)(2,1)S(1)}, bf16[256,256]{1,0:T(8,128)(2,1)S(1)}, u32[]{:S(2)}, u32[]{:S(2)}) %collective-permute-start.1) | collective-permute-done | bytes 131104 | tf_op jit(solution)/shard_map/ppermute | solution.py:33
  13.3 0.0 copy-done.1
  13.4 2.0 %collective-permute-start.2 = (bf16[512,256]{1,0:T(8,128)(2,1)S(1)}, bf16[512,256]{1,0:T(8,128)(2,1)S(1)}, u32[]{:S(2)}, u32[]{:S(2)}) collective-permute-start(bf16[512,256]{1,0:T(8,128)(2,1)S(1)} %pad_maximum_fusion), channel_id=1, source_target_pairs={{0,4},{1,5},{2,10},{3,11},{4,0},{5,1},{6,14},{7,15},{8,12},{9,13},... | collective-permute-start | bytes 786440 | tf_op jit(solution)/shard_map/ppermute | solution.py:33
  15.4 4.4 %collective-permute-done.2 = bf16[512,256]{1,0:T(8,128)(2,1)S(1)} collective-permute-done((bf16[512,256]{1,0:T(8,128)(2,1)S(1)}, bf16[512,256]{1,0:T(8,128)(2,1)S(1)}, u32[]{:S(2)}, u32[]{:S(2)}) %collective-permute-start.2) | collective-permute-done | bytes 262176 | tf_op jit(solution)/shard_map/ppermute | solution.py:33
  19.8 0.1 collective-permute-start.3
  19.9 0.0 copy-start.6
  19.9 0.7 %copy-done.6 = s32[1,1,16,2]{2,3,1,0:T(2,128)S(1)} copy-done((s32[1,1,16,2]{2,3,1,0:T(2,128)S(1)}, s32[1,1,16,2]{2,3,1,0:T(2,128)}, u32[]{:S(2)}) %copy-start.6) | copy-done | bytes 152
  20.6 0.1 copy.11
  20.7 0.1 reshape_squeeze.3.refs_1_
  20.8 0.1 pad_add_fusion.refs_0_.place
  20.8 0.0 copy-start.5
  20.8 0.0 copy-done
  20.8 0.7 %copy-done.5 = s32[1,1,16]{2,1,0:T(1,128)S(1)} copy-done((s32[1,1,16]{2,1,0:T(1,128)S(1)}, s32[1,1,16]{2,1,0:T(1,128)}, u32[]{:S(2)}) %copy-start.5) | copy-done | bytes 88
  21.5 1.0 %shard_map.94.refs_5_ = f32[256,256]{1,0:T(8,128)S(1)} custom-call(s32[2]{0:T(128)S(1)} %pad_add_fusion.refs_0_.place, s32[32]{0:T(128)S(1)} %reshape_squeeze.3.refs_1_, s32[16]{0:T(128)S(1)} %bitcast.8, bf16[16,2,128,128]{3,2,1,0:T(8,128)(2,1)S(1)} %bitcast.6, bf16[1024,256]{1,0:T(8,128)(2,1)S(1)} %constant_dynamic-update-slice_fusion.refs_4_), custom_call_target="tpu_custom_call" | custom-call | flops 268435456 | bytes 1310720 | tf_op jit(solution)/shard_map/pallas_call | solution.py:136
  22.5 0.0 collective-permute-done.3.refs_4_
  22.5 1.0 %shard_map.95 = f32[256,256]{1,0:T(8,128)S(1)} custom-call(s32[2]{0:T(128)S(1)} %pad_add_fusion.refs_0_.place, s32[32]{0:T(128)S(1)} %reshape_squeeze.3.refs_1_, s32[16]{0:T(128)S(1)} %bitcast.9, bf16[16,2,128,128]{3,2,1,0:T(8,128)(2,1)S(1)} %bitcast.7, bf16[1024,256]{1,0:T(8,128)(2,1)S(1)} %collective-permute-done.3.refs_4_, f32[256,256]{1,0:T(8,128)S(1)} %shard_map.94.refs_5_), custom_call_target="tpu_custom_call" | custom-call | flops 268435456 | bytes 1310720 | tf_op jit(solution)/shard_map/pallas_call | solution.py:140
  23.5 0.0 copy-start.4
  23.5 0.0 copy-start.2
  23.6 0.0 copy-start.3
  23.6 1.9 %collective-permute-start.4 = (bf16[128,256]{1,0:T(8,128)(2,1)S(1)}, bf16[128,256]{1,0:T(8,128)(2,1)S(1)}, u32[]{:S(2)}, u32[]{:S(2)}) collective-permute-start(bf16[128,256]{1,0:T(8,128)(2,1)S(1)} %slice.17), channel_id=1, source_target_pairs={{0,1},{1,0},{2,3},{3,2},{4,5},{5,4},{6,7},{7,6},{8,9},{9,8},{10,11... | collective-permute-start | bytes 196616 | tf_op jit(solution)/shard_map/ppermute | solution.py:33
  25.5 2.7 %collective-permute-done.4.got = bf16[128,256]{1,0:T(8,128)(2,1)S(1)} collective-permute-done((bf16[128,256]{1,0:T(8,128)(2,1)S(1)}, bf16[128,256]{1,0:T(8,128)(2,1)S(1)}, u32[]{:S(2)}, u32[]{:S(2)}) %collective-permute-start.4) | collective-permute-done | bytes 65568 | tf_op jit(solution)/shard_map/ppermute | solution.py:33
  28.3 0.0 copy-done.4
  28.3 0.0 copy-done.2
  28.3 0.0 copy-done.3
  28.3 0.8 %shard_map.96 = (bf16[128,256]{1,0:T(8,128)(2,1)}, bf16[256,256]{1,0:T(8,128)(2,1)S(1)}) custom-call(f32[128,256]{1,0:T(8,128)S(1)} %slice.13.own, bf16[128,256]{1,0:T(8,128)(2,1)S(1)} %collective-permute-done.4.got, bf16[128,256]{1,0:T(8,128)(2,1)S(1)} %copy-done.1, bf16[256,256]{1,0:T(8,128)(2,1)S(1)} %copy-done.2, bf16[256,256]{1,0:T(8,128)(2,1)S(1)} %copy-done.3, ...), custom_call_target="tpu_custom_call" | custom-call | flops 33554432 | bytes 1048576 | tf_op jit(solution)/shard_map/pallas_call | solution.py:151
  29.1 0.0 collective-permute-start.5
  29.1 1.3 %collective-permute-done.5.other = bf16[256,256]{1,0:T(8,128)(2,1)S(1)} collective-permute-done((bf16[256,256]{1,0:T(8,128)(2,1)S(1)}, bf16[256,256]{1,0:T(8,128)(2,1)S(1)}, u32[]{:S(2)}, u32[]{:S(2)}) %collective-permute-start.5) | collective-permute-done | bytes 131104 | tf_op jit(solution)/shard_map/ppermute | solution.py:33
  30.5 0.8 %shard_map.97 = bf16[256,256]{1,0:T(8,128)(2,1)S(1)} custom-call(s32[2]{0:T(128)S(1)} %pad_add_fusion.refs_0_.place, bf16[128,256]{1,0:T(8,128)(2,1)S(1)} %copy-done.1, bf16[128,256]{1,0:T(8,128)(2,1)S(1)} %slice.15.other_feats, bf16[256,256]{1,0:T(8,128)(2,1)S(1)} %get-tuple-element.6.mine, bf16[256,256]{1,0:T(8,128)(2,1)S(1)} %collective-permute-done.5.other), custom_call_target="tpu_custom_call" | custom-call | flops 33554432 | bytes 1048576 | tf_op jit(solution)/shard_map/pallas_call | solution.py:157
  31.2 1.8 %collective-permute-start.6 = (bf16[256,256]{1,0:T(8,128)(2,1)S(1)}, bf16[256,256]{1,0:T(8,128)(2,1)S(1)}, u32[]{:S(2)}, u32[]{:S(2)}) collective-permute-start(bf16[256,256]{1,0:T(8,128)(2,1)S(1)} %shard_map.97), channel_id=1, source_target_pairs={{0,1},{1,0},{2,6},{3,7},{4,5},{5,4},{6,2},{7,3},{8,9},{9,8},{10,14... | collective-permute-start | bytes 393224 | tf_op jit(solution)/shard_map/ppermute | solution.py:33
  33.0 3.2 %collective-permute-done.6 = bf16[256,256]{1,0:T(8,128)(2,1)S(1)} collective-permute-done((bf16[256,256]{1,0:T(8,128)(2,1)S(1)}, bf16[256,256]{1,0:T(8,128)(2,1)S(1)}, u32[]{:S(2)}, u32[]{:S(2)}) %collective-permute-start.6) | collective-permute-done | bytes 131104 | tf_op jit(solution)/shard_map/ppermute | solution.py:33
  36.3 1.8 %collective-permute-start.7 = (bf16[256,256]{1,0:T(8,128)(2,1)S(1)}, bf16[256,256]{1,0:T(8,128)(2,1)S(1)}, u32[]{:S(2)}, u32[]{:S(2)}) collective-permute-start(bf16[256,256]{1,0:T(8,128)(2,1)S(1)} %add_convert_fusion.2), channel_id=1, source_target_pairs={{0,4},{1,5},{2,3},{3,2},{4,0},{5,1},{6,7},{7,6},{8,12},{9,13},{10,... | collective-permute-start | bytes 393224 | tf_op jit(solution)/shard_map/ppermute | solution.py:33
  38.1 3.2 %collective-permute-done.7 = bf16[256,256]{1,0:T(8,128)(2,1)S(1)} collective-permute-done((bf16[256,256]{1,0:T(8,128)(2,1)S(1)}, bf16[256,256]{1,0:T(8,128)(2,1)S(1)}, u32[]{:S(2)}, u32[]{:S(2)}) %collective-permute-start.7) | collective-permute-done | bytes 131104 | tf_op jit(solution)/shard_map/ppermute | solution.py:33
  41.4 1.6 %collective-permute-start.8 = (bf16[256,256]{1,0:T(8,128)(2,1)S(1)}, bf16[256,256]{1,0:T(8,128)(2,1)S(1)}, u32[]{:S(2)}, u32[]{:S(2)}) collective-permute-start(bf16[256,256]{1,0:T(8,128)(2,1)S(1)} %add_convert_fusion.1), channel_id=1, source_target_pairs={{0,8},{1,9},{2,18},{3,19},{4,12},{5,13},{6,22},{7,23},{8,0},{9,1},... | collective-permute-start | bytes 393224 | tf_op jit(solution)/shard_map/ppermute | solution.py:33
  43.0 3.4 %collective-permute-done.8 = bf16[256,256]{1,0:T(8,128)(2,1)S(1)} collective-permute-done((bf16[256,256]{1,0:T(8,128)(2,1)S(1)}, bf16[256,256]{1,0:T(8,128)(2,1)S(1)}, u32[]{:S(2)}, u32[]{:S(2)}) %collective-permute-start.8) | collective-permute-done | bytes 131104 | tf_op jit(solution)/shard_map/ppermute | solution.py:33
  46.4 2.7 %collective-permute-start.9 = (bf16[256,256]{1,0:T(8,128)(2,1)S(1)}, bf16[256,256]{1,0:T(8,128)(2,1)S(1)}, u32[]{:S(2)}, u32[]{:S(2)}) collective-permute-start(bf16[256,256]{1,0:T(8,128)(2,1)S(1)} %add_convert_fusion), channel_id=1, source_target_pairs={{0,16},{1,17},{2,10},{3,11},{4,20},{5,21},{6,14},{7,15},{8,24},{9,... | collective-permute-start | bytes 393224 | tf_op jit(solution)/shard_map/ppermute | solution.py:33
  49.2 3.2 %collective-permute-done.9 = bf16[256,256]{1,0:T(8,128)(2,1)S(1)} collective-permute-done((bf16[256,256]{1,0:T(8,128)(2,1)S(1)}, bf16[256,256]{1,0:T(8,128)(2,1)S(1)}, u32[]{:S(2)}, u32[]{:S(2)}) %collective-permute-start.9) | collective-permute-done | bytes 131104 | tf_op jit(solution)/shard_map/ppermute | solution.py:33
  52.4 0.1 collective-permute-start.10
  52.5 1.5 %collective-permute-done.10 = f32[256,256]{1,0:T(8,128)S(1)} collective-permute-done((f32[256,256]{1,0:T(8,128)S(1)}, f32[256,256]{1,0:T(8,128)S(1)}, u32[]{:S(2)}, u32[]{:S(2)}) %collective-permute-start.10) | collective-permute-done | bytes 262176 | tf_op jit(solution)/shard_map/ppermute | solution.py:33
  54.0 0.8 %broadcast_select_fusion = (f32[256,256]{1,0:T(8,128)}, f32[256,256]{1,0:T(8,128)}) fusion(f32[256,256]{1,0:T(8,128)S(1)} %collective-permute-done.10, pred[]{:T(512)S(6)} %eq.3, bf16[256,256]{1,0:T(8,128)(2,1)S(1)} %collective-permute-done.9, bf16[256,256]{1,0:T(8,128)(2,1)S(1)} %add_convert_fusion), kind=kLoop, calls=%fused_computation.7 | loop fusion | flops 327680 | bytes 1048577 | tf_op jit(solution)/shard_map/jit(_where)/select_n | solution.py:173
  (12 shorter events, 0.2 us)
Async XLA Ops:
  0.6 12.7 %copy-start.1 = (bf16[128,256]{1,0:T(8,128)(2,1)S(1)}, bf16[128,256]{1,0:T(8,128)(2,1)}, u32[]{:S(2)}) copy-start(bf16[128,256]{1,0:T(8,128)(2,1)} %feats.3) | copy-start | bytes 196612
  0.6 20.2 %copy-start = (bf16[1,1,16,2,128,128]{5,4,3,2,1,0:T(8,128)(2,1)S(1)}, bf16[1,1,16,2,128,128]{5,4,3,2,1,0:T(8,128)(2,1)}, u32[]{:S(2)}) copy-start(bf16[1,1,16,2,128,128]{5,4,3,2,1,0:T(8,128)(2,1)} %param.8) | copy-start | bytes 3145732
  0.6 6.6 %collective-permute-start = (bf16[128,256]{1,0:T(8,128)(2,1)}, bf16[128,256]{1,0:T(8,128)(2,1)S(1)}, u32[]{:S(2)}, u32[]{:S(2)}) collective-permute-start(bf16[128,256]{1,0:T(8,128)(2,1)} %feats.3), channel_id=1, source_target_pairs={{0,16},{1,17},{2,6},{3,7},{4,20},{5,21},{6,2},{7,3},{8,24},{9,25},... | collective-permute-start | bytes 196616 | tf_op jit(solution)/shard_map/ppermute | solution.py:33
  8.1 5.3 %collective-permute-start.1 = (bf16[256,256]{1,0:T(8,128)(2,1)S(1)}, bf16[256,256]{1,0:T(8,128)(2,1)S(1)}, u32[]{:S(2)}, u32[]{:S(2)}) collective-permute-start(bf16[256,256]{1,0:T(8,128)(2,1)S(1)} %pad_maximum_fusion.1), channel_id=1, source_target_pairs={{0,8},{1,9},{2,18},{3,19},{4,12},{5,13},{6,22},{7,23},{8,0},{9,1},... | collective-permute-start | bytes 393224 | tf_op jit(solution)/shard_map/ppermute | solution.py:33
  13.4 6.4 %collective-permute-start.2 = (bf16[512,256]{1,0:T(8,128)(2,1)S(1)}, bf16[512,256]{1,0:T(8,128)(2,1)S(1)}, u32[]{:S(2)}, u32[]{:S(2)}) collective-permute-start(bf16[512,256]{1,0:T(8,128)(2,1)S(1)} %pad_maximum_fusion), channel_id=1, source_target_pairs={{0,4},{1,5},{2,10},{3,11},{4,0},{5,1},{6,14},{7,15},{8,12},{9,13},... | collective-permute-start | bytes 786440 | tf_op jit(solution)/shard_map/ppermute | solution.py:33
  19.8 2.7 %collective-permute-start.3 = (bf16[1024,256]{1,0:T(8,128)(2,1)S(1)}, bf16[1024,256]{1,0:T(8,128)(2,1)S(1)}, u32[]{:S(2)}, u32[]{:S(2)}) collective-permute-start(bf16[1024,256]{1,0:T(8,128)(2,1)S(1)} %constant_dynamic-update-slice_fusion.refs_4_), channel_id=1, source_target_pairs={{0,2},{1,3},{2,0},{3,1},{4,6},{5,7},{6,4},{7,5},{8,10},{9,11},{10,... | collective-permute-start | bytes 1572872 | tf_op jit(solution)/shard_map/ppermute | solution.py:33
  19.9 0.7 %copy-start.6 = (s32[1,1,16,2]{2,3,1,0:T(2,128)S(1)}, s32[1,1,16,2]{2,3,1,0:T(2,128)}, u32[]{:S(2)}) copy-start(s32[1,1,16,2]{2,3,1,0:T(2,128)} %param.9) | copy-start | bytes 388
  20.8 0.7 %copy-start.5 = (s32[1,1,16]{2,1,0:T(1,128)S(1)}, s32[1,1,16]{2,1,0:T(1,128)}, u32[]{:S(2)}) copy-start(s32[1,1,16]{2,1,0:T(1,128)} %param.10) | copy-start | bytes 196
  23.5 4.7 %copy-start.4 = (bf16[128,256]{1,0:T(8,128)(2,1)S(1)}, bf16[128,256]{1,0:T(8,128)(2,1)}, u32[]{:S(2)}) copy-start(bf16[128,256]{1,0:T(8,128)(2,1)} %out_grad.1) | copy-start | bytes 196612
  23.5 4.7 %copy-start.2 = (bf16[256,256]{1,0:T(8,128)(2,1)S(1)}, bf16[256,256]{1,0:T(8,128)(2,1)}, u32[]{:S(2)}) copy-start(bf16[256,256]{1,0:T(8,128)(2,1)} %w_self.1) | copy-start | bytes 393220
  23.6 4.7 %copy-start.3 = (bf16[256,256]{1,0:T(8,128)(2,1)S(1)}, bf16[256,256]{1,0:T(8,128)(2,1)}, u32[]{:S(2)}) copy-start(bf16[256,256]{1,0:T(8,128)(2,1)} %w_neigh.1) | copy-start | bytes 393220
  23.6 4.7 %collective-permute-start.4 = (bf16[128,256]{1,0:T(8,128)(2,1)S(1)}, bf16[128,256]{1,0:T(8,128)(2,1)S(1)}, u32[]{:S(2)}, u32[]{:S(2)}) collective-permute-start(bf16[128,256]{1,0:T(8,128)(2,1)S(1)} %slice.17), channel_id=1, source_target_pairs={{0,1},{1,0},{2,3},{3,2},{4,5},{5,4},{6,7},{7,6},{8,9},{9,8},{10,11... | collective-permute-start | bytes 196616 | tf_op jit(solution)/shard_map/ppermute | solution.py:33
  29.1 1.3 %collective-permute-start.5 = (bf16[256,256]{1,0:T(8,128)(2,1)S(1)}, bf16[256,256]{1,0:T(8,128)(2,1)S(1)}, u32[]{:S(2)}, u32[]{:S(2)}) collective-permute-start(bf16[256,256]{1,0:T(8,128)(2,1)S(1)} %get-tuple-element.6.mine), channel_id=1, source_target_pairs={{0,2},{1,3},{2,0},{3,1},{4,6},{5,7},{6,4},{7,5},{8,10},{9,11},{10,... | collective-permute-start | bytes 393224 | tf_op jit(solution)/shard_map/ppermute | solution.py:33
  31.2 5.0 %collective-permute-start.6 = (bf16[256,256]{1,0:T(8,128)(2,1)S(1)}, bf16[256,256]{1,0:T(8,128)(2,1)S(1)}, u32[]{:S(2)}, u32[]{:S(2)}) collective-permute-start(bf16[256,256]{1,0:T(8,128)(2,1)S(1)} %shard_map.97), channel_id=1, source_target_pairs={{0,1},{1,0},{2,6},{3,7},{4,5},{5,4},{6,2},{7,3},{8,9},{9,8},{10,14... | collective-permute-start | bytes 393224 | tf_op jit(solution)/shard_map/ppermute | solution.py:33
  36.3 5.0 %collective-permute-start.7 = (bf16[256,256]{1,0:T(8,128)(2,1)S(1)}, bf16[256,256]{1,0:T(8,128)(2,1)S(1)}, u32[]{:S(2)}, u32[]{:S(2)}) collective-permute-start(bf16[256,256]{1,0:T(8,128)(2,1)S(1)} %add_convert_fusion.2), channel_id=1, source_target_pairs={{0,4},{1,5},{2,3},{3,2},{4,0},{5,1},{6,7},{7,6},{8,12},{9,13},{10,... | collective-permute-start | bytes 393224 | tf_op jit(solution)/shard_map/ppermute | solution.py:33
  41.4 5.0 %collective-permute-start.8 = (bf16[256,256]{1,0:T(8,128)(2,1)S(1)}, bf16[256,256]{1,0:T(8,128)(2,1)S(1)}, u32[]{:S(2)}, u32[]{:S(2)}) collective-permute-start(bf16[256,256]{1,0:T(8,128)(2,1)S(1)} %add_convert_fusion.1), channel_id=1, source_target_pairs={{0,8},{1,9},{2,18},{3,19},{4,12},{5,13},{6,22},{7,23},{8,0},{9,1},... | collective-permute-start | bytes 393224 | tf_op jit(solution)/shard_map/ppermute | solution.py:33
  46.4 5.9 %collective-permute-start.9 = (bf16[256,256]{1,0:T(8,128)(2,1)S(1)}, bf16[256,256]{1,0:T(8,128)(2,1)S(1)}, u32[]{:S(2)}, u32[]{:S(2)}) collective-permute-start(bf16[256,256]{1,0:T(8,128)(2,1)S(1)} %add_convert_fusion), channel_id=1, source_target_pairs={{0,16},{1,17},{2,10},{3,11},{4,20},{5,21},{6,14},{7,15},{8,24},{9,... | collective-permute-start | bytes 393224 | tf_op jit(solution)/shard_map/ppermute | solution.py:33
  52.4 1.6 %collective-permute-start.10 = (f32[256,256]{1,0:T(8,128)S(1)}, f32[256,256]{1,0:T(8,128)S(1)}, u32[]{:S(2)}, u32[]{:S(2)}) collective-permute-start(f32[256,256]{1,0:T(8,128)S(1)} %convert_add_fusion), channel_id=1, source_target_pairs={{0,2},{1,3},{2,0},{3,1},{4,6},{5,7},{6,4},{7,5},{8,10},{9,11},{10,... | collective-permute-start | bytes 786440 | tf_op jit(solution)/shard_map/ppermute | solution.py:33

commit v2 on v1

v2 whole, which is shorter than its diff:
```python
import functools

import jax
import jax.numpy as jnp
from jax import lax
from jax.experimental import pallas as pl
from jax.experimental.pallas import tpu as pltpu
from jax.sharding import PartitionSpec as P

VMEM = pl.BlockSpec(memory_space=pltpu.VMEM)
SMEM = pl.BlockSpec(memory_space=pltpu.SMEM)
F32 = jnp.float32
BF16 = jnp.bfloat16


def bits_below(size):
    return [1 << i for i in reversed(range(size.bit_length() - 1))]


def doubling_masks(bits):
    masks = [0]
    for bit in bits:
        masks = masks + [mask ^ bit for mask in masks]
    return masks


def swap(x, n_node, n_rep, even, odd):
    pairs = []
    for node in range(n_node):
        flip_node, flip_rep = odd if node & 1 else even
        for rep in range(n_rep):
            pairs.append((node * n_rep + rep, (node ^ flip_node) * n_rep + (rep ^ flip_rep)))
    return lax.ppermute(x, ("node", "rep"), pairs)


def tile_sums(masks_even, masks_odd, other_core, seeded, *refs):
    if seeded:
        place, rows, count, tiles, columns, seed, out = refs
    else:
        place, rows, count, tiles, columns, out = refs
    node = place[0]
    base = place[1] - lax.rem(place[1], 2)
    tile = tiles.shape[2]
    panel_tiles = out.shape[0] // tile
    slots = tiles.shape[1]
    origin = node ^ 1 if other_core else node
    odd = (origin & 1) == 1

    total = seed[...] if seeded else None
    for step in range(len(masks_even) // 2):
        groups = [
            origin ^ jnp.where(odd, masks_odd[2 * step + i], masks_even[2 * step + i]) for i in (0, 1)
        ]
        lefts = []
        for s in range(slots):
            for k in range(panel_tiles):
                parts = []
                for group in groups:
                    live = jnp.logical_and(s < count[group], rows[group * slots + s] == base ^ k)
                    value = tiles[group, s]
                    chosen = jnp.full(value.shape, live.astype(F32)) > 0.5
                    parts.append(jnp.where(chosen, value, jnp.zeros_like(value)))
                lefts.append(jnp.concatenate(parts, axis=1))
        block = columns[step * 2 * tile : (step + 1) * 2 * tile, :]
        terms = jnp.dot(jnp.concatenate(lefts, axis=0), block, preferred_element_type=F32)
        for s in range(slots):
            term = terms[s * panel_tiles * tile : (s + 1) * panel_tiles * tile]
            total = term if total is None else total + term
    out[...] = total.astype(out.dtype)


def update(place, own, got, feats, far_feats, out_grad, far_out_grad, w_self, w_neigh, layer_out, keep, send):
    rows = feats.shape[0]
    first_rep = jnp.full((rows, feats.shape[1]), lax.rem(place[1], 2)) == 0

    def in_order(mine, far):
        return jnp.concatenate([jnp.where(first_rep, mine, far), jnp.where(first_rep, far, mine)], axis=0)

    x = in_order(feats[...], far_feats[...])
    g = in_order(out_grad[...], far_out_grad[...]).astype(F32)
    aggregate = (own[...].astype(F32) + got[...].astype(F32)).astype(BF16)
    pre = jnp.dot(x, w_self[...], preferred_element_type=F32) + jnp.dot(
        aggregate, w_neigh[...], preferred_element_type=F32
    )
    sigma = jax.nn.sigmoid(pre)
    value = (pre * sigma).astype(BF16)
    layer_out[...] = jnp.where(first_rep, value[:rows], value[rows:])
    delta = (g * sigma * (1.0 + pre * (1.0 - sigma))).astype(BF16)
    first_core = jnp.full(x.shape, place[0] & 1) == 0
    for left, out in ((jnp.where(first_core, x, aggregate), keep), (jnp.where(first_core, aggregate, x), send)):
        out[...] = lax.dot_general(
            left, delta, (((0,), (0,)), ((), ())), preferred_element_type=F32
        ).astype(out.dtype)


def copied(x_ref, out_ref):
    out_ref[...] = x_ref[...]


def call(body, out_shape, specs, flops, nbytes):
    return pl.pallas_call(
        body,
        out_shape=out_shape,
        in_specs=specs,
        out_specs=jax.tree.map(lambda _: VMEM, out_shape),
        cost_estimate=pl.CostEstimate(flops=flops, bytes_accessed=nbytes, transcendentals=0),
        compiler_params=pltpu.CompilerParams(vmem_limit_bytes=24 * 1024 * 1024),
    )


def local(n_node, n_rep, node_feats, tile_vals, tile_rows, tile_count, w_self, w_neigh, out_grad):
    tiles = tile_vals[0, 0]
    row_ids = tile_rows[0, 0].reshape(-1)
    live_count = tile_count[0, 0]
    rows, width = node_feats.shape
    place = jnp.stack([lax.axis_index("node"), lax.axis_index("rep")]).astype(jnp.int32)

    chip_bits = bits_below(n_node)[:-1]
    turned = chip_bits[-1:] + chip_bits[:-1]
    rep_bits = bits_below(n_rep)

    got = swap(node_feats, n_node, n_rep, (chip_bits[0], 0), (turned[0], 0))
    feats = call(copied, jax.ShapeDtypeStruct(node_feats.shape, BF16), [VMEM], 0, node_feats.size * 4)(node_feats)
    feats, got, place, row_ids, live_count = lax.optimization_barrier((feats, got, place, row_ids, live_count))
    held = jnp.concatenate([feats, got], axis=0)
    far = swap(jnp.concatenate([feats, out_grad], axis=0), n_node, n_rep, (0, 1), (0, 1))
    for even, odd in zip(chip_bits[1:], turned[1:], strict=True):
        held = jnp.concatenate([held, swap(held, n_node, n_rep, (even, 0), (odd, 0))], axis=0)
    other_held = swap(held, n_node, n_rep, (1, 0), (1, 0))

    masks_even, masks_odd = doubling_masks(chip_bits), doubling_masks(turned)
    flops = held.shape[0] * n_rep * rows * width * 4
    nbytes = tiles.size + held.size * 2 + n_rep * rows * width * 4
    own = call(
        functools.partial(tile_sums, masks_even, masks_odd, False, False),
        jax.ShapeDtypeStruct((n_rep * rows, width), F32), [SMEM] * 3 + [VMEM] * 2, flops, nbytes,
    )(place, row_ids, live_count, tiles, held)
    total = call(
        functools.partial(tile_sums, masks_even, masks_odd, True, True),
        jax.ShapeDtypeStruct((n_rep * rows, width), BF16 if n_rep == 2 else F32),
        [SMEM] * 3 + [VMEM] * 3, flops, nbytes,
    )(place, row_ids, live_count, tiles, other_held, own)

    for bit in rep_bits[:-1]:
        half = bit * rows
        got = swap(total[half:].astype(BF16), n_node, n_rep, (0, bit), (0, bit))
        total = total[:half].astype(F32) + got.astype(F32)
    total = total.astype(BF16)
    got = swap(total, n_node, n_rep, (0, 1), (0, 1))

    grad_shape = jax.ShapeDtypeStruct((width, width), F32)
    layer_out, keep, send = call(
        update,
        (jax.ShapeDtypeStruct((rows, width), BF16), grad_shape, grad_shape),
        [SMEM] + [VMEM] * 8, 16 * rows * width * width, 1 << 20,
    )(place, total, got, feats, far[:rows], out_grad, far[rows:], w_self, w_neigh)
    grad = keep + swap(send, n_node, n_rep, (1, 0), (1, 0))

    order_even = chip_bits[::-1]
    order_odd = chip_bits[:1] + order_even[:-1]
    steps = [((0, bit), (0, bit)) for bit in rep_bits[:-1]]
    steps += [((even, 0), (odd, 0)) for even, odd in zip(order_even, order_odd, strict=True)]
    for even, odd in steps:
        part = grad.astype(BF16)
        grad = part.astype(F32) + swap(part, n_node, n_rep, even, odd).astype(F32)
    other_grad = swap(grad, n_node, n_rep, (1, 0), (1, 0))
    first_core = (place[0] & 1) == 0
    grad_self = jnp.where(first_core, grad, other_grad)
    grad_neigh = jnp.where(first_core, other_grad, grad)
    return (layer_out, grad_self, grad_neigh)


def solution(mesh):
    placed = (
        P(("node", "rep"), None),
        P("node", "rep", None, None, None, None),
        P("node", "rep", None, None),
        P("node", "rep", None),
        P(),
        P(),
        P(("node", "rep"), None),
    )
    return jax.shard_map(
        functools.partial(local, mesh.shape["node"], mesh.shape["rep"]),
        mesh=mesh,
        in_specs=placed,
        out_specs=(P(("node", "rep"), None), P(), P()),
        check_vma=False,
    )
```

time: 55.6 us -> 50.9 us (0.915); the launches traced: 54.8 us -> 50.7 us
  starting transfers between devices: 18.1 us -> 16.4 us
  waiting for transfers between devices: 28.8 us -> 27.2 us
  other arithmetic: 1.91 us -> 1.09 us
    ppermute x11, starting transfers between devices: 18.1 us -> 16.4 us  [swap(): return lax.ppermute(x, ('node', 'rep'), pairs)]
    ppermute x11, waiting for transfers between devices: 28.8 us -> 27.2 us  [swap(): return lax.ppermute(x, ('node', 'rep'), pairs)]
    concatenate x2 -> x1, other arithmetic: 0.87 us -> 0.02 us  [local(): jnp.concatenate([held, swap(held, n_node, n_rep, (even, 0), (odd, 0))], a...]
  transfers between devices with their start and end apart: 11 -> 11, of which waited for: 10 -> 10; matrix products, arithmetic and copies ran while one was open for 1% -> 1% of each run, Pallas kernels for 2% -> 4%
where the time goes in v2:
time: 50.9 us; the launch traced here: 50.7 us
  waiting for transfers between devices  27.2 us (53%)
  starting transfers between devices  16.4 us (32%)
  Pallas kernels  3.49 us (7%)
  local copies, waits for them, and re-layouts  1.78 us (3%)
  other arithmetic  1.09 us (2%)
  between operations  0.8 us (2%)
    ppermute x11, waiting for transfers between devices, swap(): return lax.ppermute(x, ('node', 'rep'), pairs)  27.2 us
    ppermute x11, starting transfers between devices, swap(): return lax.ppermute(x, ('node', 'rep'), pairs)  16.4 us
    unnamed x18, local copies, waits for them, and re-layouts  1.66 us
    pallas_call x1, Pallas kernels, local(): call(update, (jax.ShapeDtypeStruct((rows, width), BF16), grad_shape, grad...  1.5 us
  transfers between devices with their start and end apart: 11, of which 10 were waited for; matrix products, arithmetic and copies ran while one was open for 1% of the time, Pallas kernels for 4%

profile of v2, /device:TPU:0, one launch (start us, length us, event | category | flops | bytes accessed | tf_op | source)
XLA Modules:
  0.0 50.7 jit_solution(16603023624166030088)
XLA Ops:
  0.6 0.0 copy-start.1
  0.6 4.1 %collective-permute-start = (bf16[128,256]{1,0:T(8,128)(2,1)}, bf16[128,256]{1,0:T(8,128)(2,1)S(1)}, u32[]{:S(2)}, u32[]{:S(2)}) collective-permute-start(bf16[128,256]{1,0:T(8,128)(2,1)} %x_ref.1), channel_id=1, source_target_pairs={{0,16},{1,17},{2,6},{3,7},{4,20},{5,21},{6,2},{7,3},{8,24},{9,25},... | collective-permute-start | bytes 196616 | tf_op jit(solution)/shard_map/ppermute | solution.py:33
  4.7 0.0 copy-start.4
  4.7 0.9 %copy-done.4 = bf16[128,256]{1,0:T(8,128)(2,1)S(1)} copy-done((bf16[128,256]{1,0:T(8,128)(2,1)S(1)}, bf16[128,256]{1,0:T(8,128)(2,1)}, u32[]{:S(2)}) %copy-start.4) | copy-done | bytes 65560
  5.6 0.0 copy-start.6
  5.6 0.0 copy-start
  5.6 0.7 %copy-done.6 = s32[1,1,16,2]{2,3,1,0:T(2,128)S(1)} copy-done((s32[1,1,16,2]{2,3,1,0:T(2,128)S(1)}, s32[1,1,16,2]{2,3,1,0:T(2,128)}, u32[]{:S(2)}) %copy-start.6) | copy-done | bytes 152
  6.3 0.1 copy.11
  6.4 0.1 reshape_squeeze.3.refs_1_
  6.5 0.1 pad_add_fusion.refs_0_.place
  6.5 0.7 %collective-permute-done = bf16[128,256]{1,0:T(8,128)(2,1)S(1)} collective-permute-done((bf16[128,256]{1,0:T(8,128)(2,1)}, bf16[128,256]{1,0:T(8,128)(2,1)S(1)}, u32[]{:S(2)}, u32[]{:S(2)}) %collective-permute-start) | collective-permute-done | bytes 65568 | tf_op jit(solution)/shard_map/ppermute | solution.py:33
  7.2 0.0 copy-done.1
  7.2 2.0 %collective-permute-start.1 = (bf16[256,256]{1,0:T(8,128)(2,1)S(1)}, bf16[256,256]{1,0:T(8,128)(2,1)S(1)}, u32[]{:S(2)}, u32[]{:S(2)}) collective-permute-start(bf16[256,256]{1,0:T(8,128)(2,1)S(1)} %get-tuple-element.24), channel_id=1, source_target_pairs={{0,8},{1,9},{2,18},{3,19},{4,12},{5,13},{6,22},{7,23},{8,0},{9,1},... | collective-permute-start | bytes 393224 | tf_op jit(solution)/shard_map/ppermute | solution.py:33
  9.2 3.3 %collective-permute-done.1 = bf16[256,256]{1,0:T(8,128)(2,1)S(1)} collective-permute-done((bf16[256,256]{1,0:T(8,128)(2,1)S(1)}, bf16[256,256]{1,0:T(8,128)(2,1)S(1)}, u32[]{:S(2)}, u32[]{:S(2)}) %collective-permute-start.1) | collective-permute-done | bytes 131104 | tf_op jit(solution)/shard_map/ppermute | solution.py:33
  12.5 2.0 %collective-permute-start.2 = (bf16[512,256]{1,0:T(8,128)(2,1)S(1)}, bf16[512,256]{1,0:T(8,128)(2,1)S(1)}, u32[]{:S(2)}, u32[]{:S(2)}) collective-permute-start(bf16[512,256]{1,0:T(8,128)(2,1)S(1)} %pad_maximum_fusion), channel_id=1, source_target_pairs={{0,4},{1,5},{2,10},{3,11},{4,0},{5,1},{6,14},{7,15},{8,12},{9,13},... | collective-permute-start | bytes 786440 | tf_op jit(solution)/shard_map/ppermute | solution.py:33
  14.5 4.4 %collective-permute-done.2 = bf16[512,256]{1,0:T(8,128)(2,1)S(1)} collective-permute-done((bf16[512,256]{1,0:T(8,128)(2,1)S(1)}, bf16[512,256]{1,0:T(8,128)(2,1)S(1)}, u32[]{:S(2)}, u32[]{:S(2)}) %collective-permute-start.2) | collective-permute-done | bytes 262176 | tf_op jit(solution)/shard_map/ppermute | solution.py:33
  19.0 0.1 collective-permute-start.3
  19.1 0.0 copy-start.5
  19.1 1.9 %collective-permute-start.5 = (bf16[256,256]{1,0:T(8,128)(2,1)S(1)}, bf16[256,256]{1,0:T(8,128)(2,1)S(1)}, u32[]{:S(2)}, u32[]{:S(2)}) collective-permute-start(bf16[256,256]{1,0:T(8,128)(2,1)S(1)} %get-tuple-element.23), channel_id=1, source_target_pairs={{0,1},{1,0},{2,3},{3,2},{4,5},{5,4},{6,7},{7,6},{8,9},{9,8},{10,11... | collective-permute-start | bytes 393224 | tf_op jit(solution)/shard_map/ppermute | solution.py:33
  21.0 0.0 copy-done
  21.0 0.0 copy-done.5
  21.0 1.0 %shard_map.95.refs_5_ = f32[256,256]{1,0:T(8,128)S(1)} custom-call(s32[2]{0:T(128)S(1)} %pad_add_fusion.refs_0_.place, s32[32]{0:T(128)S(1)} %reshape_squeeze.3.refs_1_, s32[16]{0:T(128)S(1)} %bitcast.11, bf16[16,2,128,128]{3,2,1,0:T(8,128)(2,1)S(1)} %bitcast.8, bf16[1024,256]{1,0:T(8,128)(2,1)S(1)} %constant_dynamic-update-slice_fusion.refs_4_), custom_call_target="tpu_custom_call" | custom-call | flops 268435456 | bytes 1310720 | tf_op jit(solution)/shard_map/pallas_call | solution.py:134
  22.0 0.0 collective-permute-done.3.refs_4_
  22.0 1.0 %shard_map.96.own = bf16[256,256]{1,0:T(8,128)(2,1)S(1)} custom-call(s32[2]{0:T(128)S(1)} %pad_add_fusion.refs_0_.place, s32[32]{0:T(128)S(1)} %reshape_squeeze.3.refs_1_, s32[16]{0:T(128)S(1)} %bitcast.12, bf16[16,2,128,128]{3,2,1,0:T(8,128)(2,1)S(1)} %bitcast.9, bf16[1024,256]{1,0:T(8,128)(2,1)S(1)} %collective-permute-done.3.refs_4_, ...), custom_call_target="tpu_custom_call" | custom-call | flops 268435456 | bytes 1310720 | tf_op jit(solution)/shard_map/pallas_call | solution.py:138
  23.0 0.0 copy-start.2
  23.0 0.0 copy-start.3
  23.1 0.9 %collective-permute-start.4 = (bf16[256,256]{1,0:T(8,128)(2,1)S(1)}, bf16[256,256]{1,0:T(8,128)(2,1)S(1)}, u32[]{:S(2)}, u32[]{:S(2)}) collective-permute-start(bf16[256,256]{1,0:T(8,128)(2,1)S(1)} %shard_map.96.own), channel_id=1, source_target_pairs={{0,1},{1,0},{2,3},{3,2},{4,5},{5,4},{6,7},{7,6},{8,9},{9,8},{10,11... | collective-permute-start | bytes 393224 | tf_op jit(solution)/shard_map/ppermute | solution.py:33
  23.9 1.2 %collective-permute-done.5 = bf16[256,256]{1,0:T(8,128)(2,1)S(1)} collective-permute-done((bf16[256,256]{1,0:T(8,128)(2,1)S(1)}, bf16[256,256]{1,0:T(8,128)(2,1)S(1)}, u32[]{:S(2)}, u32[]{:S(2)}) %collective-permute-start.5) | collective-permute-done | bytes 131104 | tf_op jit(solution)/shard_map/ppermute | solution.py:33
  25.1 3.6 %collective-permute-done.4.got = bf16[256,256]{1,0:T(8,128)(2,1)S(1)} collective-permute-done((bf16[256,256]{1,0:T(8,128)(2,1)S(1)}, bf16[256,256]{1,0:T(8,128)(2,1)S(1)}, u32[]{:S(2)}, u32[]{:S(2)}) %collective-permute-start.4) | collective-permute-done | bytes 131104 | tf_op jit(solution)/shard_map/ppermute | solution.py:33
  28.7 0.0 copy-done.2
  28.7 0.0 copy-done.3
  28.7 1.5 %shard_map.97 = (bf16[128,256]{1,0:T(8,128)(2,1)}, f32[256,256]{1,0:T(8,128)S(1)}, f32[256,256]{1,0:T(8,128)S(1)}) custom-call(s32[2]{0:T(128)S(1)} %pad_add_fusion.refs_0_.place, bf16[256,256]{1,0:T(8,128)(2,1)S(1)} %shard_map.96.own, bf16[256,256]{1,0:T(8,128)(2,1)S(1)} %collective-permute-done.4.got, bf16[128,256]{1,0:T(8,128)(2,1)S(1)} %shard_map.94.feats, ...), custom_call_target="tpu_custom_call" | custom-call | flops 134217728 | bytes 1048576 | tf_op jit(solution)/shard_map/pallas_call | solution.py:152
  30.2 0.0 collective-permute-start.6
  30.2 1.5 %collective-permute-done.6 = f32[256,256]{1,0:T(8,128)S(1)} collective-permute-done((f32[256,256]{1,0:T(8,128)S(1)}, f32[256,256]{1,0:T(8,128)S(1)}, u32[]{:S(2)}, u32[]{:S(2)}) %collective-permute-start.6) | collective-permute-done | bytes 262176 | tf_op jit(solution)/shard_map/ppermute | solution.py:33
  31.7 1.6 %collective-permute-start.7 = (bf16[256,256]{1,0:T(8,128)(2,1)S(1)}, bf16[256,256]{1,0:T(8,128)(2,1)S(1)}, u32[]{:S(2)}, u32[]{:S(2)}) collective-permute-start(bf16[256,256]{1,0:T(8,128)(2,1)S(1)} %add_convert_fusion.2), channel_id=1, source_target_pairs={{0,4},{1,5},{2,18},{3,19},{4,0},{5,1},{6,22},{7,23},{8,12},{9,13},... | collective-permute-start | bytes 393224 | tf_op jit(solution)/shard_map/ppermute | solution.py:33
  33.3 3.4 %collective-permute-done.7 = bf16[256,256]{1,0:T(8,128)(2,1)S(1)} collective-permute-done((bf16[256,256]{1,0:T(8,128)(2,1)S(1)}, bf16[256,256]{1,0:T(8,128)(2,1)S(1)}, u32[]{:S(2)}, u32[]{:S(2)}) %collective-permute-start.7) | collective-permute-done | bytes 131104 | tf_op jit(solution)/shard_map/ppermute | solution.py:33
  36.8 1.3 %collective-permute-start.8 = (bf16[256,256]{1,0:T(8,128)(2,1)S(1)}, bf16[256,256]{1,0:T(8,128)(2,1)S(1)}, u32[]{:S(2)}, u32[]{:S(2)}) collective-permute-start(bf16[256,256]{1,0:T(8,128)(2,1)S(1)} %add_convert_fusion.1), channel_id=1, source_target_pairs={{0,8},{1,9},{2,6},{3,7},{4,12},{5,13},{6,2},{7,3},{8,0},{9,1},{10,... | collective-permute-start | bytes 393224 | tf_op jit(solution)/shard_map/ppermute | solution.py:33
  38.2 3.7 %collective-permute-done.8 = bf16[256,256]{1,0:T(8,128)(2,1)S(1)} collective-permute-done((bf16[256,256]{1,0:T(8,128)(2,1)S(1)}, bf16[256,256]{1,0:T(8,128)(2,1)S(1)}, u32[]{:S(2)}, u32[]{:S(2)}) %collective-permute-start.8) | collective-permute-done | bytes 131104 | tf_op jit(solution)/shard_map/ppermute | solution.py:33
  41.9 2.5 %collective-permute-start.9 = (bf16[256,256]{1,0:T(8,128)(2,1)S(1)}, bf16[256,256]{1,0:T(8,128)(2,1)S(1)}, u32[]{:S(2)}, u32[]{:S(2)}) collective-permute-start(bf16[256,256]{1,0:T(8,128)(2,1)S(1)} %add_convert_fusion), channel_id=1, source_target_pairs={{0,16},{1,17},{2,10},{3,11},{4,20},{5,21},{6,14},{7,15},{8,24},{9,... | collective-permute-start | bytes 393224 | tf_op jit(solution)/shard_map/ppermute | solution.py:33
  44.4 3.9 %collective-permute-done.9 = bf16[256,256]{1,0:T(8,128)(2,1)S(1)} collective-permute-done((bf16[256,256]{1,0:T(8,128)(2,1)S(1)}, bf16[256,256]{1,0:T(8,128)(2,1)S(1)}, u32[]{:S(2)}, u32[]{:S(2)}) %collective-permute-start.9) | collective-permute-done | bytes 131104 | tf_op jit(solution)/shard_map/ppermute | solution.py:33
  48.3 0.1 collective-permute-start.10
  48.4 1.5 %collective-permute-done.10 = f32[256,256]{1,0:T(8,128)S(1)} collective-permute-done((f32[256,256]{1,0:T(8,128)S(1)}, f32[256,256]{1,0:T(8,128)S(1)}, u32[]{:S(2)}, u32[]{:S(2)}) %collective-permute-start.10) | collective-permute-done | bytes 262176 | tf_op jit(solution)/shard_map/ppermute | solution.py:33
  49.9 0.8 %broadcast_select_fusion = (f32[256,256]{1,0:T(8,128)}, f32[256,256]{1,0:T(8,128)}) fusion(f32[256,256]{1,0:T(8,128)S(1)} %collective-permute-done.10, pred[]{:T(512)} %bitcast.4, bf16[256,256]{1,0:T(8,128)(2,1)S(1)} %collective-permute-done.9, bf16[256,256]{1,0:T(8,128)(2,1)S(1)} %add_convert_fusion), kind=kLoop, calls=%fused_computation.7 | loop fusion | flops 327680 | bytes 1048577 | tf_op jit(solution)/shard_map/jit(_where)/select_n | solution.py:169
  (12 shorter events, 0.2 us)
Async XLA Ops:
  0.6 6.6 %copy-start.1 = (bf16[128,256]{1,0:T(8,128)(2,1)S(1)}, bf16[128,256]{1,0:T(8,128)(2,1)}, u32[]{:S(2)}) copy-start(bf16[128,256]{1,0:T(8,128)(2,1)} %out_grad.1) | copy-start | bytes 196612
  0.6 6.6 %collective-permute-start = (bf16[128,256]{1,0:T(8,128)(2,1)}, bf16[128,256]{1,0:T(8,128)(2,1)S(1)}, u32[]{:S(2)}, u32[]{:S(2)}) collective-permute-start(bf16[128,256]{1,0:T(8,128)(2,1)} %x_ref.1), channel_id=1, source_target_pairs={{0,16},{1,17},{2,6},{3,7},{4,20},{5,21},{6,2},{7,3},{8,24},{9,25},... | collective-permute-start | bytes 196616 | tf_op jit(solution)/shard_map/ppermute | solution.py:33
  4.7 0.9 %copy-start.4 = (bf16[128,256]{1,0:T(8,128)(2,1)S(1)}, bf16[128,256]{1,0:T(8,128)(2,1)}, u32[]{:S(2)}) copy-start(bf16[128,256]{1,0:T(8,128)(2,1)} %x_ref.1) | copy-start | bytes 196612
  5.6 0.7 %copy-start.6 = (s32[1,1,16,2]{2,3,1,0:T(2,128)S(1)}, s32[1,1,16,2]{2,3,1,0:T(2,128)}, u32[]{:S(2)}) copy-start(s32[1,1,16,2]{2,3,1,0:T(2,128)} %param.9) | copy-start | bytes 388
  5.6 15.4 %copy-start = (bf16[1,1,16,2,128,128]{5,4,3,2,1,0:T(8,128)(2,1)S(1)}, bf16[1,1,16,2,128,128]{5,4,3,2,1,0:T(8,128)(2,1)}, u32[]{:S(2)}) copy-start(bf16[1,1,16,2,128,128]{5,4,3,2,1,0:T(8,128)(2,1)} %param.8) | copy-start | bytes 3145732
  7.2 5.3 %collective-permute-start.1 = (bf16[256,256]{1,0:T(8,128)(2,1)S(1)}, bf16[256,256]{1,0:T(8,128)(2,1)S(1)}, u32[]{:S(2)}, u32[]{:S(2)}) collective-permute-start(bf16[256,256]{1,0:T(8,128)(2,1)S(1)} %get-tuple-element.24), channel_id=1, source_target_pairs={{0,8},{1,9},{2,18},{3,19},{4,12},{5,13},{6,22},{7,23},{8,0},{9,1},... | collective-permute-start | bytes 393224 | tf_op jit(solution)/shard_map/ppermute | solution.py:33
  12.5 6.4 %collective-permute-start.2 = (bf16[512,256]{1,0:T(8,128)(2,1)S(1)}, bf16[512,256]{1,0:T(8,128)(2,1)S(1)}, u32[]{:S(2)}, u32[]{:S(2)}) collective-permute-start(bf16[512,256]{1,0:T(8,128)(2,1)S(1)} %pad_maximum_fusion), channel_id=1, source_target_pairs={{0,4},{1,5},{2,10},{3,11},{4,0},{5,1},{6,14},{7,15},{8,12},{9,13},... | collective-permute-start | bytes 786440 | tf_op jit(solution)/shard_map/ppermute | solution.py:33
  19.0 3.0 %collective-permute-start.3 = (bf16[1024,256]{1,0:T(8,128)(2,1)S(1)}, bf16[1024,256]{1,0:T(8,128)(2,1)S(1)}, u32[]{:S(2)}, u32[]{:S(2)}) collective-permute-start(bf16[1024,256]{1,0:T(8,128)(2,1)S(1)} %constant_dynamic-update-slice_fusion.refs_4_), channel_id=1, source_target_pairs={{0,2},{1,3},{2,0},{3,1},{4,6},{5,7},{6,4},{7,5},{8,10},{9,11},{10,... | collective-permute-start | bytes 1572872 | tf_op jit(solution)/shard_map/ppermute | solution.py:33
  19.1 2.0 %copy-start.5 = (s32[1,1,16]{2,1,0:T(1,128)S(1)}, s32[1,1,16]{2,1,0:T(1,128)}, u32[]{:S(2)}) copy-start(s32[1,1,16]{2,1,0:T(1,128)} %param.10) | copy-start | bytes 196
  19.1 6.0 %collective-permute-start.5 = (bf16[256,256]{1,0:T(8,128)(2,1)S(1)}, bf16[256,256]{1,0:T(8,128)(2,1)S(1)}, u32[]{:S(2)}, u32[]{:S(2)}) collective-permute-start(bf16[256,256]{1,0:T(8,128)(2,1)S(1)} %get-tuple-element.23), channel_id=1, source_target_pairs={{0,1},{1,0},{2,3},{3,2},{4,5},{5,4},{6,7},{7,6},{8,9},{9,8},{10,11... | collective-permute-start | bytes 393224 | tf_op jit(solution)/shard_map/ppermute | solution.py:33
  23.0 5.6 %copy-start.2 = (bf16[256,256]{1,0:T(8,128)(2,1)S(1)}, bf16[256,256]{1,0:T(8,128)(2,1)}, u32[]{:S(2)}) copy-start(bf16[256,256]{1,0:T(8,128)(2,1)} %w_self.1) | copy-start | bytes 393220
  23.0 5.6 %copy-start.3 = (bf16[256,256]{1,0:T(8,128)(2,1)S(1)}, bf16[256,256]{1,0:T(8,128)(2,1)}, u32[]{:S(2)}) copy-start(bf16[256,256]{1,0:T(8,128)(2,1)} %w_neigh.1) | copy-start | bytes 393220
  23.1 5.6 %collective-permute-start.4 = (bf16[256,256]{1,0:T(8,128)(2,1)S(1)}, bf16[256,256]{1,0:T(8,128)(2,1)S(1)}, u32[]{:S(2)}, u32[]{:S(2)}) collective-permute-start(bf16[256,256]{1,0:T(8,128)(2,1)S(1)} %shard_map.96.own), channel_id=1, source_target_pairs={{0,1},{1,0},{2,3},{3,2},{4,5},{5,4},{6,7},{7,6},{8,9},{9,8},{10,11... | collective-permute-start | bytes 393224 | tf_op jit(solution)/shard_map/ppermute | solution.py:33
  30.2 1.5 %collective-permute-start.6 = (f32[256,256]{1,0:T(8,128)S(1)}, f32[256,256]{1,0:T(8,128)S(1)}, u32[]{:S(2)}, u32[]{:S(2)}) collective-permute-start(f32[256,256]{1,0:T(8,128)S(1)} %get-tuple-element.18), channel_id=1, source_target_pairs={{0,2},{1,3},{2,0},{3,1},{4,6},{5,7},{6,4},{7,5},{8,10},{9,11},{10,... | collective-permute-start | bytes 786440 | tf_op jit(solution)/shard_map/ppermute | solution.py:33
  31.7 5.0 %collective-permute-start.7 = (bf16[256,256]{1,0:T(8,128)(2,1)S(1)}, bf16[256,256]{1,0:T(8,128)(2,1)S(1)}, u32[]{:S(2)}, u32[]{:S(2)}) collective-permute-start(bf16[256,256]{1,0:T(8,128)(2,1)S(1)} %add_convert_fusion.2), channel_id=1, source_target_pairs={{0,4},{1,5},{2,18},{3,19},{4,0},{5,1},{6,22},{7,23},{8,12},{9,13},... | collective-permute-start | bytes 393224 | tf_op jit(solution)/shard_map/ppermute | solution.py:33
  36.8 5.0 %collective-permute-start.8 = (bf16[256,256]{1,0:T(8,128)(2,1)S(1)}, bf16[256,256]{1,0:T(8,128)(2,1)S(1)}, u32[]{:S(2)}, u32[]{:S(2)}) collective-permute-start(bf16[256,256]{1,0:T(8,128)(2,1)S(1)} %add_convert_fusion.1), channel_id=1, source_target_pairs={{0,8},{1,9},{2,6},{3,7},{4,12},{5,13},{6,2},{7,3},{8,0},{9,1},{10,... | collective-permute-start | bytes 393224 | tf_op jit(solution)/shard_map/ppermute | solution.py:33
  41.9 6.4 %collective-permute-start.9 = (bf16[256,256]{1,0:T(8,128)(2,1)S(1)}, bf16[256,256]{1,0:T(8,128)(2,1)S(1)}, u32[]{:S(2)}, u32[]{:S(2)}) collective-permute-start(bf16[256,256]{1,0:T(8,128)(2,1)S(1)} %add_convert_fusion), channel_id=1, source_target_pairs={{0,16},{1,17},{2,10},{3,11},{4,20},{5,21},{6,14},{7,15},{8,24},{9,... | collective-permute-start | bytes 393224 | tf_op jit(solution)/shard_map/ppermute | solution.py:33
  48.3 1.6 %collective-permute-start.10 = (f32[256,256]{1,0:T(8,128)S(1)}, f32[256,256]{1,0:T(8,128)S(1)}, u32[]{:S(2)}, u32[]{:S(2)}) collective-permute-start(f32[256,256]{1,0:T(8,128)S(1)} %convert_add_fusion), channel_id=1, source_target_pairs={{0,2},{1,3},{2,0},{3,1},{4,6},{5,7},{6,4},{7,5},{8,10},{9,11},{10,... | collective-permute-start | bytes 786440 | tf_op jit(solution)/shard_map/ppermute | solution.py:33

commit v3 on v2

v3 whole, which is shorter than its diff:
```python
import functools

import jax
import jax.numpy as jnp
from jax import lax
from jax.experimental import pallas as pl
from jax.experimental.pallas import tpu as pltpu
from jax.sharding import PartitionSpec as P

VMEM = pl.BlockSpec(memory_space=pltpu.VMEM)
SMEM = pl.BlockSpec(memory_space=pltpu.SMEM)
F32 = jnp.float32
BF16 = jnp.bfloat16


def bits_below(size):
    return [1 << i for i in reversed(range(size.bit_length() - 1))]


def doubling_masks(bits):
    masks = [0]
    for bit in bits:
        masks = masks + [mask ^ bit for mask in masks]
    return masks


def swap(x, n_node, n_rep, even, odd):
    pairs = []
    for node in range(n_node):
        flip_node, flip_rep = odd if node.bit_count() & 1 else even
        for rep in range(n_rep):
            pairs.append((node * n_rep + rep, (node ^ flip_node) * n_rep + (rep ^ flip_rep)))
    return lax.ppermute(x, ("node", "rep"), pairs)


def masked_pair(place, rows, count, tiles, out_tiles, mates, even, odd):
    node = place[0]
    base = place[1] - place[3]
    groups = []
    for mate, e, o in zip(mates, even, odd, strict=True):
        origin = node ^ 1 if mate else node
        groups.append(origin ^ jnp.where(place[2] == (0 if mate else 1), o, e))
    lefts = []
    for s in range(tiles.shape[1]):
        for k in range(out_tiles):
            parts = []
            for group in groups:
                live = jnp.logical_and(s < count[group], rows[group * tiles.shape[1] + s] == base ^ k)
                value = tiles[group, s]
                chosen = jnp.full(value.shape, live.astype(F32)) > 0.5
                parts.append(jnp.where(chosen, value, jnp.zeros_like(value)))
            lefts.append(jnp.concatenate(parts, axis=1))
    return jnp.concatenate(lefts, axis=0)


def build_lefts(steps, place, rows, count, tiles, *outs):
    at = 0
    for out in outs:
        for i in range(out.shape[0]):
            out_tiles = out.shape[1] // (tiles.shape[1] * tiles.shape[2])
            out[i] = masked_pair(place, rows, count, tiles, out_tiles, *steps[at])
            at += 1


def tile_sums(steps, prebuilt, n_columns, seeded, *refs):
    refs, out = refs[:-1], refs[-1]
    if seeded:
        refs, seed = refs[:-1], refs[-1]
    refs, columns = refs[:-n_columns], refs[-n_columns:]
    total = seed[...] if seeded else None
    panel = out.shape[0]
    tile = sum(part.shape[0] for part in columns) // (2 * len(steps))
    at = 0
    for part in columns:
        for i in range(0, part.shape[0], 2 * tile):
            size = 2 * tile
            if prebuilt:
                left = refs[0][at]
            else:
                left = masked_pair(*refs, panel // refs[3].shape[2], *steps[at])
            terms = jnp.dot(left, part[i : i + size, :], preferred_element_type=F32)
            for s in range(terms.shape[0] // panel):
                term = terms[s * panel : (s + 1) * panel]
                total = term if total is None else total + term
            at += 1
    out[...] = total.astype(out.dtype)


def update(place, own, got, feats, far_feats, out_grad, far_out_grad, w_self, w_neigh, value, keep_top, keep_low, send_top, send_low, side):
    side[...] = jnp.full(side.shape, place[2])
    rows = feats.shape[0]
    first_rep = jnp.full((rows, feats.shape[1]), place[3]) == 0

    def in_order(mine, far):
        return jnp.concatenate([jnp.where(first_rep, mine, far), jnp.where(first_rep, far, mine)], axis=0)

    x = in_order(feats[...], far_feats[...])
    g = in_order(out_grad[...], far_out_grad[...]).astype(F32)
    aggregate = (own[...].astype(F32) + got[...].astype(F32)).astype(BF16)
    pre = jnp.dot(x, w_self[...], preferred_element_type=F32) + jnp.dot(
        aggregate, w_neigh[...], preferred_element_type=F32
    )
    sigma = jax.nn.sigmoid(pre)
    both = (pre * sigma).astype(BF16)
    value[...] = jnp.where(first_rep, both[:rows], both[rows:])
    delta = (g * sigma * (1.0 + pre * (1.0 - sigma))).astype(BF16)
    first_core = jnp.full(x.shape, place[2]) == 0
    for left, top, low in (
        (jnp.where(first_core, aggregate, x), send_top, send_low),
        (jnp.where(first_core, x, aggregate), keep_top, keep_low),
    ):
        grad = lax.dot_general(left, delta, (((0,), (0,)), ((), ())), preferred_element_type=F32)
        top[...] = grad[: top.shape[0]]
        low[...] = grad[top.shape[0] :]


def copied(x_ref, out_ref):
    out_ref[...] = x_ref[...]


def call(body, out_shape, specs, flops, nbytes):
    return pl.pallas_call(
        body,
        out_shape=out_shape,
        in_specs=specs,
        out_specs=jax.tree.map(lambda _: VMEM, out_shape),
        cost_estimate=pl.CostEstimate(flops=flops, bytes_accessed=nbytes, transcendentals=0),
        compiler_params=pltpu.CompilerParams(vmem_limit_bytes=24 * 1024 * 1024),
    )


def local(n_node, n_rep, node_feats, tile_vals, tile_rows, tile_count, w_self, w_neigh, out_grad):
    tiles = tile_vals[0, 0]
    rows, width = node_feats.shape
    node, rep = lax.axis_index("node"), lax.axis_index("rep")
    barrier = lax.optimization_barrier

    hops = [bit | 1 for bit in bits_below(n_node)[:-1]]
    turned = hops[-1:] + hops[:-1]
    rep_bits = bits_below(n_rep)

    def trade(x, even, odd):
        return swap(x, n_node, n_rep, even, odd)

    def core_swap(x):
        return trade(x, (1, 0), (1, 0))

    got = trade(node_feats, (hops[0], 0), (turned[0], 0))
    feats = call(copied, jax.ShapeDtypeStruct(node_feats.shape, BF16), [VMEM], 0, node_feats.size * 4)(node_feats)
    far = trade(jnp.concatenate([feats, out_grad], axis=0), (0, 1), (0, 1))
    feats, got, tables = barrier((feats, got, (node, rep, tile_rows, tile_count)))
    node, rep, tile_rows, tile_count = tables
    row_ids = tile_rows[0, 0].reshape(-1)
    live_count = tile_count[0, 0]
    parity = node
    for shift in bits_below(n_node.bit_length()):
        parity = parity ^ (parity >> shift)
    place = jnp.stack([node, rep, parity & 1, rep & 1]).astype(jnp.int32)
    held = jnp.concatenate([feats, got], axis=0)
    for even, odd in zip(hops[1:-1], turned[1:-1], strict=True):
        got = trade(held, (even, 0), (odd, 0))
        far, got, place, row_ids, live_count = barrier((far, got, place, row_ids, live_count))
        held = jnp.concatenate([held, got], axis=0)
    late = trade(held, (hops[-1], 0), (turned[-1], 0))
    other = core_swap(held)

    masks_even, masks_odd = doubling_masks(hops), doubling_masks(turned)
    half = len(masks_even) // 2

    def steps_of(mate, first):
        return [
            ((mate, mate), masks_even[i : i + 2], masks_odd[i : i + 2]) for i in range(first, first + half, 2)
        ]

    groups = [steps_of(False, 0), steps_of(False, half), steps_of(True, 0) + steps_of(True, half)]
    panel = n_rep * rows
    slots = tiles.shape[1]
    left_sizes = [len(steps) * slots * panel * 2 * rows * 2 for steps in groups]
    prebuilt = sum(left_sizes) <= 4 * 1024 * 1024
    tables = [place, row_ids, live_count, tiles]
    table_specs = [SMEM] * 3 + [VMEM]
    if prebuilt:
        lefts = call(
            functools.partial(build_lefts, sum(groups, [])),
            tuple(jax.ShapeDtypeStruct((len(steps), slots * panel, 2 * rows), BF16) for steps in groups),
            table_specs, 0, 3 * sum(left_sizes),
        )(*tables)

    def sums(index, columns, seed, dtype):
        steps = groups[index]
        given, specs = ([lefts[index]], [VMEM]) if prebuilt else (tables, table_specs)
        more = columns + ([seed] if seed is not None else [])
        flops = len(steps) * slots * panel * 2 * rows * width * 2
        return call(
            functools.partial(tile_sums, steps, prebuilt, len(columns), seed is not None),
            jax.ShapeDtypeStruct((panel, width), dtype), specs + [VMEM] * len(more), flops, left_sizes[index],
        )(*given, *more)

    total = sums(0, [held], None, F32)
    late, total = barrier((late, total))
    other_late = core_swap(late)
    total = sums(1, [late], total, F32)
    total = sums(2, [other, other_late], total, BF16 if n_rep == 2 else F32)

    for bit in rep_bits[:-1]:
        got = trade(total[bit * rows :].astype(BF16), (0, bit), (0, bit))
        total = total[: bit * rows].astype(F32) + got.astype(F32)
    total = total.astype(BF16)
    got = trade(total, (0, 1), (0, 1))

    half_grad = jax.ShapeDtypeStruct((width // 2, width), F32)
    value, keep_top, keep_low, send_top, send_low, side = call(
        update,
        (
            jax.ShapeDtypeStruct((rows, width), BF16), half_grad, half_grad, half_grad, half_grad,
            jax.ShapeDtypeStruct((1, width), jnp.int32),
        ),
        [SMEM] + [VMEM] * 8, 16 * rows * width * width, 1 << 20,
    )(place, total, got, feats, far[:rows], out_grad, far[rows:], w_self, w_neigh)
    grads = [keep_top + core_swap(send_top), keep_low + core_swap(send_low)]
    layer_out = call(copied, jax.ShapeDtypeStruct((rows, width), BF16), [VMEM], 0, 4 * rows * width)(value)

    order_even = hops
    order_odd = hops[::-1]
    steps = [((0, bit), (0, bit)) for bit in rep_bits[:-1]]
    steps += [((even, 0), (odd, 0)) for even, odd in zip(order_even, order_odd, strict=True)]
    for even, odd in steps[:-1]:
        parts = [grad.astype(BF16) for grad in grads]
        gots = [trade(part, even, odd) for part in parts]
        gots[0], layer_out = barrier((gots[0], layer_out))
        grads = [part.astype(F32) + got.astype(F32) for part, got in zip(parts, gots, strict=True)]
    parts = [grad.astype(BF16) for grad in grads]
    gots = [trade(part, *steps[-1]) for part in parts]
    part, got = jnp.concatenate(parts, axis=0), jnp.concatenate(gots, axis=0)
    other_part = core_swap(part)
    other_got = jnp.concatenate([core_swap(got) for got in gots], axis=0)
    grad = part.astype(F32) + got.astype(F32)
    other_grad = other_part.astype(F32) + other_got.astype(F32)
    first_core = side == 0
    grad_self = jnp.where(first_core, grad, other_grad)
    grad_neigh = jnp.where(first_core, other_grad, grad)
    return (layer_out, grad_self, grad_neigh)


def solution(mesh):
    placed = (
        P(("node", "rep"), None),
        P("node", "rep", None, None, None, None),
        P("node", "rep", None, None),
        P("node", "rep", None),
        P(),
        P(),
        P(("node", "rep"), None),
    )
    return jax.shard_map(
        functools.partial(local, mesh.shape["node"], mesh.shape["rep"]),
        mesh=mesh,
        in_specs=placed,
        out_specs=(P(("node", "rep"), None), P(), P()),
        check_vma=False,
    )
```

time: 50.9 us -> 46.1 us (0.906)
  waiting for transfers between devices: 27.2 us -> 15.3 us
  starting transfers between devices: 16.4 us -> 23.3 us
    ppermute x11 -> x18, waiting for transfers between devices: 27.2 us -> 15.3 us  [swap(): return lax.ppermute(x, ('node', 'rep'), pairs)]
    ppermute x11 -> x18, starting transfers between devices: 16.4 us -> 23.3 us  [swap(): return lax.ppermute(x, ('node', 'rep'), pairs)]
    optimization_barrier x0 -> x1, local copies, waits for them, and re-layouts: none -> 0.76 us  [local(): barrier((feats, got, (node, rep, tile_rows, tile_count)))]
    unnamed x18 -> x14, local copies, waits for them, and re-layouts: 1.66 us -> 0.91 us
    pallas_call x3 -> x6, Pallas kernels: 3.48 us -> 3.61 us  [the longest x1 1.12 us: local(): call(update, (jax.ShapeDtypeStruct((rows, width), BF16), half_grad, half_...]
  transfers between devices with their start and end apart: 11 -> 18, of which waited for: 10 -> 13; matrix products, arithmetic and copies ran while one was open for 1% -> 2% of each run, Pallas kernels for 4% -> 4%
where the time goes in v3:
time: 46.1 us; the launch traced here: 45.9 us
  starting transfers between devices  23.3 us (51%)
  waiting for transfers between devices  15.3 us (33%)
  Pallas kernels  3.62 us (8%)
  local copies, waits for them, and re-layouts  1.77 us (4%)
  other arithmetic  1.09 us (2%)
  between operations  0.82 us (2%)
    ppermute x18, starting transfers between devices, swap(): return lax.ppermute(x, ('node', 'rep'), pairs)  23.3 us
    ppermute x18, waiting for transfers between devices, swap(): return lax.ppermute(x, ('node', 'rep'), pairs)  15.3 us
    pallas_call x1, Pallas kernels, local(): call(update, (jax.ShapeDtypeStruct((rows, width), BF16), half_grad, half_...  1.12 us
    pallas_call x3, Pallas kernels, sums(): call(functools.partial(tile_sums, steps, prebuilt, len(columns), seed is...  1.02 us
  transfers between devices with their start and end apart: 18, of which 13 were waited for; matrix products, arithmetic and copies ran while one was open for 2% of the time, Pallas kernels for 4%

profile of v3, /device:TPU:0, one launch (start us, length us, event | category | flops | bytes accessed | tf_op | source)
XLA Modules:
  0.0 45.9 jit_solution(9251623880310821565)
XLA Ops:
  0.6 0.0 copy-start.1
  0.6 0.0 copy-start
  0.7 3.5 %collective-permute-start.1 = (bf16[128,256]{1,0:T(8,128)(2,1)}, bf16[128,256]{1,0:T(8,128)(2,1)S(1)}, u32[]{:S(2)}, u32[]{:S(2)}) collective-permute-start(bf16[128,256]{1,0:T(8,128)(2,1)} %x_ref.1), channel_id=1, source_target_pairs={{0,18},{1,19},{2,4},{3,5},{4,2},{5,3},{6,20},{7,21},{8,14},{9,15},... | collective-permute-start | bytes 196616 | tf_op jit(solution)/shard_map/ppermute | solution.py:33
  4.2 0.0 copy-start.4
  4.2 0.9 %copy-done.4 = bf16[128,256]{1,0:T(8,128)(2,1)S(1)} copy-done((bf16[128,256]{1,0:T(8,128)(2,1)S(1)}, bf16[128,256]{1,0:T(8,128)(2,1)}, u32[]{:S(2)}) %copy-start.4) | copy-done | bytes 65560
  5.1 0.0 copy-done.1
  5.1 1.6 %collective-permute-start = (bf16[256,256]{1,0:T(8,128)(2,1)S(1)}, bf16[256,256]{1,0:T(8,128)(2,1)S(1)}, u32[]{:S(2)}, u32[]{:S(2)}) collective-permute-start(bf16[256,256]{1,0:T(8,128)(2,1)S(1)} %pad_maximum_fusion), channel_id=1, source_target_pairs={{0,1},{1,0},{2,3},{3,2},{4,5},{5,4},{6,7},{7,6},{8,9},{9,8},{10,11... | collective-permute-start | bytes 393224 | tf_op jit(solution)/shard_map/ppermute | solution.py:33
  6.7 0.0 collective-permute-done.1
  6.7 1.6 %collective-permute-start.2 = (bf16[256,256]{1,0:T(8,128)(2,1)S(1)}, bf16[256,256]{1,0:T(8,128)(2,1)S(1)}, u32[]{:S(2)}, u32[]{:S(2)}) collective-permute-start(bf16[256,256]{1,0:T(8,128)(2,1)S(1)} %pad_maximum_fusion.1), channel_id=1, source_target_pairs={{0,10},{1,11},{2,16},{3,17},{4,22},{5,23},{6,12},{7,13},{8,26},{9,... | collective-permute-start | bytes 393224 | tf_op jit(solution)/shard_map/ppermute | solution.py:33
  8.3 0.1 pad_add_fusion.place
  8.4 0.8 %copy.11 = s32[1,1,16,2]{3,2,1,0:T(8,128)S(1)} copy(s32[1,1,16,2]{2,3,1,0:T(2,128)} %param.9) | data formatting | bytes 256 | tf_op jit(solution)/shard_map/optimization_barrier | solution.py:151
  9.2 0.1 reshape_squeeze.3.rows
  9.3 0.9 %collective-permute-done = bf16[256,256]{1,0:T(8,128)(2,1)S(1)} collective-permute-done((bf16[256,256]{1,0:T(8,128)(2,1)S(1)}, bf16[256,256]{1,0:T(8,128)(2,1)S(1)}, u32[]{:S(2)}, u32[]{:S(2)}) %collective-permute-start) | collective-permute-done | bytes 131104 | tf_op jit(solution)/shard_map/ppermute | solution.py:33
  10.2 1.9 %collective-permute-done.2 = bf16[256,256]{1,0:T(8,128)(2,1)S(1)} collective-permute-done((bf16[256,256]{1,0:T(8,128)(2,1)S(1)}, bf16[256,256]{1,0:T(8,128)(2,1)S(1)}, u32[]{:S(2)}, u32[]{:S(2)}) %collective-permute-start.2) | collective-permute-done | bytes 131104 | tf_op jit(solution)/shard_map/ppermute | solution.py:33
  12.1 0.0 copy-start.5
  12.1 1.8 %collective-permute-start.4 = (bf16[512,256]{1,0:T(8,128)(2,1)S(1)}, bf16[512,256]{1,0:T(8,128)(2,1)S(1)}, u32[]{:S(2)}, u32[]{:S(2)}) collective-permute-start(bf16[512,256]{1,0:T(8,128)(2,1)S(1)} %constant_dynamic-update-slice_fusion.refs_1_), channel_id=1, source_target_pairs={{0,6},{1,7},{2,8},{3,9},{4,14},{5,15},{6,0},{7,1},{8,2},{9,3},{10,... | collective-permute-start | bytes 786440 | tf_op jit(solution)/shard_map/ppermute | solution.py:33
  13.9 0.0 collective-permute-start.3
  13.9 0.0 copy-done
  13.9 0.0 copy-done.5
  13.9 0.8 %shard_map.95 = (bf16[2,512,256]{2,1,0:T(8,128)(2,1)S(1)}, bf16[2,512,256]{2,1,0:T(8,128)(2,1)S(1)}, bf16[4,512,256]{2,1,0:T(8,128)(2,1)S(1)}) custom-call(s32[4]{0:T(128)S(1)} %pad_add_fusion.place, s32[32]{0:T(128)S(1)} %reshape_squeeze.3.rows, s32[16]{0:T(128)S(1)} %bitcast.9, bf16[16,2,128,128]{3,2,1,0:T(8,128)(2,1)S(1)} %bitcast.8), custom_call_target="tpu_custom_call" | custom-call | bytes 6291456 | tf_op jit(solution)/shard_map/pallas_call | solution.py:183
  14.7 0.3 shard_map.96.refs_2_
  15.0 2.9 %collective-permute-done.4.refs_1_ = bf16[512,256]{1,0:T(8,128)(2,1)S(1)} collective-permute-done((bf16[512,256]{1,0:T(8,128)(2,1)S(1)}, bf16[512,256]{1,0:T(8,128)(2,1)S(1)}, u32[]{:S(2)}, u32[]{:S(2)}) %collective-permute-start.4) | collective-permute-done | bytes 262176 | tf_op jit(solution)/shard_map/ppermute | solution.py:33
  17.9 1.0 %collective-permute-start.5 = (bf16[512,256]{1,0:T(8,128)(2,1)S(1)}, bf16[512,256]{1,0:T(8,128)(2,1)S(1)}, u32[]{:S(2)}, u32[]{:S(2)}) collective-permute-start(bf16[512,256]{1,0:T(8,128)(2,1)S(1)} %collective-permute-done.4.refs_1_), channel_id=1, source_target_pairs={{0,2},{1,3},{2,0},{3,1},{4,6},{5,7},{6,4},{7,5},{8,10},{9,11},{10,... | collective-permute-start | bytes 786440 | tf_op jit(solution)/shard_map/ppermute | solution.py:33
  18.9 0.3 shard_map.97.refs_3_
  19.2 0.0 collective-permute-done.3.refs_1_
  19.2 0.8 %collective-permute-done.5.refs_2_ = bf16[512,256]{1,0:T(8,128)(2,1)S(1)} collective-permute-done((bf16[512,256]{1,0:T(8,128)(2,1)S(1)}, bf16[512,256]{1,0:T(8,128)(2,1)S(1)}, u32[]{:S(2)}, u32[]{:S(2)}) %collective-permute-start.5) | collective-permute-done | bytes 262176 | tf_op jit(solution)/shard_map/ppermute | solution.py:33
  20.1 0.4 shard_map.98.own
  20.5 0.0 copy-start.2
  20.5 0.0 copy-start.3
  20.6 1.4 %collective-permute-start.6 = (bf16[256,256]{1,0:T(8,128)(2,1)S(1)}, bf16[256,256]{1,0:T(8,128)(2,1)S(1)}, u32[]{:S(2)}, u32[]{:S(2)}) collective-permute-start(bf16[256,256]{1,0:T(8,128)(2,1)S(1)} %shard_map.98.own), channel_id=1, source_target_pairs={{0,1},{1,0},{2,3},{3,2},{4,5},{5,4},{6,7},{7,6},{8,9},{9,8},{10,11... | collective-permute-start | bytes 393224 | tf_op jit(solution)/shard_map/ppermute | solution.py:33
  22.0 4.4 %collective-permute-done.6.got = bf16[256,256]{1,0:T(8,128)(2,1)S(1)} collective-permute-done((bf16[256,256]{1,0:T(8,128)(2,1)S(1)}, bf16[256,256]{1,0:T(8,128)(2,1)S(1)}, u32[]{:S(2)}, u32[]{:S(2)}) %collective-permute-start.6) | collective-permute-done | bytes 131104 | tf_op jit(solution)/shard_map/ppermute | solution.py:33
  26.4 0.0 copy-done.2
  26.4 0.0 copy-done.3
  26.4 1.1 %shard_map.99 = (bf16[128,256]{1,0:T(8,128)(2,1)S(1)}, f32[128,256]{1,0:T(8,128)S(1)}, f32[128,256]{1,0:T(8,128)S(1)}, f32[128,256]{1,0:T(8,128)S(1)}, f32[128,256]{1,0:T(8,128)S(1)}, /*index=5*/s32[1,256]{1,0:T(1,128)S(1)}) custom-call(s32[4]{0:T(128)S(1)} %pad_add_fusion.place, bf16[256,256]{1,0:T(8,128)(2,1)S(1)} %shard_map.98.own, ...), custom_call_target="tpu_custom_call" | custom-call | flops 134217728 | bytes 1048576 | tf_op jit(solution)/shard_map/pallas_call | solution.py:212
  27.5 0.1 collective-permute-start.7
  27.6 0.6 %shard_map.100 = bf16[128,256]{1,0:T(8,128)(2,1)} custom-call(bf16[128,256]{1,0:T(8,128)(2,1)S(1)} %get-tuple-element.47.x_ref), custom_call_target="tpu_custom_call" | custom-call | bytes 131072 | tf_op jit(solution)/shard_map/pallas_call | solution.py:221
  28.2 0.5 %collective-permute-start.10 = (f32[128,256]{1,0:T(8,128)S(1)}, f32[128,256]{1,0:T(8,128)S(1)}, u32[]{:S(2)}, u32[]{:S(2)}) collective-permute-start(f32[128,256]{1,0:T(8,128)S(1)} %get-tuple-element.54), channel_id=1, source_target_pairs={{0,2},{1,3},{2,0},{3,1},{4,6},{5,7},{6,4},{7,5},{8,10},{9,11},{10,... | collective-permute-start | bytes 393224 | tf_op jit(solution)/shard_map/ppermute | solution.py:33
  28.7 0.2 collective-permute-done.7
  29.0 2.2 %collective-permute-start.8 = (bf16[128,256]{1,0:T(8,128)(2,1)S(1)}, bf16[128,256]{1,0:T(8,128)(2,1)S(1)}, u32[]{:S(2)}, u32[]{:S(2)}) collective-permute-start(bf16[128,256]{1,0:T(8,128)(2,1)S(1)} %add_convert_fusion.5), channel_id=1, source_target_pairs={{0,18},{1,19},{2,4},{3,5},{4,2},{5,3},{6,20},{7,21},{8,14},{9,15},... | collective-permute-start | bytes 196616 | tf_op jit(solution)/shard_map/ppermute | solution.py:33
  31.1 0.0 collective-permute-done.10
  31.2 1.0 %collective-permute-start.11 = (bf16[128,256]{1,0:T(8,128)(2,1)S(1)}, bf16[128,256]{1,0:T(8,128)(2,1)S(1)}, u32[]{:S(2)}, u32[]{:S(2)}) collective-permute-start(bf16[128,256]{1,0:T(8,128)(2,1)S(1)} %add_convert_fusion.2), channel_id=1, source_target_pairs={{0,18},{1,19},{2,4},{3,5},{4,2},{5,3},{6,20},{7,21},{8,14},{9,15},... | collective-permute-start | bytes 196616 | tf_op jit(solution)/shard_map/ppermute | solution.py:33
  32.1 1.5 %collective-permute-done.8 = bf16[128,256]{1,0:T(8,128)(2,1)S(1)} collective-permute-done((bf16[128,256]{1,0:T(8,128)(2,1)S(1)}, bf16[128,256]{1,0:T(8,128)(2,1)S(1)}, u32[]{:S(2)}, u32[]{:S(2)}) %collective-permute-start.8) | collective-permute-done | bytes 65568 | tf_op jit(solution)/shard_map/ppermute | solution.py:33
  33.6 2.0 %collective-permute-start.9 = (bf16[128,256]{1,0:T(8,128)(2,1)S(1)}, bf16[128,256]{1,0:T(8,128)(2,1)S(1)}, u32[]{:S(2)}, u32[]{:S(2)}) collective-permute-start(bf16[128,256]{1,0:T(8,128)(2,1)S(1)} %add_convert_fusion.4), channel_id=1, source_target_pairs={{0,10},{1,11},{2,8},{3,9},{4,14},{5,15},{6,12},{7,13},{8,2},{9,3},... | collective-permute-start | bytes 196616 | tf_op jit(solution)/shard_map/ppermute | solution.py:33
  35.6 0.3 collective-permute-done.11
  35.9 2.1 %collective-permute-start.12 = (bf16[128,256]{1,0:T(8,128)(2,1)S(1)}, bf16[128,256]{1,0:T(8,128)(2,1)S(1)}, u32[]{:S(2)}, u32[]{:S(2)}) collective-permute-start(bf16[128,256]{1,0:T(8,128)(2,1)S(1)} %add_convert_fusion.1), channel_id=1, source_target_pairs={{0,10},{1,11},{2,8},{3,9},{4,14},{5,15},{6,12},{7,13},{8,2},{9,3},... | collective-permute-start | bytes 196616 | tf_op jit(solution)/shard_map/ppermute | solution.py:33
  38.0 0.2 collective-permute-done.9
  38.2 1.3 %collective-permute-start.13 = (bf16[128,256]{1,0:T(8,128)(2,1)S(1)}, bf16[128,256]{1,0:T(8,128)(2,1)S(1)}, u32[]{:S(2)}, u32[]{:S(2)}) collective-permute-start(bf16[128,256]{1,0:T(8,128)(2,1)S(1)} %add_convert_fusion.3), channel_id=1, source_target_pairs={{0,6},{1,7},{2,16},{3,17},{4,22},{5,23},{6,0},{7,1},{8,26},{9,27},... | collective-permute-start | bytes 196616 | tf_op jit(solution)/shard_map/ppermute | solution.py:33
  39.6 0.4 collective-permute-done.12
  39.9 1.3 %collective-permute-start.14 = (bf16[128,256]{1,0:T(8,128)(2,1)S(1)}, bf16[128,256]{1,0:T(8,128)(2,1)S(1)}, u32[]{:S(2)}, u32[]{:S(2)}) collective-permute-start(bf16[128,256]{1,0:T(8,128)(2,1)S(1)} %add_convert_fusion), channel_id=1, source_target_pairs={{0,6},{1,7},{2,16},{3,17},{4,22},{5,23},{6,0},{7,1},{8,26},{9,27},... | collective-permute-start | bytes 196616 | tf_op jit(solution)/shard_map/ppermute | solution.py:33
  41.2 0.5 %collective-permute-start.15 = (bf16[256,256]{1,0:T(8,128)(2,1)S(1)}, bf16[256,256]{1,0:T(8,128)(2,1)S(1)}, u32[]{:S(2)}, u32[]{:S(2)}) collective-permute-start(bf16[256,256]{1,0:T(8,128)(2,1)S(1)} %pad_maximum_fusion.2), channel_id=1, source_target_pairs={{0,2},{1,3},{2,0},{3,1},{4,6},{5,7},{6,4},{7,5},{8,10},{9,11},{10,... | collective-permute-start | bytes 393224 | tf_op jit(solution)/shard_map/ppermute | solution.py:33
  41.7 0.2 collective-permute-done.13
  42.0 1.0 %collective-permute-start.16 = (bf16[128,256]{1,0:T(8,128)(2,1)S(1)}, bf16[128,256]{1,0:T(8,128)(2,1)S(1)}, u32[]{:S(2)}, u32[]{:S(2)}) collective-permute-start(bf16[128,256]{1,0:T(8,128)(2,1)S(1)} %collective-permute-done.13), channel_id=1, source_target_pairs={{0,2},{1,3},{2,0},{3,1},{4,6},{5,7},{6,4},{7,5},{8,10},{9,11},{10,... | collective-permute-start | bytes 196616 | tf_op jit(solution)/shard_map/ppermute | solution.py:33
  43.0 0.8 %collective-permute-done.14 = bf16[128,256]{1,0:T(8,128)(2,1)S(1)} collective-permute-done((bf16[128,256]{1,0:T(8,128)(2,1)S(1)}, bf16[128,256]{1,0:T(8,128)(2,1)S(1)}, u32[]{:S(2)}, u32[]{:S(2)}) %collective-permute-start.14) | collective-permute-done | bytes 65568 | tf_op jit(solution)/shard_map/ppermute | solution.py:33
  43.7 0.4 collective-permute-start.17
  44.2 0.0 collective-permute-done.15
  44.2 0.0 collective-permute-done.16
  44.2 0.9 %collective-permute-done.17 = bf16[128,256]{1,0:T(8,128)(2,1)S(1)} collective-permute-done((bf16[128,256]{1,0:T(8,128)(2,1)S(1)}, bf16[128,256]{1,0:T(8,128)(2,1)S(1)}, u32[]{:S(2)}, u32[]{:S(2)}) %collective-permute-start.17) | collective-permute-done | bytes 65568 | tf_op jit(solution)/shard_map/ppermute | solution.py:33
  45.1 0.9 %fusion = (f32[256,256]{1,0:T(8,128)}, f32[256,256]{1,0:T(8,128)}) fusion(bf16[256,256]{1,0:T(8,128)(2,1)S(1)} %collective-permute-done.15, pred[256]{0:T(512)(128)(4,1)S(1)} %compare_reduce_fusion, bf16[128,256]{1,0:T(8,128)(2,1)S(1)} %collective-permute-done.17, bf16[128,256]{1,0:T(8,128)(2,1)S(1)} %collective-permute-done.16, ...), kind=kLoop, calls=%fused_computation.2 | loop fusion | flops 1114112 | bytes 1048832 | tf_op jit(solution)/shard_map/jit(_where)/select_n | solution.py:241
  (15 shorter events, 0.2 us)
Async XLA Ops:
  0.6 4.4 %copy-start.1 = (bf16[128,256]{1,0:T(8,128)(2,1)S(1)}, bf16[128,256]{1,0:T(8,128)(2,1)}, u32[]{:S(2)}) copy-start(bf16[128,256]{1,0:T(8,128)(2,1)} %out_grad.1) | copy-start | bytes 196612
  0.6 13.2 %copy-start = (bf16[1,1,16,2,128,128]{5,4,3,2,1,0:T(8,128)(2,1)S(1)}, bf16[1,1,16,2,128,128]{5,4,3,2,1,0:T(8,128)(2,1)}, u32[]{:S(2)}) copy-start(bf16[1,1,16,2,128,128]{5,4,3,2,1,0:T(8,128)(2,1)} %param.8) | copy-start | bytes 3145732
  0.7 6.0 %collective-permute-start.1 = (bf16[128,256]{1,0:T(8,128)(2,1)}, bf16[128,256]{1,0:T(8,128)(2,1)S(1)}, u32[]{:S(2)}, u32[]{:S(2)}) collective-permute-start(bf16[128,256]{1,0:T(8,128)(2,1)} %x_ref.1), channel_id=1, source_target_pairs={{0,18},{1,19},{2,4},{3,5},{4,2},{5,3},{6,20},{7,21},{8,14},{9,15},... | collective-permute-start | bytes 196616 | tf_op jit(solution)/shard_map/ppermute | solution.py:33
  4.2 0.9 %copy-start.4 = (bf16[128,256]{1,0:T(8,128)(2,1)S(1)}, bf16[128,256]{1,0:T(8,128)(2,1)}, u32[]{:S(2)}) copy-start(bf16[128,256]{1,0:T(8,128)(2,1)} %x_ref.1) | copy-start | bytes 196612
  5.1 5.1 %collective-permute-start = (bf16[256,256]{1,0:T(8,128)(2,1)S(1)}, bf16[256,256]{1,0:T(8,128)(2,1)S(1)}, u32[]{:S(2)}, u32[]{:S(2)}) collective-permute-start(bf16[256,256]{1,0:T(8,128)(2,1)S(1)} %pad_maximum_fusion), channel_id=1, source_target_pairs={{0,1},{1,0},{2,3},{3,2},{4,5},{5,4},{6,7},{7,6},{8,9},{9,8},{10,11... | collective-permute-start | bytes 393224 | tf_op jit(solution)/shard_map/ppermute | solution.py:33
  6.7 5.4 %collective-permute-start.2 = (bf16[256,256]{1,0:T(8,128)(2,1)S(1)}, bf16[256,256]{1,0:T(8,128)(2,1)S(1)}, u32[]{:S(2)}, u32[]{:S(2)}) collective-permute-start(bf16[256,256]{1,0:T(8,128)(2,1)S(1)} %pad_maximum_fusion.1), channel_id=1, source_target_pairs={{0,10},{1,11},{2,16},{3,17},{4,22},{5,23},{6,12},{7,13},{8,26},{9,... | collective-permute-start | bytes 393224 | tf_op jit(solution)/shard_map/ppermute | solution.py:33
  12.1 1.8 %copy-start.5 = (s32[1,1,16]{2,1,0:T(1,128)S(1)}, s32[1,1,16]{2,1,0:T(1,128)}, u32[]{:S(2)}) copy-start(s32[1,1,16]{2,1,0:T(1,128)} %param.10) | copy-start | bytes 196
  12.1 5.9 %collective-permute-start.4 = (bf16[512,256]{1,0:T(8,128)(2,1)S(1)}, bf16[512,256]{1,0:T(8,128)(2,1)S(1)}, u32[]{:S(2)}, u32[]{:S(2)}) collective-permute-start(bf16[512,256]{1,0:T(8,128)(2,1)S(1)} %constant_dynamic-update-slice_fusion.refs_1_), channel_id=1, source_target_pairs={{0,6},{1,7},{2,8},{3,9},{4,14},{5,15},{6,0},{7,1},{8,2},{9,3},{10,... | collective-permute-start | bytes 786440 | tf_op jit(solution)/shard_map/ppermute | solution.py:33
  13.9 5.3 %collective-permute-start.3 = (bf16[512,256]{1,0:T(8,128)(2,1)S(1)}, bf16[512,256]{1,0:T(8,128)(2,1)S(1)}, u32[]{:S(2)}, u32[]{:S(2)}) collective-permute-start(bf16[512,256]{1,0:T(8,128)(2,1)S(1)} %constant_dynamic-update-slice_fusion.refs_1_), channel_id=1, source_target_pairs={{0,2},{1,3},{2,0},{3,1},{4,6},{5,7},{6,4},{7,5},{8,10},{9,11},{10,... | collective-permute-start | bytes 786440 | tf_op jit(solution)/shard_map/ppermute | solution.py:33
  17.9 2.1 %collective-permute-start.5 = (bf16[512,256]{1,0:T(8,128)(2,1)S(1)}, bf16[512,256]{1,0:T(8,128)(2,1)S(1)}, u32[]{:S(2)}, u32[]{:S(2)}) collective-permute-start(bf16[512,256]{1,0:T(8,128)(2,1)S(1)} %collective-permute-done.4.refs_1_), channel_id=1, source_target_pairs={{0,2},{1,3},{2,0},{3,1},{4,6},{5,7},{6,4},{7,5},{8,10},{9,11},{10,... | collective-permute-start | bytes 786440 | tf_op jit(solution)/shard_map/ppermute | solution.py:33
  20.5 5.9 %copy-start.2 = (bf16[256,256]{1,0:T(8,128)(2,1)S(1)}, bf16[256,256]{1,0:T(8,128)(2,1)}, u32[]{:S(2)}) copy-start(bf16[256,256]{1,0:T(8,128)(2,1)} %w_self.1) | copy-start | bytes 393220
  20.5 5.9 %copy-start.3 = (bf16[256,256]{1,0:T(8,128)(2,1)S(1)}, bf16[256,256]{1,0:T(8,128)(2,1)}, u32[]{:S(2)}) copy-start(bf16[256,256]{1,0:T(8,128)(2,1)} %w_neigh.1) | copy-start | bytes 393220
  20.6 5.8 %collective-permute-start.6 = (bf16[256,256]{1,0:T(8,128)(2,1)S(1)}, bf16[256,256]{1,0:T(8,128)(2,1)S(1)}, u32[]{:S(2)}, u32[]{:S(2)}) collective-permute-start(bf16[256,256]{1,0:T(8,128)(2,1)S(1)} %shard_map.98.own), channel_id=1, source_target_pairs={{0,1},{1,0},{2,3},{3,2},{4,5},{5,4},{6,7},{7,6},{8,9},{9,8},{10,11... | collective-permute-start | bytes 393224 | tf_op jit(solution)/shard_map/ppermute | solution.py:33
  27.5 1.4 %collective-permute-start.7 = (f32[128,256]{1,0:T(8,128)S(1)}, f32[128,256]{1,0:T(8,128)S(1)}, u32[]{:S(2)}, u32[]{:S(2)}) collective-permute-start(f32[128,256]{1,0:T(8,128)S(1)} %get-tuple-element.46), channel_id=1, source_target_pairs={{0,2},{1,3},{2,0},{3,1},{4,6},{5,7},{6,4},{7,5},{8,10},{9,11},{10,... | collective-permute-start | bytes 393224 | tf_op jit(solution)/shard_map/ppermute | solution.py:33
  28.2 2.9 %collective-permute-start.10 = (f32[128,256]{1,0:T(8,128)S(1)}, f32[128,256]{1,0:T(8,128)S(1)}, u32[]{:S(2)}, u32[]{:S(2)}) collective-permute-start(f32[128,256]{1,0:T(8,128)S(1)} %get-tuple-element.54), channel_id=1, source_target_pairs={{0,2},{1,3},{2,0},{3,1},{4,6},{5,7},{6,4},{7,5},{8,10},{9,11},{10,... | collective-permute-start | bytes 393224 | tf_op jit(solution)/shard_map/ppermute | solution.py:33
  29.0 4.7 %collective-permute-start.8 = (bf16[128,256]{1,0:T(8,128)(2,1)S(1)}, bf16[128,256]{1,0:T(8,128)(2,1)S(1)}, u32[]{:S(2)}, u32[]{:S(2)}) collective-permute-start(bf16[128,256]{1,0:T(8,128)(2,1)S(1)} %add_convert_fusion.5), channel_id=1, source_target_pairs={{0,18},{1,19},{2,4},{3,5},{4,2},{5,3},{6,20},{7,21},{8,14},{9,15},... | collective-permute-start | bytes 196616 | tf_op jit(solution)/shard_map/ppermute | solution.py:33
  31.2 4.7 %collective-permute-start.11 = (bf16[128,256]{1,0:T(8,128)(2,1)S(1)}, bf16[128,256]{1,0:T(8,128)(2,1)S(1)}, u32[]{:S(2)}, u32[]{:S(2)}) collective-permute-start(bf16[128,256]{1,0:T(8,128)(2,1)S(1)} %add_convert_fusion.2), channel_id=1, source_target_pairs={{0,18},{1,19},{2,4},{3,5},{4,2},{5,3},{6,20},{7,21},{8,14},{9,15},... | collective-permute-start | bytes 196616 | tf_op jit(solution)/shard_map/ppermute | solution.py:33
  33.6 4.6 %collective-permute-start.9 = (bf16[128,256]{1,0:T(8,128)(2,1)S(1)}, bf16[128,256]{1,0:T(8,128)(2,1)S(1)}, u32[]{:S(2)}, u32[]{:S(2)}) collective-permute-start(bf16[128,256]{1,0:T(8,128)(2,1)S(1)} %add_convert_fusion.4), channel_id=1, source_target_pairs={{0,10},{1,11},{2,8},{3,9},{4,14},{5,15},{6,12},{7,13},{8,2},{9,3},... | collective-permute-start | bytes 196616 | tf_op jit(solution)/shard_map/ppermute | solution.py:33
  35.9 4.0 %collective-permute-start.12 = (bf16[128,256]{1,0:T(8,128)(2,1)S(1)}, bf16[128,256]{1,0:T(8,128)(2,1)S(1)}, u32[]{:S(2)}, u32[]{:S(2)}) collective-permute-start(bf16[128,256]{1,0:T(8,128)(2,1)S(1)} %add_convert_fusion.1), channel_id=1, source_target_pairs={{0,10},{1,11},{2,8},{3,9},{4,14},{5,15},{6,12},{7,13},{8,2},{9,3},... | collective-permute-start | bytes 196616 | tf_op jit(solution)/shard_map/ppermute | solution.py:33
  38.2 3.8 %collective-permute-start.13 = (bf16[128,256]{1,0:T(8,128)(2,1)S(1)}, bf16[128,256]{1,0:T(8,128)(2,1)S(1)}, u32[]{:S(2)}, u32[]{:S(2)}) collective-permute-start(bf16[128,256]{1,0:T(8,128)(2,1)S(1)} %add_convert_fusion.3), channel_id=1, source_target_pairs={{0,6},{1,7},{2,16},{3,17},{4,22},{5,23},{6,0},{7,1},{8,26},{9,27},... | collective-permute-start | bytes 196616 | tf_op jit(solution)/shard_map/ppermute | solution.py:33
  39.9 3.8 %collective-permute-start.14 = (bf16[128,256]{1,0:T(8,128)(2,1)S(1)}, bf16[128,256]{1,0:T(8,128)(2,1)S(1)}, u32[]{:S(2)}, u32[]{:S(2)}) collective-permute-start(bf16[128,256]{1,0:T(8,128)(2,1)S(1)} %add_convert_fusion), channel_id=1, source_target_pairs={{0,6},{1,7},{2,16},{3,17},{4,22},{5,23},{6,0},{7,1},{8,26},{9,27},... | collective-permute-start | bytes 196616 | tf_op jit(solution)/shard_map/ppermute | solution.py:33
  41.2 2.9 %collective-permute-start.15 = (bf16[256,256]{1,0:T(8,128)(2,1)S(1)}, bf16[256,256]{1,0:T(8,128)(2,1)S(1)}, u32[]{:S(2)}, u32[]{:S(2)}) collective-permute-start(bf16[256,256]{1,0:T(8,128)(2,1)S(1)} %pad_maximum_fusion.2), channel_id=1, source_target_pairs={{0,2},{1,3},{2,0},{3,1},{4,6},{5,7},{6,4},{7,5},{8,10},{9,11},{10,... | collective-permute-start | bytes 393224 | tf_op jit(solution)/shard_map/ppermute | solution.py:33
  42.0 2.2 %collective-permute-start.16 = (bf16[128,256]{1,0:T(8,128)(2,1)S(1)}, bf16[128,256]{1,0:T(8,128)(2,1)S(1)}, u32[]{:S(2)}, u32[]{:S(2)}) collective-permute-start(bf16[128,256]{1,0:T(8,128)(2,1)S(1)} %collective-permute-done.13), channel_id=1, source_target_pairs={{0,2},{1,3},{2,0},{3,1},{4,6},{5,7},{6,4},{7,5},{8,10},{9,11},{10,... | collective-permute-start | bytes 196616 | tf_op jit(solution)/shard_map/ppermute | solution.py:33
  43.7 1.3 %collective-permute-start.17 = (bf16[128,256]{1,0:T(8,128)(2,1)S(1)}, bf16[128,256]{1,0:T(8,128)(2,1)S(1)}, u32[]{:S(2)}, u32[]{:S(2)}) collective-permute-start(bf16[128,256]{1,0:T(8,128)(2,1)S(1)} %collective-permute-done.14), channel_id=1, source_target_pairs={{0,2},{1,3},{2,0},{3,1},{4,6},{5,7},{6,4},{7,5},{8,10},{9,11},{10,... | collective-permute-start | bytes 196616 | tf_op jit(solution)/shard_map/ppermute | solution.py:33

commit v4 on v3

--- a/solution.py
+++ b/solution.py
@@ -62,52 +62,63 @@
             at += 1
 
 
-def tile_sums(steps, prebuilt, n_columns, seeded, *refs):
+def tile_sums(groups, prebuilt, n_columns, seeded, *refs):
     refs, out = refs[:-1], refs[-1]
     if seeded:
         refs, seed = refs[:-1], refs[-1]
     refs, columns = refs[:-n_columns], refs[-n_columns:]
     total = seed[...] if seeded else None
     panel = out.shape[0]
-    tile = sum(part.shape[0] for part in columns) // (2 * len(steps))
-    at = 0
-    for part in columns:
-        for i in range(0, part.shape[0], 2 * tile):
-            size = 2 * tile
+    size = sum(part.shape[0] for part in columns) // sum(len(steps) for steps in groups)
+    blocks = [part.at[pl.ds(i, size), :] for part in columns for i in range(0, part.shape[0], size)]
+    for at, steps in enumerate(groups):
+        for i, step in enumerate(steps):
             if prebuilt:
-                left = refs[0][at]
+                left = refs[at][i]
             else:
-                left = masked_pair(*refs, panel // refs[3].shape[2], *steps[at])
-            terms = jnp.dot(left, part[i : i + size, :], preferred_element_type=F32)
+                left = masked_pair(*refs, panel // refs[3].shape[2], *step)
+            terms = jnp.dot(left, blocks.pop(0)[...], preferred_element_type=F32)
             for s in range(terms.shape[0] // panel):
                 term = terms[s * panel : (s + 1) * panel]
                 total = term if total is None else total + term
-            at += 1
     out[...] = total.astype(out.dtype)
 
 
-def update(place, own, got, feats, far_feats, out_grad, far_out_grad, w_self, w_neigh, value, keep_top, keep_low, send_top, send_low, side):
+def summed(total, got):
+    return (total[...].astype(F32) + got[...].astype(F32)).astype(BF16)
+
+
+def in_order(place, mine, far):
+    first_rep = jnp.full(mine.shape, place[3]) == 0
+    return jnp.concatenate(
+        [jnp.where(first_rep, mine[...], far[...]), jnp.where(first_rep, far[...], mine[...])], axis=0
+    )
+
+
+def update_first(place, total, got, feats, far_feats, w_self, w_neigh, x, aggregate, pre):
+    x[...] = in_order(place, feats, far_feats)
+    aggregate[...] = summed(total, got)
+    pre[...] = jnp.dot(x[...], w_self[...], preferred_element_type=F32) + jnp.dot(
+        aggregate[...], w_neigh[: aggregate.shape[1], :], preferred_element_type=F32
+    )
+
+
+def update_second(place, total, got, x, first_aggregate, first_pre, out_grad, far_out_grad, w_neigh, *outs):
+    value, keep_top, keep_low, send_top, send_low, side = outs
     side[...] = jnp.full(side.shape, place[2])
-    rows = feats.shape[0]
-    first_rep = jnp.full((rows, feats.shape[1]), place[3]) == 0
-
-    def in_order(mine, far):
-        return jnp.concatenate([jnp.where(first_rep, mine, far), jnp.where(first_rep, far, mine)], axis=0)
-
-    x = in_order(feats[...], far_feats[...])
-    g = in_order(out_grad[...], far_out_grad[...]).astype(F32)
-    aggregate = (own[...].astype(F32) + got[...].astype(F32)).astype(BF16)
-    pre = jnp.dot(x, w_self[...], preferred_element_type=F32) + jnp.dot(
-        aggregate, w_neigh[...], preferred_element_type=F32
-    )
+    rows, split = out_grad.shape[0], first_aggregate.shape[1]
+    second_aggregate = summed(total, got)
+    aggregate = jnp.concatenate([first_aggregate[...], second_aggregate], axis=1)
+    pre = first_pre[...] + jnp.dot(second_aggregate, w_neigh[split:, :], preferred_element_type=F32)
     sigma = jax.nn.sigmoid(pre)
     both = (pre * sigma).astype(BF16)
-    value[...] = jnp.where(first_rep, both[:rows], both[rows:])
+    value[...] = jnp.where(jnp.full(value.shape, place[3]) == 0, both[:rows], both[rows:])
+    g = in_order(place, out_grad, far_out_grad).astype(F32)
     delta = (g * sigma * (1.0 + pre * (1.0 - sigma))).astype(BF16)
     first_core = jnp.full(x.shape, place[2]) == 0
     for left, top, low in (
-        (jnp.where(first_core, aggregate, x), send_top, send_low),
-        (jnp.where(first_core, x, aggregate), keep_top, keep_low),
+        (jnp.where(first_core, aggregate, x[...]), send_top, send_low),
+        (jnp.where(first_core, x[...], aggregate), keep_top, keep_low),
     ):
         grad = lax.dot_general(left, delta, (((0,), (0,)), ((), ())), preferred_element_type=F32)
         top[...] = grad[: top.shape[0]]
@@ -136,7 +147,8 @@
     barrier = lax.optimization_barrier
 
     hops = [bit | 1 for bit in bits_below(n_node)[:-1]]
-    turned = hops[-1:] + hops[:-1]
+    plain = hops
+    hops, turned = [plain[1], plain[0], plain[2]], [plain[0], plain[2], plain[1]]
     rep_bits = bits_below(n_rep)
 
     def trade(x, even, odd):
@@ -156,72 +168,88 @@
     for shift in bits_below(n_node.bit_length()):
         parity = parity ^ (parity >> shift)
     place = jnp.stack([node, rep, parity & 1, rep & 1]).astype(jnp.int32)
-    held = jnp.concatenate([feats, got], axis=0)
-    for even, odd in zip(hops[1:-1], turned[1:-1], strict=True):
-        got = trade(held, (even, 0), (odd, 0))
-        far, got, place, row_ids, live_count = barrier((far, got, place, row_ids, live_count))
-        held = jnp.concatenate([held, got], axis=0)
-    late = trade(held, (hops[-1], 0), (turned[-1], 0))
-    other = core_swap(held)
-
     masks_even, masks_odd = doubling_masks(hops), doubling_masks(turned)
-    half = len(masks_even) // 2
-
-    def steps_of(mate, first):
-        return [
-            ((mate, mate), masks_even[i : i + 2], masks_odd[i : i + 2]) for i in range(first, first + half, 2)
-        ]
-
-    groups = [steps_of(False, 0), steps_of(False, half), steps_of(True, 0) + steps_of(True, half)]
+    pairs = [
+        [((mate, mate), masks_even[i : i + 2], masks_odd[i : i + 2]) for i in range(0, len(masks_even), 2)]
+        for mate in (False, True)
+    ]
+    early = len(pairs[0]) // 2
+    groups = [pairs[0][:early], pairs[0][early:], pairs[1]]
     panel = n_rep * rows
     slots = tiles.shape[1]
     left_sizes = [len(steps) * slots * panel * 2 * rows * 2 for steps in groups]
     prebuilt = sum(left_sizes) <= 4 * 1024 * 1024
+    halves = [slice(0, width // 2), slice(width // 2, width)]
+    held = [jnp.concatenate([feats[:, half], got[:, half]], axis=0) for half in halves]
+    for even, odd in zip(hops[1:-1], turned[1:-1], strict=True):
+        gots = [trade(part, (even, 0), (odd, 0)) for part in held]
+        gots[0], place, row_ids, live_count = barrier((gots[0], place, row_ids, live_count))
+        gots[-1], far = barrier((gots[-1], far))
+        held = [jnp.concatenate([part, got], axis=0) for part, got in zip(held, gots, strict=True)]
     tables = [place, row_ids, live_count, tiles]
     table_specs = [SMEM] * 3 + [VMEM]
+    gots = [trade(part, (hops[-1], 0), (turned[-1], 0)) for part in held]
     if prebuilt:
         lefts = call(
             functools.partial(build_lefts, sum(groups, [])),
             tuple(jax.ShapeDtypeStruct((len(steps), slots * panel, 2 * rows), BF16) for steps in groups),
             table_specs, 0, 3 * sum(left_sizes),
         )(*tables)
-
-    def sums(index, columns, seed, dtype):
-        steps = groups[index]
-        given, specs = ([lefts[index]], [VMEM]) if prebuilt else (tables, table_specs)
+        gots[0], lefts = barrier((gots[0], lefts))
+
+    def sums(indices, columns, seed, dtype):
+        steps = [groups[i] for i in indices]
+        given, specs = ([lefts[i] for i in indices], [VMEM] * len(indices)) if prebuilt else (tables, table_specs)
         more = columns + ([seed] if seed is not None else [])
-        flops = len(steps) * slots * panel * 2 * rows * width * 2
+        size = sum(left_sizes[i] for i in indices)
         return call(
             functools.partial(tile_sums, steps, prebuilt, len(columns), seed is not None),
-            jax.ShapeDtypeStruct((panel, width), dtype), specs + [VMEM] * len(more), flops, left_sizes[index],
+            jax.ShapeDtypeStruct((panel, columns[0].shape[1]), dtype),
+            specs + [VMEM] * len(more), size * columns[0].shape[1], size,
         )(*given, *more)
 
-    total = sums(0, [held], None, F32)
-    late, total = barrier((late, total))
-    other_late = core_swap(late)
-    total = sums(1, [late], total, F32)
-    total = sums(2, [other, other_late], total, BF16 if n_rep == 2 else F32)
-
-    for bit in rep_bits[:-1]:
-        got = trade(total[bit * rows :].astype(BF16), (0, bit), (0, bit))
-        total = total[: bit * rows].astype(F32) + got.astype(F32)
-    total = total.astype(BF16)
-    got = trade(total, (0, 1), (0, 1))
-
+    sums_type = BF16 if n_rep == 2 else F32
+    first = jnp.concatenate([held[0], gots[0]], axis=0)
+    own = sums([0, 1], [first], None, F32)
+    gots[1], own = barrier((gots[1], own))
+    second = jnp.concatenate([held[1], gots[1]], axis=0)
+    total = sums([2], [core_swap(first)], own, sums_type)
+    mates = core_swap(second)
+    second, total = barrier((second, total))
+    totals = [total, sums([0, 1, 2], [second, mates], None, sums_type)]
+
+    gots = []
+    for i in (0, 1):
+        for bit in rep_bits[:-1]:
+            got = trade(totals[i][bit * rows :].astype(BF16), (0, bit), (0, bit))
+            totals[i] = totals[i][: bit * rows].astype(F32) + got.astype(F32)
+        totals[i] = totals[i].astype(BF16)
+        gots.append(trade(totals[i], (0, 1), (0, 1)))
+
+    two_blocks = (2 * rows, width)
+    x, aggregate, pre = call(
+        update_first,
+        (
+            jax.ShapeDtypeStruct(two_blocks, BF16),
+            jax.ShapeDtypeStruct(totals[0].shape, BF16),
+            jax.ShapeDtypeStruct(two_blocks, F32),
+        ),
+        [SMEM] + [VMEM] * 6, 6 * rows * width * width, 1 << 19,
+    )(place, totals[0], gots[0], feats, far[:rows], w_self, w_neigh)
     half_grad = jax.ShapeDtypeStruct((width // 2, width), F32)
     value, keep_top, keep_low, send_top, send_low, side = call(
-        update,
+        update_second,
         (
             jax.ShapeDtypeStruct((rows, width), BF16), half_grad, half_grad, half_grad, half_grad,
             jax.ShapeDtypeStruct((1, width), jnp.int32),
         ),
-        [SMEM] + [VMEM] * 8, 16 * rows * width * width, 1 << 20,
-    )(place, total, got, feats, far[:rows], out_grad, far[rows:], w_self, w_neigh)
+        [SMEM] + [VMEM] * 8, 10 * rows * width * width, 1 << 20,
+    )(place, totals[1], gots[1], x, aggregate, pre, out_grad, far[rows:], w_neigh)
     grads = [keep_top + core_swap(send_top), keep_low + core_swap(send_low)]
     layer_out = call(copied, jax.ShapeDtypeStruct((rows, width), BF16), [VMEM], 0, 4 * rows * width)(value)
 
-    order_even = hops
-    order_odd = hops[::-1]
+    order_even = [plain[0], plain[2], plain[1]]
+    order_odd = [plain[1], plain[0], plain[2]]
     steps = [((0, bit), (0, bit)) for bit in rep_bits[:-1]]
     steps += [((even, 0), (odd, 0)) for even, odd in zip(order_even, order_odd, strict=True)]
     for even, odd in steps[:-1]:

time: 46.1 us -> 45.1 us (0.978)
  waiting for transfers between devices: 15.3 us -> 10.3 us
  starting transfers between devices: 23.3 us -> 26 us
  Pallas kernels: 3.62 us -> 4.81 us
    ppermute x18 -> x21, waiting for transfers between devices: 15.3 us -> 10.3 us  [swap(): return lax.ppermute(x, ('node', 'rep'), pairs)]
    ppermute x18 -> x21, starting transfers between devices: 23.3 us -> 26 us  [swap(): return lax.ppermute(x, ('node', 'rep'), pairs)]
    pallas_call x1 -> x2, Pallas kernels: 1.12 us -> 1.76 us  [the longest x1 1 us: local(): call(update_second, (jax.ShapeDtypeStruct((rows, width), BF16), half_grad...]
    pallas_call x3, Pallas kernels: 1.02 us -> 1.58 us  [sums(): call(functools.partial(tile_sums, steps, prebuilt, len(columns), seed is...]
  transfers between devices with their start and end apart: 18 -> 21, of which waited for: 13 -> 11; matrix products, arithmetic and copies ran while one was open for 2% -> 3% of each run, Pallas kernels for 4% -> 8%
where the time goes in v4:
time: 45.1 us; the launch traced here: 44.9 us
  starting transfers between devices  26 us (58%)
  waiting for transfers between devices  10.3 us (23%)
  Pallas kernels  4.81 us (11%)
  local copies, waits for them, and re-layouts  1.77 us (4%)
  other arithmetic  1.15 us (3%)
  between operations  0.86 us (2%)
    ppermute x21, starting transfers between devices, swap(): return lax.ppermute(x, ('node', 'rep'), pairs)  26 us
    ppermute x21, waiting for transfers between devices, swap(): return lax.ppermute(x, ('node', 'rep'), pairs)  10.3 us
    pallas_call x3, Pallas kernels, sums(): call(functools.partial(tile_sums, steps, prebuilt, len(columns), seed is...  1.58 us
    pallas_call x1, Pallas kernels, local(): call(update_second, (jax.ShapeDtypeStruct((rows, width), BF16), half_grad...  1 us
  transfers between devices with their start and end apart: 21, of which 11 were waited for; matrix products, arithmetic and copies ran while one was open for 3% of the time, Pallas kernels for 8%

profile of v4, /device:TPU:0, one launch (start us, length us, event | category | flops | bytes accessed | tf_op | source)
XLA Modules:
  0.0 44.9 jit_solution(9271152262523108272)
XLA Ops:
  0.6 0.0 copy-start.2
  0.6 0.0 copy-start
  0.7 2.5 %collective-permute-start = (bf16[128,256]{1,0:T(8,128)(2,1)}, bf16[128,256]{1,0:T(8,128)(2,1)S(1)}, u32[]{:S(2)}, u32[]{:S(2)}) collective-permute-start(bf16[128,256]{1,0:T(8,128)(2,1)} %x_ref.1), channel_id=1, source_target_pairs={{0,10},{1,11},{2,16},{3,17},{4,22},{5,23},{6,12},{7,13},{8,26},{9,... | collective-permute-start | bytes 196616 | tf_op jit(solution)/shard_map/ppermute | solution.py:33
  3.2 0.9 %copy-done.4 = bf16[128,256]{1,0:T(8,128)(2,1)S(1)} copy-done((bf16[128,256]{1,0:T(8,128)(2,1)S(1)}, bf16[128,256]{1,0:T(8,128)(2,1)}, u32[]{:S(2)}) %copy-start.4) | copy-done | bytes 65560
  4.1 0.0 copy-done.2
  4.1 1.6 %collective-permute-start.4 = (bf16[256,256]{1,0:T(8,128)(2,1)S(1)}, bf16[256,256]{1,0:T(8,128)(2,1)S(1)}, u32[]{:S(2)}, u32[]{:S(2)}) collective-permute-start(bf16[256,256]{1,0:T(8,128)(2,1)S(1)} %pad_maximum_fusion.3), channel_id=1, source_target_pairs={{0,1},{1,0},{2,3},{3,2},{4,5},{5,4},{6,7},{7,6},{8,9},{9,8},{10,11... | collective-permute-start | bytes 393224 | tf_op jit(solution)/shard_map/ppermute | solution.py:33
  5.6 0.0 collective-permute-done
  5.7 3.4 %collective-permute-start.1 = (bf16[256,128]{1,0:T(8,128)(2,1)S(1)}, bf16[256,128]{1,0:T(8,128)(2,1)S(1)}, u32[]{:S(2)}, u32[]{:S(2)}) collective-permute-start(bf16[256,128]{1,0:T(8,128)(2,1)S(1)} %pad_maximum_fusion.8), channel_id=1, source_target_pairs={{0,18},{1,19},{2,4},{3,5},{4,2},{5,3},{6,20},{7,21},{8,14},{9,15},... | collective-permute-start | bytes 196616 | tf_op jit(solution)/shard_map/ppermute | solution.py:33
  9.1 0.1 collective-permute-start.3
  9.2 0.1 pad_add_fusion.place
  9.2 0.8 %copy.11 = s32[1,1,16,2]{3,2,1,0:T(8,128)S(1)} copy(s32[1,1,16,2]{2,3,1,0:T(2,128)} %param.9) | data formatting | bytes 256 | tf_op jit(solution)/shard_map/optimization_barrier | solution.py:163
  10.0 0.1 reshape_squeeze.3.rows
  10.1 0.9 %collective-permute-done.1 = bf16[256,128]{1,0:T(8,128)(2,1)S(1)} collective-permute-done((bf16[256,128]{1,0:T(8,128)(2,1)S(1)}, bf16[256,128]{1,0:T(8,128)(2,1)S(1)}, u32[]{:S(2)}, u32[]{:S(2)}) %collective-permute-start.1) | collective-permute-done | bytes 65568 | tf_op jit(solution)/shard_map/ppermute | solution.py:33
  11.0 2.3 %collective-permute-start.2 = (bf16[512,128]{1,0:T(8,128)(2,1)S(1)}, bf16[512,128]{1,0:T(8,128)(2,1)S(1)}, u32[]{:S(2)}, u32[]{:S(2)}) collective-permute-start(bf16[512,128]{1,0:T(8,128)(2,1)S(1)} %pad_maximum_fusion.2), channel_id=1, source_target_pairs={{0,6},{1,7},{2,8},{3,9},{4,14},{5,15},{6,0},{7,1},{8,2},{9,3},{10,... | collective-permute-start | bytes 393224 | tf_op jit(solution)/shard_map/ppermute | solution.py:33
  13.3 0.4 collective-permute-done.3
  13.7 0.0 collective-permute-done.4
  13.7 0.0 copy-start.5
  13.7 1.9 %collective-permute-start.5 = (bf16[512,128]{1,0:T(8,128)(2,1)S(1)}, bf16[512,128]{1,0:T(8,128)(2,1)S(1)}, u32[]{:S(2)}, u32[]{:S(2)}) collective-permute-start(bf16[512,128]{1,0:T(8,128)(2,1)S(1)} %pad_maximum_fusion.4), channel_id=1, source_target_pairs={{0,6},{1,7},{2,8},{3,9},{4,14},{5,15},{6,0},{7,1},{8,2},{9,3},{10,... | collective-permute-start | bytes 393224 | tf_op jit(solution)/shard_map/ppermute | solution.py:33
  15.6 0.0 copy-done
  15.6 0.0 copy-done.5
  15.6 0.8 %shard_map.95 = (bf16[2,512,256]{2,1,0:T(8,128)(2,1)S(1)}, bf16[2,512,256]{2,1,0:T(8,128)(2,1)S(1)}, bf16[4,512,256]{2,1,0:T(8,128)(2,1)S(1)}) custom-call(s32[4]{0:T(128)S(1)} %pad_add_fusion.place, s32[32]{0:T(128)S(1)} %reshape_squeeze.3.rows, s32[16]{0:T(128)S(1)} %bitcast.9, bf16[16,2,128,128]{3,2,1,0:T(8,128)(2,1)S(1)} %bitcast.8), custom_call_target="tpu_custom_call" | custom-call | bytes 6291456 | tf_op jit(solution)/shard_map/pallas_call | solution.py:193
  16.5 0.0 collective-permute-done.2
  16.5 0.1 collective-permute-start.6
  16.6 0.4 shard_map.96.refs_2_
  17.0 1.3 %collective-permute-done.5 = bf16[512,128]{1,0:T(8,128)(2,1)S(1)} collective-permute-done((bf16[512,128]{1,0:T(8,128)(2,1)S(1)}, bf16[512,128]{1,0:T(8,128)(2,1)S(1)}, u32[]{:S(2)}, u32[]{:S(2)}) %collective-permute-start.5) | collective-permute-done | bytes 131104 | tf_op jit(solution)/shard_map/ppermute | solution.py:33
  18.3 0.1 collective-permute-start.7
  18.4 0.0 collective-permute-done.6.refs_1_
  18.4 0.4 shard_map.97.total
  18.8 1.6 %collective-permute-start.9 = (bf16[256,128]{1,0:T(8,128)(2,1)S(1)}, bf16[256,128]{1,0:T(8,128)(2,1)S(1)}, u32[]{:S(2)}, u32[]{:S(2)}) collective-permute-start(bf16[256,128]{1,0:T(8,128)(2,1)S(1)} %shard_map.97.total), channel_id=1, source_target_pairs={{0,1},{1,0},{2,3},{3,2},{4,5},{5,4},{6,7},{7,6},{8,9},{9,8},{10,11... | collective-permute-start | bytes 196616 | tf_op jit(solution)/shard_map/ppermute | solution.py:33
  20.4 0.0 collective-permute-done.7.refs_4_
  20.4 0.7 %shard_map.98.total = bf16[256,128]{1,0:T(8,128)(2,1)S(1)} custom-call(bf16[2,512,256]{2,1,0:T(8,128)(2,1)S(1)} %get-tuple-element.52.refs_0_, bf16[2,512,256]{2,1,0:T(8,128)(2,1)S(1)} %get-tuple-element.53.refs_1_, bf16[4,512,256]{2,1,0:T(8,128)(2,1)S(1)} %get-tuple-element.54.refs_0_.refs_2_, bf16[1024,128]{1,0:T(8,128)(2,1)S(1)} %pad_maximum_fusion.1.refs_3_, ...), custom_call_target="tpu_custom_call" | custom-call | flops 268435456 | bytes 2097152 | tf_op jit(solution)/shard_map/pallas_call | solution.py:205
  21.1 0.0 copy-start.1
  21.1 0.0 copy-start.3
  21.1 1.1 %collective-permute-start.8 = (bf16[256,128]{1,0:T(8,128)(2,1)S(1)}, bf16[256,128]{1,0:T(8,128)(2,1)S(1)}, u32[]{:S(2)}, u32[]{:S(2)}) collective-permute-start(bf16[256,128]{1,0:T(8,128)(2,1)S(1)} %shard_map.98.total), channel_id=1, source_target_pairs={{0,1},{1,0},{2,3},{3,2},{4,5},{5,4},{6,7},{7,6},{8,9},{9,8},{10,11... | collective-permute-start | bytes 196616 | tf_op jit(solution)/shard_map/ppermute | solution.py:33
  22.2 1.2 %collective-permute-done.9.got = bf16[256,128]{1,0:T(8,128)(2,1)S(1)} collective-permute-done((bf16[256,128]{1,0:T(8,128)(2,1)S(1)}, bf16[256,128]{1,0:T(8,128)(2,1)S(1)}, u32[]{:S(2)}, u32[]{:S(2)}) %collective-permute-start.9) | collective-permute-done | bytes 65568 | tf_op jit(solution)/shard_map/ppermute | solution.py:33
  23.4 0.0 copy-done.1
  23.4 0.0 copy-done.3
  23.4 0.8 %shard_map.99 = (bf16[256,256]{1,0:T(8,128)(2,1)S(1)}, bf16[256,128]{1,0:T(8,128)(2,1)S(1)}, f32[256,256]{1,0:T(8,128)S(1)}) custom-call(s32[4]{0:T(128)S(1)} %pad_add_fusion.place, bf16[256,128]{1,0:T(8,128)(2,1)S(1)} %shard_map.97.total, bf16[256,128]{1,0:T(8,128)(2,1)S(1)} %collective-permute-done.9.got, bf16[128,256]{1,0:T(8,128)(2,1)S(1)} %shard_map.94.feats, ...), custom_call_target="tpu_custom_call" | custom-call | flops 50331648 | bytes 524288 | tf_op jit(solution)/shard_map/pallas_call | solution.py:230
  24.2 1.3 %collective-permute-done.8.got = bf16[256,128]{1,0:T(8,128)(2,1)S(1)} collective-permute-done((bf16[256,128]{1,0:T(8,128)(2,1)S(1)}, bf16[256,128]{1,0:T(8,128)(2,1)S(1)}, u32[]{:S(2)}, u32[]{:S(2)}) %collective-permute-start.8) | collective-permute-done | bytes 65568 | tf_op jit(solution)/shard_map/ppermute | solution.py:33
  25.5 1.0 %shard_map.100 = (bf16[128,256]{1,0:T(8,128)(2,1)S(1)}, f32[128,256]{1,0:T(8,128)S(1)}, f32[128,256]{1,0:T(8,128)S(1)}, f32[128,256]{1,0:T(8,128)S(1)}, f32[128,256]{1,0:T(8,128)S(1)}, /*index=5*/s32[1,256]{1,0:T(1,128)S(1)}) custom-call(s32[4]{0:T(128)S(1)} %pad_add_fusion.place, bf16[256,128]{1,0:T(8,128)(2,1)S(1)} %shard_map.98.total, ...), custom_call_target="tpu_custom_call" | custom-call | flops 83886080 | bytes 1048576 | tf_op jit(solution)/shard_map/pallas_call | solution.py:240
  26.5 0.1 collective-permute-start.10
  26.5 0.6 %shard_map.101 = bf16[128,256]{1,0:T(8,128)(2,1)} custom-call(bf16[128,256]{1,0:T(8,128)(2,1)S(1)} %get-tuple-element.67.x_ref), custom_call_target="tpu_custom_call" | custom-call | bytes 131072 | tf_op jit(solution)/shard_map/pallas_call | solution.py:249
  27.2 0.5 %collective-permute-start.13 = (f32[128,256]{1,0:T(8,128)S(1)}, f32[128,256]{1,0:T(8,128)S(1)}, u32[]{:S(2)}, u32[]{:S(2)}) collective-permute-start(f32[128,256]{1,0:T(8,128)S(1)} %get-tuple-element.74), channel_id=1, source_target_pairs={{0,2},{1,3},{2,0},{3,1},{4,6},{5,7},{6,4},{7,5},{8,10},{9,11},{10,... | collective-permute-start | bytes 393224 | tf_op jit(solution)/shard_map/ppermute | solution.py:33
  27.7 0.2 collective-permute-done.10
  27.9 1.8 %collective-permute-start.11 = (bf16[128,256]{1,0:T(8,128)(2,1)S(1)}, bf16[128,256]{1,0:T(8,128)(2,1)S(1)}, u32[]{:S(2)}, u32[]{:S(2)}) collective-permute-start(bf16[128,256]{1,0:T(8,128)(2,1)S(1)} %add_convert_fusion.5), channel_id=1, source_target_pairs={{0,18},{1,19},{2,8},{3,9},{4,14},{5,15},{6,20},{7,21},{8,2},{9,3},... | collective-permute-start | bytes 196616 | tf_op jit(solution)/shard_map/ppermute | solution.py:33
  29.7 0.0 collective-permute-done.13
  29.7 1.0 %collective-permute-start.14 = (bf16[128,256]{1,0:T(8,128)(2,1)S(1)}, bf16[128,256]{1,0:T(8,128)(2,1)S(1)}, u32[]{:S(2)}, u32[]{:S(2)}) collective-permute-start(bf16[128,256]{1,0:T(8,128)(2,1)S(1)} %add_convert_fusion.2), channel_id=1, source_target_pairs={{0,18},{1,19},{2,8},{3,9},{4,14},{5,15},{6,20},{7,21},{8,2},{9,3},... | collective-permute-start | bytes 196616 | tf_op jit(solution)/shard_map/ppermute | solution.py:33
  30.7 2.0 %collective-permute-done.11 = bf16[128,256]{1,0:T(8,128)(2,1)S(1)} collective-permute-done((bf16[128,256]{1,0:T(8,128)(2,1)S(1)}, bf16[128,256]{1,0:T(8,128)(2,1)S(1)}, u32[]{:S(2)}, u32[]{:S(2)}) %collective-permute-start.11) | collective-permute-done | bytes 65568 | tf_op jit(solution)/shard_map/ppermute | solution.py:33
  32.7 2.0 %collective-permute-start.12 = (bf16[128,256]{1,0:T(8,128)(2,1)S(1)}, bf16[128,256]{1,0:T(8,128)(2,1)S(1)}, u32[]{:S(2)}, u32[]{:S(2)}) collective-permute-start(bf16[128,256]{1,0:T(8,128)(2,1)S(1)} %add_convert_fusion.4), channel_id=1, source_target_pairs={{0,6},{1,7},{2,16},{3,17},{4,22},{5,23},{6,0},{7,1},{8,26},{9,27},... | collective-permute-start | bytes 196616 | tf_op jit(solution)/shard_map/ppermute | solution.py:33
  34.7 0.0 collective-permute-done.14
  34.7 1.2 %collective-permute-start.15 = (bf16[128,256]{1,0:T(8,128)(2,1)S(1)}, bf16[128,256]{1,0:T(8,128)(2,1)S(1)}, u32[]{:S(2)}, u32[]{:S(2)}) collective-permute-start(bf16[128,256]{1,0:T(8,128)(2,1)S(1)} %add_convert_fusion.1), channel_id=1, source_target_pairs={{0,6},{1,7},{2,16},{3,17},{4,22},{5,23},{6,0},{7,1},{8,26},{9,27},... | collective-permute-start | bytes 196616 | tf_op jit(solution)/shard_map/ppermute | solution.py:33
  35.9 0.8 %collective-permute-done.12 = bf16[128,256]{1,0:T(8,128)(2,1)S(1)} collective-permute-done((bf16[128,256]{1,0:T(8,128)(2,1)S(1)}, bf16[128,256]{1,0:T(8,128)(2,1)S(1)}, u32[]{:S(2)}, u32[]{:S(2)}) %collective-permute-start.12) | collective-permute-done | bytes 65568 | tf_op jit(solution)/shard_map/ppermute | solution.py:33
  36.7 1.3 %collective-permute-start.16 = (bf16[128,256]{1,0:T(8,128)(2,1)S(1)}, bf16[128,256]{1,0:T(8,128)(2,1)S(1)}, u32[]{:S(2)}, u32[]{:S(2)}) collective-permute-start(bf16[128,256]{1,0:T(8,128)(2,1)S(1)} %add_convert_fusion.3), channel_id=1, source_target_pairs={{0,10},{1,11},{2,4},{3,5},{4,2},{5,3},{6,12},{7,13},{8,14},{9,15},... | collective-permute-start | bytes 196616 | tf_op jit(solution)/shard_map/ppermute | solution.py:33
  38.0 0.5 %collective-permute-done.15 = bf16[128,256]{1,0:T(8,128)(2,1)S(1)} collective-permute-done((bf16[128,256]{1,0:T(8,128)(2,1)S(1)}, bf16[128,256]{1,0:T(8,128)(2,1)S(1)}, u32[]{:S(2)}, u32[]{:S(2)}) %collective-permute-start.15) | collective-permute-done | bytes 65568 | tf_op jit(solution)/shard_map/ppermute | solution.py:33
  38.5 1.6 %collective-permute-start.17 = (bf16[128,256]{1,0:T(8,128)(2,1)S(1)}, bf16[128,256]{1,0:T(8,128)(2,1)S(1)}, u32[]{:S(2)}, u32[]{:S(2)}) collective-permute-start(bf16[128,256]{1,0:T(8,128)(2,1)S(1)} %add_convert_fusion), channel_id=1, source_target_pairs={{0,10},{1,11},{2,4},{3,5},{4,2},{5,3},{6,12},{7,13},{8,14},{9,15},... | collective-permute-start | bytes 196616 | tf_op jit(solution)/shard_map/ppermute | solution.py:33
  40.1 0.3 collective-permute-start.18
  40.5 0.0 collective-permute-done.16
  40.5 0.9 %collective-permute-start.19 = (bf16[128,256]{1,0:T(8,128)(2,1)S(1)}, bf16[128,256]{1,0:T(8,128)(2,1)S(1)}, u32[]{:S(2)}, u32[]{:S(2)}) collective-permute-start(bf16[128,256]{1,0:T(8,128)(2,1)S(1)} %collective-permute-done.16), channel_id=1, source_target_pairs={{0,2},{1,3},{2,0},{3,1},{4,6},{5,7},{6,4},{7,5},{8,10},{9,11},{10,... | collective-permute-start | bytes 196616 | tf_op jit(solution)/shard_map/ppermute | solution.py:33
  41.3 0.9 %collective-permute-done.17 = bf16[128,256]{1,0:T(8,128)(2,1)S(1)} collective-permute-done((bf16[128,256]{1,0:T(8,128)(2,1)S(1)}, bf16[128,256]{1,0:T(8,128)(2,1)S(1)}, u32[]{:S(2)}, u32[]{:S(2)}) %collective-permute-start.17) | collective-permute-done | bytes 65568 | tf_op jit(solution)/shard_map/ppermute | solution.py:33
  42.3 0.9 %collective-permute-start.20 = (bf16[128,256]{1,0:T(8,128)(2,1)S(1)}, bf16[128,256]{1,0:T(8,128)(2,1)S(1)}, u32[]{:S(2)}, u32[]{:S(2)}) collective-permute-start(bf16[128,256]{1,0:T(8,128)(2,1)S(1)} %collective-permute-done.17), channel_id=1, source_target_pairs={{0,2},{1,3},{2,0},{3,1},{4,6},{5,7},{6,4},{7,5},{8,10},{9,11},{10,... | collective-permute-start | bytes 196616 | tf_op jit(solution)/shard_map/ppermute | solution.py:33
  43.2 0.0 collective-permute-done.18
  43.2 0.0 collective-permute-done.19
  43.2 0.9 %collective-permute-done.20 = bf16[128,256]{1,0:T(8,128)(2,1)S(1)} collective-permute-done((bf16[128,256]{1,0:T(8,128)(2,1)S(1)}, bf16[128,256]{1,0:T(8,128)(2,1)S(1)}, u32[]{:S(2)}, u32[]{:S(2)}) %collective-permute-start.20) | collective-permute-done | bytes 65568 | tf_op jit(solution)/shard_map/ppermute | solution.py:33
  44.0 0.9 %fusion = (f32[256,256]{1,0:T(8,128)}, f32[256,256]{1,0:T(8,128)}) fusion(bf16[256,256]{1,0:T(8,128)(2,1)S(1)} %collective-permute-done.18, pred[256]{0:T(512)(128)(4,1)S(1)} %compare_reduce_fusion, bf16[128,256]{1,0:T(8,128)(2,1)S(1)} %collective-permute-done.20, bf16[128,256]{1,0:T(8,128)(2,1)S(1)} %collective-permute-done.19, ...), kind=kLoop, calls=%fused_computation.4 | loop fusion | flops 1114112 | bytes 1048832 | tf_op jit(solution)/shard_map/jit(_where)/select_n | solution.py:269
  (19 shorter events, 0.3 us)
Async XLA Ops:
  0.6 3.4 %copy-start.2 = (bf16[128,256]{1,0:T(8,128)(2,1)S(1)}, bf16[128,256]{1,0:T(8,128)(2,1)}, u32[]{:S(2)}) copy-start(bf16[128,256]{1,0:T(8,128)(2,1)} %out_grad.1) | copy-start | bytes 196612
  0.6 15.0 %copy-start = (bf16[1,1,16,2,128,128]{5,4,3,2,1,0:T(8,128)(2,1)S(1)}, bf16[1,1,16,2,128,128]{5,4,3,2,1,0:T(8,128)(2,1)}, u32[]{:S(2)}) copy-start(bf16[1,1,16,2,128,128]{5,4,3,2,1,0:T(8,128)(2,1)} %param.8) | copy-start | bytes 3145732
  0.7 5.0 %collective-permute-start = (bf16[128,256]{1,0:T(8,128)(2,1)}, bf16[128,256]{1,0:T(8,128)(2,1)S(1)}, u32[]{:S(2)}, u32[]{:S(2)}) collective-permute-start(bf16[128,256]{1,0:T(8,128)(2,1)} %x_ref.1), channel_id=1, source_target_pairs={{0,10},{1,11},{2,16},{3,17},{4,22},{5,23},{6,12},{7,13},{8,26},{9,... | collective-permute-start | bytes 196616 | tf_op jit(solution)/shard_map/ppermute | solution.py:33
  3.2 0.9 %copy-start.4 = (bf16[128,256]{1,0:T(8,128)(2,1)S(1)}, bf16[128,256]{1,0:T(8,128)(2,1)}, u32[]{:S(2)}) copy-start(bf16[128,256]{1,0:T(8,128)(2,1)} %x_ref.1) | copy-start | bytes 196612
  4.1 9.6 %collective-permute-start.4 = (bf16[256,256]{1,0:T(8,128)(2,1)S(1)}, bf16[256,256]{1,0:T(8,128)(2,1)S(1)}, u32[]{:S(2)}, u32[]{:S(2)}) collective-permute-start(bf16[256,256]{1,0:T(8,128)(2,1)S(1)} %pad_maximum_fusion.3), channel_id=1, source_target_pairs={{0,1},{1,0},{2,3},{3,2},{4,5},{5,4},{6,7},{7,6},{8,9},{9,8},{10,11... | collective-permute-start | bytes 393224 | tf_op jit(solution)/shard_map/ppermute | solution.py:33
  5.7 5.3 %collective-permute-start.1 = (bf16[256,128]{1,0:T(8,128)(2,1)S(1)}, bf16[256,128]{1,0:T(8,128)(2,1)S(1)}, u32[]{:S(2)}, u32[]{:S(2)}) collective-permute-start(bf16[256,128]{1,0:T(8,128)(2,1)S(1)} %pad_maximum_fusion.8), channel_id=1, source_target_pairs={{0,18},{1,19},{2,4},{3,5},{4,2},{5,3},{6,20},{7,21},{8,14},{9,15},... | collective-permute-start | bytes 196616 | tf_op jit(solution)/shard_map/ppermute | solution.py:33
  9.1 4.6 %collective-permute-start.3 = (bf16[256,128]{1,0:T(8,128)(2,1)S(1)}, bf16[256,128]{1,0:T(8,128)(2,1)S(1)}, u32[]{:S(2)}, u32[]{:S(2)}) collective-permute-start(bf16[256,128]{1,0:T(8,128)(2,1)S(1)} %pad_maximum_fusion.9), channel_id=1, source_target_pairs={{0,18},{1,19},{2,4},{3,5},{4,2},{5,3},{6,20},{7,21},{8,14},{9,15},... | collective-permute-start | bytes 196616 | tf_op jit(solution)/shard_map/ppermute | solution.py:33
  11.0 5.4 %collective-permute-start.2 = (bf16[512,128]{1,0:T(8,128)(2,1)S(1)}, bf16[512,128]{1,0:T(8,128)(2,1)S(1)}, u32[]{:S(2)}, u32[]{:S(2)}) collective-permute-start(bf16[512,128]{1,0:T(8,128)(2,1)S(1)} %pad_maximum_fusion.2), channel_id=1, source_target_pairs={{0,6},{1,7},{2,8},{3,9},{4,14},{5,15},{6,0},{7,1},{8,2},{9,3},{10,... | collective-permute-start | bytes 393224 | tf_op jit(solution)/shard_map/ppermute | solution.py:33
  13.7 1.9 %copy-start.5 = (s32[1,1,16]{2,1,0:T(1,128)S(1)}, s32[1,1,16]{2,1,0:T(1,128)}, u32[]{:S(2)}) copy-start(s32[1,1,16]{2,1,0:T(1,128)} %param.10) | copy-start | bytes 196
  13.7 4.6 %collective-permute-start.5 = (bf16[512,128]{1,0:T(8,128)(2,1)S(1)}, bf16[512,128]{1,0:T(8,128)(2,1)S(1)}, u32[]{:S(2)}, u32[]{:S(2)}) collective-permute-start(bf16[512,128]{1,0:T(8,128)(2,1)S(1)} %pad_maximum_fusion.4), channel_id=1, source_target_pairs={{0,6},{1,7},{2,8},{3,9},{4,14},{5,15},{6,0},{7,1},{8,2},{9,3},{10,... | collective-permute-start | bytes 393224 | tf_op jit(solution)/shard_map/ppermute | solution.py:33
  16.5 1.9 %collective-permute-start.6 = (bf16[1024,128]{1,0:T(8,128)(2,1)S(1)}, bf16[1024,128]{1,0:T(8,128)(2,1)S(1)}, u32[]{:S(2)}, u32[]{:S(2)}) collective-permute-start(bf16[1024,128]{1,0:T(8,128)(2,1)S(1)} %pad_maximum_fusion.refs_2_), channel_id=1, source_target_pairs={{0,2},{1,3},{2,0},{3,1},{4,6},{5,7},{6,4},{7,5},{8,10},{9,11},{10,... | collective-permute-start | bytes 786440 | tf_op jit(solution)/shard_map/ppermute | solution.py:33
  18.3 2.1 %collective-permute-start.7 = (bf16[1024,128]{1,0:T(8,128)(2,1)S(1)}, bf16[1024,128]{1,0:T(8,128)(2,1)S(1)}, u32[]{:S(2)}, u32[]{:S(2)}) collective-permute-start(bf16[1024,128]{1,0:T(8,128)(2,1)S(1)} %pad_maximum_fusion.1.refs_3_), channel_id=1, source_target_pairs={{0,2},{1,3},{2,0},{3,1},{4,6},{5,7},{6,4},{7,5},{8,10},{9,11},{10,... | collective-permute-start | bytes 786440 | tf_op jit(solution)/shard_map/ppermute | solution.py:33
  18.8 4.6 %collective-permute-start.9 = (bf16[256,128]{1,0:T(8,128)(2,1)S(1)}, bf16[256,128]{1,0:T(8,128)(2,1)S(1)}, u32[]{:S(2)}, u32[]{:S(2)}) collective-permute-start(bf16[256,128]{1,0:T(8,128)(2,1)S(1)} %shard_map.97.total), channel_id=1, source_target_pairs={{0,1},{1,0},{2,3},{3,2},{4,5},{5,4},{6,7},{7,6},{8,9},{9,8},{10,11... | collective-permute-start | bytes 196616 | tf_op jit(solution)/shard_map/ppermute | solution.py:33
  21.1 2.3 %copy-start.1 = (bf16[256,256]{1,0:T(8,128)(2,1)S(1)}, bf16[256,256]{1,0:T(8,128)(2,1)}, u32[]{:S(2)}) copy-start(bf16[256,256]{1,0:T(8,128)(2,1)} %w_neigh.3) | copy-start | bytes 393220
  21.1 2.3 %copy-start.3 = (bf16[256,256]{1,0:T(8,128)(2,1)S(1)}, bf16[256,256]{1,0:T(8,128)(2,1)}, u32[]{:S(2)}) copy-start(bf16[256,256]{1,0:T(8,128)(2,1)} %w_self.1) | copy-start | bytes 393220
  21.1 4.3 %collective-permute-start.8 = (bf16[256,128]{1,0:T(8,128)(2,1)S(1)}, bf16[256,128]{1,0:T(8,128)(2,1)S(1)}, u32[]{:S(2)}, u32[]{:S(2)}) collective-permute-start(bf16[256,128]{1,0:T(8,128)(2,1)S(1)} %shard_map.98.total), channel_id=1, source_target_pairs={{0,1},{1,0},{2,3},{3,2},{4,5},{5,4},{6,7},{7,6},{8,9},{9,8},{10,11... | collective-permute-start | bytes 196616 | tf_op jit(solution)/shard_map/ppermute | solution.py:33
  26.5 1.4 %collective-permute-start.10 = (f32[128,256]{1,0:T(8,128)S(1)}, f32[128,256]{1,0:T(8,128)S(1)}, u32[]{:S(2)}, u32[]{:S(2)}) collective-permute-start(f32[128,256]{1,0:T(8,128)S(1)} %get-tuple-element.66), channel_id=1, source_target_pairs={{0,2},{1,3},{2,0},{3,1},{4,6},{5,7},{6,4},{7,5},{8,10},{9,11},{10,... | collective-permute-start | bytes 393224 | tf_op jit(solution)/shard_map/ppermute | solution.py:33
  27.2 2.5 %collective-permute-start.13 = (f32[128,256]{1,0:T(8,128)S(1)}, f32[128,256]{1,0:T(8,128)S(1)}, u32[]{:S(2)}, u32[]{:S(2)}) collective-permute-start(f32[128,256]{1,0:T(8,128)S(1)} %get-tuple-element.74), channel_id=1, source_target_pairs={{0,2},{1,3},{2,0},{3,1},{4,6},{5,7},{6,4},{7,5},{8,10},{9,11},{10,... | collective-permute-start | bytes 393224 | tf_op jit(solution)/shard_map/ppermute | solution.py:33
  27.9 4.8 %collective-permute-start.11 = (bf16[128,256]{1,0:T(8,128)(2,1)S(1)}, bf16[128,256]{1,0:T(8,128)(2,1)S(1)}, u32[]{:S(2)}, u32[]{:S(2)}) collective-permute-start(bf16[128,256]{1,0:T(8,128)(2,1)S(1)} %add_convert_fusion.5), channel_id=1, source_target_pairs={{0,18},{1,19},{2,8},{3,9},{4,14},{5,15},{6,20},{7,21},{8,2},{9,3},... | collective-permute-start | bytes 196616 | tf_op jit(solution)/shard_map/ppermute | solution.py:33
  29.7 5.0 %collective-permute-start.14 = (bf16[128,256]{1,0:T(8,128)(2,1)S(1)}, bf16[128,256]{1,0:T(8,128)(2,1)S(1)}, u32[]{:S(2)}, u32[]{:S(2)}) collective-permute-start(bf16[128,256]{1,0:T(8,128)(2,1)S(1)} %add_convert_fusion.2), channel_id=1, source_target_pairs={{0,18},{1,19},{2,8},{3,9},{4,14},{5,15},{6,20},{7,21},{8,2},{9,3},... | collective-permute-start | bytes 196616 | tf_op jit(solution)/shard_map/ppermute | solution.py:33
  32.7 4.0 %collective-permute-start.12 = (bf16[128,256]{1,0:T(8,128)(2,1)S(1)}, bf16[128,256]{1,0:T(8,128)(2,1)S(1)}, u32[]{:S(2)}, u32[]{:S(2)}) collective-permute-start(bf16[128,256]{1,0:T(8,128)(2,1)S(1)} %add_convert_fusion.4), channel_id=1, source_target_pairs={{0,6},{1,7},{2,16},{3,17},{4,22},{5,23},{6,0},{7,1},{8,26},{9,27},... | collective-permute-start | bytes 196616 | tf_op jit(solution)/shard_map/ppermute | solution.py:33
  34.7 3.8 %collective-permute-start.15 = (bf16[128,256]{1,0:T(8,128)(2,1)S(1)}, bf16[128,256]{1,0:T(8,128)(2,1)S(1)}, u32[]{:S(2)}, u32[]{:S(2)}) collective-permute-start(bf16[128,256]{1,0:T(8,128)(2,1)S(1)} %add_convert_fusion.1), channel_id=1, source_target_pairs={{0,6},{1,7},{2,16},{3,17},{4,22},{5,23},{6,0},{7,1},{8,26},{9,27},... | collective-permute-start | bytes 196616 | tf_op jit(solution)/shard_map/ppermute | solution.py:33
  36.7 3.8 %collective-permute-start.16 = (bf16[128,256]{1,0:T(8,128)(2,1)S(1)}, bf16[128,256]{1,0:T(8,128)(2,1)S(1)}, u32[]{:S(2)}, u32[]{:S(2)}) collective-permute-start(bf16[128,256]{1,0:T(8,128)(2,1)S(1)} %add_convert_fusion.3), channel_id=1, source_target_pairs={{0,10},{1,11},{2,4},{3,5},{4,2},{5,3},{6,12},{7,13},{8,14},{9,15},... | collective-permute-start | bytes 196616 | tf_op jit(solution)/shard_map/ppermute | solution.py:33
  38.5 3.8 %collective-permute-start.17 = (bf16[128,256]{1,0:T(8,128)(2,1)S(1)}, bf16[128,256]{1,0:T(8,128)(2,1)S(1)}, u32[]{:S(2)}, u32[]{:S(2)}) collective-permute-start(bf16[128,256]{1,0:T(8,128)(2,1)S(1)} %add_convert_fusion), channel_id=1, source_target_pairs={{0,10},{1,11},{2,4},{3,5},{4,2},{5,3},{6,12},{7,13},{8,14},{9,15},... | collective-permute-start | bytes 196616 | tf_op jit(solution)/shard_map/ppermute | solution.py:33
  40.1 3.0 %collective-permute-start.18 = (bf16[256,256]{1,0:T(8,128)(2,1)S(1)}, bf16[256,256]{1,0:T(8,128)(2,1)S(1)}, u32[]{:S(2)}, u32[]{:S(2)}) collective-permute-start(bf16[256,256]{1,0:T(8,128)(2,1)S(1)} %pad_maximum_fusion.5), channel_id=1, source_target_pairs={{0,2},{1,3},{2,0},{3,1},{4,6},{5,7},{6,4},{7,5},{8,10},{9,11},{10,... | collective-permute-start | bytes 393224 | tf_op jit(solution)/shard_map/ppermute | solution.py:33
  40.5 2.7 %collective-permute-start.19 = (bf16[128,256]{1,0:T(8,128)(2,1)S(1)}, bf16[128,256]{1,0:T(8,128)(2,1)S(1)}, u32[]{:S(2)}, u32[]{:S(2)}) collective-permute-start(bf16[128,256]{1,0:T(8,128)(2,1)S(1)} %collective-permute-done.16), channel_id=1, source_target_pairs={{0,2},{1,3},{2,0},{3,1},{4,6},{5,7},{6,4},{7,5},{8,10},{9,11},{10,... | collective-permute-start | bytes 196616 | tf_op jit(solution)/shard_map/ppermute | solution.py:33
  42.3 1.8 %collective-permute-start.20 = (bf16[128,256]{1,0:T(8,128)(2,1)S(1)}, bf16[128,256]{1,0:T(8,128)(2,1)S(1)}, u32[]{:S(2)}, u32[]{:S(2)}) collective-permute-start(bf16[128,256]{1,0:T(8,128)(2,1)S(1)} %collective-permute-done.17), channel_id=1, source_target_pairs={{0,2},{1,3},{2,0},{3,1},{4,6},{5,7},{6,4},{7,5},{8,10},{9,11},{10,... | collective-permute-start | bytes 196616 | tf_op jit(solution)/shard_map/ppermute | solution.py:33

commit v5 on v4

--- a/solution.py
+++ b/solution.py
@@ -88,34 +88,37 @@
     return (total[...].astype(F32) + got[...].astype(F32)).astype(BF16)
 
 
-def in_order(place, mine, far):
-    first_rep = jnp.full(mine.shape, place[3]) == 0
+def flag_like(flags, i, x):
+    return jnp.broadcast_to(flags[i : i + 1, : x.shape[1]], x.shape) == 0
+
+
+def in_order(flags, mine, far):
+    first_rep = flag_like(flags, 1, mine)
     return jnp.concatenate(
         [jnp.where(first_rep, mine[...], far[...]), jnp.where(first_rep, far[...], mine[...])], axis=0
     )
 
 
-def update_first(place, total, got, feats, far_feats, w_self, w_neigh, x, aggregate, pre):
-    x[...] = in_order(place, feats, far_feats)
+def update_first(flags, total, got, feats, far_feats, w_self, w_neigh, x, aggregate, pre):
+    x[...] = in_order(flags, feats, far_feats)
     aggregate[...] = summed(total, got)
     pre[...] = jnp.dot(x[...], w_self[...], preferred_element_type=F32) + jnp.dot(
         aggregate[...], w_neigh[: aggregate.shape[1], :], preferred_element_type=F32
     )
 
 
-def update_second(place, total, got, x, first_aggregate, first_pre, out_grad, far_out_grad, w_neigh, *outs):
-    value, keep_top, keep_low, send_top, send_low, side = outs
-    side[...] = jnp.full(side.shape, place[2])
+def update_second(flags, total, got, x, first_aggregate, first_pre, out_grad, far_out_grad, w_neigh, *outs):
+    value, keep_top, keep_low, send_top, send_low = outs
     rows, split = out_grad.shape[0], first_aggregate.shape[1]
     second_aggregate = summed(total, got)
     aggregate = jnp.concatenate([first_aggregate[...], second_aggregate], axis=1)
     pre = first_pre[...] + jnp.dot(second_aggregate, w_neigh[split:, :], preferred_element_type=F32)
     sigma = jax.nn.sigmoid(pre)
     both = (pre * sigma).astype(BF16)
-    value[...] = jnp.where(jnp.full(value.shape, place[3]) == 0, both[:rows], both[rows:])
-    g = in_order(place, out_grad, far_out_grad).astype(F32)
+    value[...] = jnp.where(flag_like(flags, 1, value), both[:rows], both[rows:])
+    g = in_order(flags, out_grad, far_out_grad).astype(F32)
     delta = (g * sigma * (1.0 + pre * (1.0 - sigma))).astype(BF16)
-    first_core = jnp.full(x.shape, place[2]) == 0
+    first_core = flag_like(flags, 0, x)
     for left, top, low in (
         (jnp.where(first_core, aggregate, x[...]), send_top, send_low),
         (jnp.where(first_core, x[...], aggregate), keep_top, keep_low),
@@ -146,9 +149,8 @@
     node, rep = lax.axis_index("node"), lax.axis_index("rep")
     barrier = lax.optimization_barrier
 
-    hops = [bit | 1 for bit in bits_below(n_node)[:-1]]
-    plain = hops
-    hops, turned = [plain[1], plain[0], plain[2]], [plain[0], plain[2], plain[1]]
+    bits = [bit | 1 for bit in bits_below(n_node)[:-1]]
+    hops, turned = bits[1:2] + bits[:1] + bits[2:], bits[:1] + bits[2:] + bits[1:2]
     rep_bits = bits_below(n_rep)
 
     def trade(x, even, odd):
@@ -165,9 +167,10 @@
     row_ids = tile_rows[0, 0].reshape(-1)
     live_count = tile_count[0, 0]
     parity = node
-    for shift in bits_below(n_node.bit_length()):
-        parity = parity ^ (parity >> shift)
+    for shift in reversed(range((n_node.bit_length() - 2).bit_length())):
+        parity = parity ^ (parity >> (1 << shift))
     place = jnp.stack([node, rep, parity & 1, rep & 1]).astype(jnp.int32)
+    flags = jnp.broadcast_to(place[2:, None], (2, width))
     masks_even, masks_odd = doubling_masks(hops), doubling_masks(turned)
     pairs = [
         [((mate, mate), masks_even[i : i + 2], masks_odd[i : i + 2]) for i in range(0, len(masks_even), 2)]
@@ -183,7 +186,7 @@
     held = [jnp.concatenate([feats[:, half], got[:, half]], axis=0) for half in halves]
     for even, odd in zip(hops[1:-1], turned[1:-1], strict=True):
         gots = [trade(part, (even, 0), (odd, 0)) for part in held]
-        gots[0], place, row_ids, live_count = barrier((gots[0], place, row_ids, live_count))
+        gots[0], place, flags, row_ids, live_count = barrier((gots[0], place, flags, row_ids, live_count))
         gots[-1], far = barrier((gots[-1], far))
         held = [jnp.concatenate([part, got], axis=0) for part, got in zip(held, gots, strict=True)]
     tables = [place, row_ids, live_count, tiles]
@@ -234,24 +237,21 @@
             jax.ShapeDtypeStruct(totals[0].shape, BF16),
             jax.ShapeDtypeStruct(two_blocks, F32),
         ),
-        [SMEM] + [VMEM] * 6, 6 * rows * width * width, 1 << 19,
-    )(place, totals[0], gots[0], feats, far[:rows], w_self, w_neigh)
+        [VMEM] * 7, 6 * rows * width * width, 1 << 19,
+    )(flags, totals[0], gots[0], feats, far[:rows], w_self, w_neigh)
     half_grad = jax.ShapeDtypeStruct((width // 2, width), F32)
-    value, keep_top, keep_low, send_top, send_low, side = call(
+    value, keep_top, keep_low, send_top, send_low = call(
         update_second,
         (
             jax.ShapeDtypeStruct((rows, width), BF16), half_grad, half_grad, half_grad, half_grad,
-            jax.ShapeDtypeStruct((1, width), jnp.int32),
         ),
-        [SMEM] + [VMEM] * 8, 10 * rows * width * width, 1 << 20,
-    )(place, totals[1], gots[1], x, aggregate, pre, out_grad, far[rows:], w_neigh)
+        [VMEM] * 9, 10 * rows * width * width, 1 << 20,
+    )(flags, totals[1], gots[1], x, aggregate, pre, out_grad, far[rows:], w_neigh)
     grads = [keep_top + core_swap(send_top), keep_low + core_swap(send_low)]
     layer_out = call(copied, jax.ShapeDtypeStruct((rows, width), BF16), [VMEM], 0, 4 * rows * width)(value)
 
-    order_even = [plain[0], plain[2], plain[1]]
-    order_odd = [plain[1], plain[0], plain[2]]
     steps = [((0, bit), (0, bit)) for bit in rep_bits[:-1]]
-    steps += [((even, 0), (odd, 0)) for even, odd in zip(order_even, order_odd, strict=True)]
+    steps += [((even, 0), (odd, 0)) for even, odd in zip(turned, hops, strict=True)]
     for even, odd in steps[:-1]:
         parts = [grad.astype(BF16) for grad in grads]
         gots = [trade(part, even, odd) for part in parts]
@@ -264,7 +264,7 @@
     other_got = jnp.concatenate([core_swap(got) for got in gots], axis=0)
     grad = part.astype(F32) + got.astype(F32)
     other_grad = other_part.astype(F32) + other_got.astype(F32)
-    first_core = side == 0
+    first_core = flags[:1] == 0
     grad_self = jnp.where(first_core, grad, other_grad)
     grad_neigh = jnp.where(first_core, other_grad, grad)
     return (layer_out, grad_self, grad_neigh)

time: 45.1 us -> 44.5 us (0.987)
  Pallas kernels: 4.81 us -> 3.72 us
    pallas_call x1, Pallas kernels: 0.76 us -> 0.22 us  [local(): call(update_first, (jax.ShapeDtypeStruct(two_blocks, BF16), jax.ShapeDtyp...]
    pallas_call x1, Pallas kernels: 1 us -> 0.46 us  [local(): call(update_second, (jax.ShapeDtypeStruct((rows, width), BF16), half_grad...]
  transfers between devices with their start and end apart: 21 -> 21, of which waited for: 11 -> 11; matrix products, arithmetic and copies ran while one was open for 3% -> 3% of each run, Pallas kernels for 8% -> 7%
where the time goes in v5:
time: 44.5 us; the launch traced here: 44.3 us
  starting transfers between devices  26.1 us (59%)
  waiting for transfers between devices  10.6 us (24%)
  Pallas kernels  3.72 us (8%)
  local copies, waits for them, and re-layouts  1.84 us (4%)
  other arithmetic  1.23 us (3%)
  between operations  0.86 us (2%)
    ppermute x21, starting transfers between devices, swap(): return lax.ppermute(x, ('node', 'rep'), pairs)  26.1 us
    ppermute x21, waiting for transfers between devices, swap(): return lax.ppermute(x, ('node', 'rep'), pairs)  10.6 us
    pallas_call x3, Pallas kernels, sums(): call(functools.partial(tile_sums, steps, prebuilt, len(columns), seed is...  1.58 us
    unnamed x12, local copies, waits for them, and re-layouts  0.9 us
  transfers between devices with their start and end apart: 21, of which 11 were waited for; matrix products, arithmetic and copies ran while one was open for 3% of the time, Pallas kernels for 7%

profile of v5, /device:TPU:0, one launch (start us, length us, event | category | flops | bytes accessed | tf_op | source)
XLA Modules:
  0.0 44.3 jit_solution(7441624613481032514)
XLA Ops:
  0.6 0.0 copy-start.2
  0.6 0.0 copy-start
  0.7 2.5 %collective-permute-start = (bf16[128,256]{1,0:T(8,128)(2,1)}, bf16[128,256]{1,0:T(8,128)(2,1)S(1)}, u32[]{:S(2)}, u32[]{:S(2)}) collective-permute-start(bf16[128,256]{1,0:T(8,128)(2,1)} %x_ref.1), channel_id=1, source_target_pairs={{0,10},{1,11},{2,16},{3,17},{4,22},{5,23},{6,12},{7,13},{8,26},{9,... | collective-permute-start | bytes 196616 | tf_op jit(solution)/shard_map/ppermute | solution.py:33
  3.2 0.9 %copy-done.4 = bf16[128,256]{1,0:T(8,128)(2,1)S(1)} copy-done((bf16[128,256]{1,0:T(8,128)(2,1)S(1)}, bf16[128,256]{1,0:T(8,128)(2,1)}, u32[]{:S(2)}) %copy-start.4) | copy-done | bytes 65560
  4.1 0.0 copy-done.2
  4.1 1.6 %collective-permute-start.4 = (bf16[256,256]{1,0:T(8,128)(2,1)S(1)}, bf16[256,256]{1,0:T(8,128)(2,1)S(1)}, u32[]{:S(2)}, u32[]{:S(2)}) collective-permute-start(bf16[256,256]{1,0:T(8,128)(2,1)S(1)} %pad_maximum_fusion.3), channel_id=1, source_target_pairs={{0,1},{1,0},{2,3},{3,2},{4,5},{5,4},{6,7},{7,6},{8,9},{9,8},{10,11... | collective-permute-start | bytes 393224 | tf_op jit(solution)/shard_map/ppermute | solution.py:33
  5.6 0.0 collective-permute-done
  5.7 3.4 %collective-permute-start.1 = (bf16[256,128]{1,0:T(8,128)(2,1)S(1)}, bf16[256,128]{1,0:T(8,128)(2,1)S(1)}, u32[]{:S(2)}, u32[]{:S(2)}) collective-permute-start(bf16[256,128]{1,0:T(8,128)(2,1)S(1)} %pad_maximum_fusion.8), channel_id=1, source_target_pairs={{0,18},{1,19},{2,4},{3,5},{4,2},{5,3},{6,20},{7,21},{8,14},{9,15},... | collective-permute-start | bytes 196616 | tf_op jit(solution)/shard_map/ppermute | solution.py:33
  9.1 0.1 collective-permute-start.3
  9.2 0.1 pad_add_fusion.1
  9.2 0.1 pad_add_fusion.place
  9.3 0.8 %copy.11 = s32[1,1,16,2]{3,2,1,0:T(8,128)S(1)} copy(s32[1,1,16,2]{2,3,1,0:T(2,128)} %param.9) | data formatting | bytes 256 | tf_op jit(solution)/shard_map/optimization_barrier | solution.py:165
  10.1 0.1 reshape_squeeze.3.rows
  10.2 0.9 %collective-permute-done.1 = bf16[256,128]{1,0:T(8,128)(2,1)S(1)} collective-permute-done((bf16[256,128]{1,0:T(8,128)(2,1)S(1)}, bf16[256,128]{1,0:T(8,128)(2,1)S(1)}, u32[]{:S(2)}, u32[]{:S(2)}) %collective-permute-start.1) | collective-permute-done | bytes 65568 | tf_op jit(solution)/shard_map/ppermute | solution.py:33
  11.0 0.1 broadcast_in_dim.19.flags
  11.1 2.3 %collective-permute-start.2 = (bf16[512,128]{1,0:T(8,128)(2,1)S(1)}, bf16[512,128]{1,0:T(8,128)(2,1)S(1)}, u32[]{:S(2)}, u32[]{:S(2)}) collective-permute-start(bf16[512,128]{1,0:T(8,128)(2,1)S(1)} %pad_maximum_fusion.2), channel_id=1, source_target_pairs={{0,6},{1,7},{2,8},{3,9},{4,14},{5,15},{6,0},{7,1},{8,2},{9,3},{10,... | collective-permute-start | bytes 393224 | tf_op jit(solution)/shard_map/ppermute | solution.py:33
  13.4 0.3 collective-permute-done.3
  13.7 0.0 collective-permute-done.4
  13.7 0.0 copy-start.5
  13.7 1.9 %collective-permute-start.5 = (bf16[512,128]{1,0:T(8,128)(2,1)S(1)}, bf16[512,128]{1,0:T(8,128)(2,1)S(1)}, u32[]{:S(2)}, u32[]{:S(2)}) collective-permute-start(bf16[512,128]{1,0:T(8,128)(2,1)S(1)} %pad_maximum_fusion.4), channel_id=1, source_target_pairs={{0,6},{1,7},{2,8},{3,9},{4,14},{5,15},{6,0},{7,1},{8,2},{9,3},{10,... | collective-permute-start | bytes 393224 | tf_op jit(solution)/shard_map/ppermute | solution.py:33
  15.6 0.0 copy-done
  15.6 0.0 copy-done.5
  15.6 0.8 %shard_map.95 = (bf16[2,512,256]{2,1,0:T(8,128)(2,1)S(1)}, bf16[2,512,256]{2,1,0:T(8,128)(2,1)S(1)}, bf16[4,512,256]{2,1,0:T(8,128)(2,1)S(1)}) custom-call(s32[4]{0:T(128)S(1)} %pad_add_fusion.place, s32[32]{0:T(128)S(1)} %reshape_squeeze.3.rows, s32[16]{0:T(128)S(1)} %bitcast.9, bf16[16,2,128,128]{3,2,1,0:T(8,128)(2,1)S(1)} %bitcast.8), custom_call_target="tpu_custom_call" | custom-call | bytes 6291456 | tf_op jit(solution)/shard_map/pallas_call | solution.py:196
  16.4 0.0 collective-permute-done.2
  16.5 0.1 collective-permute-start.6
  16.6 0.4 shard_map.96.refs_2_
  17.0 1.3 %collective-permute-done.5 = bf16[512,128]{1,0:T(8,128)(2,1)S(1)} collective-permute-done((bf16[512,128]{1,0:T(8,128)(2,1)S(1)}, bf16[512,128]{1,0:T(8,128)(2,1)S(1)}, u32[]{:S(2)}, u32[]{:S(2)}) %collective-permute-start.5) | collective-permute-done | bytes 131104 | tf_op jit(solution)/shard_map/ppermute | solution.py:33
  18.3 0.1 collective-permute-start.7
  18.4 0.0 collective-permute-done.6.refs_1_
  18.4 0.4 shard_map.97.total
  18.8 1.6 %collective-permute-start.9 = (bf16[256,128]{1,0:T(8,128)(2,1)S(1)}, bf16[256,128]{1,0:T(8,128)(2,1)S(1)}, u32[]{:S(2)}, u32[]{:S(2)}) collective-permute-start(bf16[256,128]{1,0:T(8,128)(2,1)S(1)} %shard_map.97.total), channel_id=1, source_target_pairs={{0,1},{1,0},{2,3},{3,2},{4,5},{5,4},{6,7},{7,6},{8,9},{9,8},{10,11... | collective-permute-start | bytes 196616 | tf_op jit(solution)/shard_map/ppermute | solution.py:33
  20.4 0.0 collective-permute-done.7.refs_4_
  20.4 0.7 %shard_map.98.total = bf16[256,128]{1,0:T(8,128)(2,1)S(1)} custom-call(bf16[2,512,256]{2,1,0:T(8,128)(2,1)S(1)} %get-tuple-element.53.refs_0_, bf16[2,512,256]{2,1,0:T(8,128)(2,1)S(1)} %get-tuple-element.54.refs_1_, bf16[4,512,256]{2,1,0:T(8,128)(2,1)S(1)} %get-tuple-element.55.refs_0_.refs_2_, bf16[1024,128]{1,0:T(8,128)(2,1)S(1)} %pad_maximum_fusion.1.refs_3_, ...), custom_call_target="tpu_custom_call" | custom-call | flops 268435456 | bytes 2097152 | tf_op jit(solution)/shard_map/pallas_call | solution.py:208
  21.1 0.0 copy-start.1
  21.1 0.0 copy-start.3
  21.1 1.1 %collective-permute-start.8 = (bf16[256,128]{1,0:T(8,128)(2,1)S(1)}, bf16[256,128]{1,0:T(8,128)(2,1)S(1)}, u32[]{:S(2)}, u32[]{:S(2)}) collective-permute-start(bf16[256,128]{1,0:T(8,128)(2,1)S(1)} %shard_map.98.total), channel_id=1, source_target_pairs={{0,1},{1,0},{2,3},{3,2},{4,5},{5,4},{6,7},{7,6},{8,9},{9,8},{10,11... | collective-permute-start | bytes 196616 | tf_op jit(solution)/shard_map/ppermute | solution.py:33
  22.2 1.2 %collective-permute-done.9.got = bf16[256,128]{1,0:T(8,128)(2,1)S(1)} collective-permute-done((bf16[256,128]{1,0:T(8,128)(2,1)S(1)}, bf16[256,128]{1,0:T(8,128)(2,1)S(1)}, u32[]{:S(2)}, u32[]{:S(2)}) %collective-permute-start.9) | collective-permute-done | bytes 65568 | tf_op jit(solution)/shard_map/ppermute | solution.py:33
  23.4 0.2 shard_map.99
  23.6 1.8 %collective-permute-done.8.got = bf16[256,128]{1,0:T(8,128)(2,1)S(1)} collective-permute-done((bf16[256,128]{1,0:T(8,128)(2,1)S(1)}, bf16[256,128]{1,0:T(8,128)(2,1)S(1)}, u32[]{:S(2)}, u32[]{:S(2)}) %collective-permute-start.8) | collective-permute-done | bytes 65568 | tf_op jit(solution)/shard_map/ppermute | solution.py:33
  25.4 0.5 %shard_map.100 = (bf16[128,256]{1,0:T(8,128)(2,1)S(1)}, f32[128,256]{1,0:T(8,128)S(1)}, f32[128,256]{1,0:T(8,128)S(1)}, f32[128,256]{1,0:T(8,128)S(1)}, f32[128,256]{1,0:T(8,128)S(1)}) custom-call(s32[2,256]{1,0:T(2,128)S(1)} %broadcast_in_dim.19.flags, bf16[256,128]{1,0:T(8,128)(2,1)S(1)} %shard_map.98.total, ...), custom_call_target="tpu_custom_call" | custom-call | flops 83886080 | bytes 1048576 | tf_op jit(solution)/shard_map/pallas_call | solution.py:243
  25.9 0.1 collective-permute-start.10
  26.0 0.6 %shard_map.101 = bf16[128,256]{1,0:T(8,128)(2,1)} custom-call(bf16[128,256]{1,0:T(8,128)(2,1)S(1)} %get-tuple-element.68.x_ref), custom_call_target="tpu_custom_call" | custom-call | bytes 131072 | tf_op jit(solution)/shard_map/pallas_call | solution.py:251
  26.6 0.5 %collective-permute-start.13 = (f32[128,256]{1,0:T(8,128)S(1)}, f32[128,256]{1,0:T(8,128)S(1)}, u32[]{:S(2)}, u32[]{:S(2)}) collective-permute-start(f32[128,256]{1,0:T(8,128)S(1)} %get-tuple-element.74), channel_id=1, source_target_pairs={{0,2},{1,3},{2,0},{3,1},{4,6},{5,7},{6,4},{7,5},{8,10},{9,11},{10,... | collective-permute-start | bytes 393224 | tf_op jit(solution)/shard_map/ppermute | solution.py:33
  27.1 0.2 collective-permute-done.10
  27.3 1.8 %collective-permute-start.11 = (bf16[128,256]{1,0:T(8,128)(2,1)S(1)}, bf16[128,256]{1,0:T(8,128)(2,1)S(1)}, u32[]{:S(2)}, u32[]{:S(2)}) collective-permute-start(bf16[128,256]{1,0:T(8,128)(2,1)S(1)} %add_convert_fusion.5), channel_id=1, source_target_pairs={{0,18},{1,19},{2,8},{3,9},{4,14},{5,15},{6,20},{7,21},{8,2},{9,3},... | collective-permute-start | bytes 196616 | tf_op jit(solution)/shard_map/ppermute | solution.py:33
  29.2 0.0 collective-permute-done.13
  29.2 1.0 %collective-permute-start.14 = (bf16[128,256]{1,0:T(8,128)(2,1)S(1)}, bf16[128,256]{1,0:T(8,128)(2,1)S(1)}, u32[]{:S(2)}, u32[]{:S(2)}) collective-permute-start(bf16[128,256]{1,0:T(8,128)(2,1)S(1)} %add_convert_fusion.2), channel_id=1, source_target_pairs={{0,18},{1,19},{2,8},{3,9},{4,14},{5,15},{6,20},{7,21},{8,2},{9,3},... | collective-permute-start | bytes 196616 | tf_op jit(solution)/shard_map/ppermute | solution.py:33
  30.2 1.9 %collective-permute-done.11 = bf16[128,256]{1,0:T(8,128)(2,1)S(1)} collective-permute-done((bf16[128,256]{1,0:T(8,128)(2,1)S(1)}, bf16[128,256]{1,0:T(8,128)(2,1)S(1)}, u32[]{:S(2)}, u32[]{:S(2)}) %collective-permute-start.11) | collective-permute-done | bytes 65568 | tf_op jit(solution)/shard_map/ppermute | solution.py:33
  32.1 2.1 %collective-permute-start.12 = (bf16[128,256]{1,0:T(8,128)(2,1)S(1)}, bf16[128,256]{1,0:T(8,128)(2,1)S(1)}, u32[]{:S(2)}, u32[]{:S(2)}) collective-permute-start(bf16[128,256]{1,0:T(8,128)(2,1)S(1)} %add_convert_fusion.4), channel_id=1, source_target_pairs={{0,6},{1,7},{2,16},{3,17},{4,22},{5,23},{6,0},{7,1},{8,26},{9,27},... | collective-permute-start | bytes 196616 | tf_op jit(solution)/shard_map/ppermute | solution.py:33
  34.2 0.0 collective-permute-done.14
  34.2 1.2 %collective-permute-start.15 = (bf16[128,256]{1,0:T(8,128)(2,1)S(1)}, bf16[128,256]{1,0:T(8,128)(2,1)S(1)}, u32[]{:S(2)}, u32[]{:S(2)}) collective-permute-start(bf16[128,256]{1,0:T(8,128)(2,1)S(1)} %add_convert_fusion.1), channel_id=1, source_target_pairs={{0,6},{1,7},{2,16},{3,17},{4,22},{5,23},{6,0},{7,1},{8,26},{9,27},... | collective-permute-start | bytes 196616 | tf_op jit(solution)/shard_map/ppermute | solution.py:33
  35.4 0.7 %collective-permute-done.12 = bf16[128,256]{1,0:T(8,128)(2,1)S(1)} collective-permute-done((bf16[128,256]{1,0:T(8,128)(2,1)S(1)}, bf16[128,256]{1,0:T(8,128)(2,1)S(1)}, u32[]{:S(2)}, u32[]{:S(2)}) %collective-permute-start.12) | collective-permute-done | bytes 65568 | tf_op jit(solution)/shard_map/ppermute | solution.py:33
  36.2 1.3 %collective-permute-start.16 = (bf16[128,256]{1,0:T(8,128)(2,1)S(1)}, bf16[128,256]{1,0:T(8,128)(2,1)S(1)}, u32[]{:S(2)}, u32[]{:S(2)}) collective-permute-start(bf16[128,256]{1,0:T(8,128)(2,1)S(1)} %add_convert_fusion.3), channel_id=1, source_target_pairs={{0,10},{1,11},{2,4},{3,5},{4,2},{5,3},{6,12},{7,13},{8,14},{9,15},... | collective-permute-start | bytes 196616 | tf_op jit(solution)/shard_map/ppermute | solution.py:33
  37.5 0.5 %collective-permute-done.15 = bf16[128,256]{1,0:T(8,128)(2,1)S(1)} collective-permute-done((bf16[128,256]{1,0:T(8,128)(2,1)S(1)}, bf16[128,256]{1,0:T(8,128)(2,1)S(1)}, u32[]{:S(2)}, u32[]{:S(2)}) %collective-permute-start.15) | collective-permute-done | bytes 65568 | tf_op jit(solution)/shard_map/ppermute | solution.py:33
  38.0 1.6 %collective-permute-start.17 = (bf16[128,256]{1,0:T(8,128)(2,1)S(1)}, bf16[128,256]{1,0:T(8,128)(2,1)S(1)}, u32[]{:S(2)}, u32[]{:S(2)}) collective-permute-start(bf16[128,256]{1,0:T(8,128)(2,1)S(1)} %add_convert_fusion), channel_id=1, source_target_pairs={{0,10},{1,11},{2,4},{3,5},{4,2},{5,3},{6,12},{7,13},{8,14},{9,15},... | collective-permute-start | bytes 196616 | tf_op jit(solution)/shard_map/ppermute | solution.py:33
  39.7 0.3 collective-permute-start.18
  40.0 0.0 collective-permute-done.16
  40.0 0.8 %collective-permute-start.19 = (bf16[128,256]{1,0:T(8,128)(2,1)S(1)}, bf16[128,256]{1,0:T(8,128)(2,1)S(1)}, u32[]{:S(2)}, u32[]{:S(2)}) collective-permute-start(bf16[128,256]{1,0:T(8,128)(2,1)S(1)} %collective-permute-done.16), channel_id=1, source_target_pairs={{0,2},{1,3},{2,0},{3,1},{4,6},{5,7},{6,4},{7,5},{8,10},{9,11},{10,... | collective-permute-start | bytes 196616 | tf_op jit(solution)/shard_map/ppermute | solution.py:33
  40.9 0.9 %collective-permute-done.17 = bf16[128,256]{1,0:T(8,128)(2,1)S(1)} collective-permute-done((bf16[128,256]{1,0:T(8,128)(2,1)S(1)}, bf16[128,256]{1,0:T(8,128)(2,1)S(1)}, u32[]{:S(2)}, u32[]{:S(2)}) %collective-permute-start.17) | collective-permute-done | bytes 65568 | tf_op jit(solution)/shard_map/ppermute | solution.py:33
  41.8 0.8 %collective-permute-start.20 = (bf16[128,256]{1,0:T(8,128)(2,1)S(1)}, bf16[128,256]{1,0:T(8,128)(2,1)S(1)}, u32[]{:S(2)}, u32[]{:S(2)}) collective-permute-start(bf16[128,256]{1,0:T(8,128)(2,1)S(1)} %collective-permute-done.17), channel_id=1, source_target_pairs={{0,2},{1,3},{2,0},{3,1},{4,6},{5,7},{6,4},{7,5},{8,10},{9,11},{10,... | collective-permute-start | bytes 196616 | tf_op jit(solution)/shard_map/ppermute | solution.py:33
  42.6 0.0 collective-permute-done.18
  42.6 0.0 collective-permute-done.19
  42.6 0.9 %collective-permute-done.20 = bf16[128,256]{1,0:T(8,128)(2,1)S(1)} collective-permute-done((bf16[128,256]{1,0:T(8,128)(2,1)S(1)}, bf16[128,256]{1,0:T(8,128)(2,1)S(1)}, u32[]{:S(2)}, u32[]{:S(2)}) %collective-permute-start.20) | collective-permute-done | bytes 65568 | tf_op jit(solution)/shard_map/ppermute | solution.py:33
  43.5 0.9 %fusion = (f32[256,256]{1,0:T(8,128)}, f32[256,256]{1,0:T(8,128)}) fusion(bf16[256,256]{1,0:T(8,128)(2,1)S(1)} %collective-permute-done.18, pred[256]{0:T(512)(128)(4,1)S(1)} %compare_reduce_fusion, bf16[128,256]{1,0:T(8,128)(2,1)S(1)} %collective-permute-done.20, bf16[128,256]{1,0:T(8,128)(2,1)S(1)} %collective-permute-done.19, ...), kind=kLoop, calls=%fused_computation.4 | loop fusion | flops 1114112 | bytes 1048832 | tf_op jit(solution)/shard_map/jit(_where)/select_n | solution.py:269
  (21 shorter events, 0.3 us)
Async XLA Ops:
  0.6 3.4 %copy-start.2 = (bf16[128,256]{1,0:T(8,128)(2,1)S(1)}, bf16[128,256]{1,0:T(8,128)(2,1)}, u32[]{:S(2)}) copy-start(bf16[128,256]{1,0:T(8,128)(2,1)} %out_grad.1) | copy-start | bytes 196612
  0.6 15.0 %copy-start = (bf16[1,1,16,2,128,128]{5,4,3,2,1,0:T(8,128)(2,1)S(1)}, bf16[1,1,16,2,128,128]{5,4,3,2,1,0:T(8,128)(2,1)}, u32[]{:S(2)}) copy-start(bf16[1,1,16,2,128,128]{5,4,3,2,1,0:T(8,128)(2,1)} %param.8) | copy-start | bytes 3145732
  0.7 5.0 %collective-permute-start = (bf16[128,256]{1,0:T(8,128)(2,1)}, bf16[128,256]{1,0:T(8,128)(2,1)S(1)}, u32[]{:S(2)}, u32[]{:S(2)}) collective-permute-start(bf16[128,256]{1,0:T(8,128)(2,1)} %x_ref.1), channel_id=1, source_target_pairs={{0,10},{1,11},{2,16},{3,17},{4,22},{5,23},{6,12},{7,13},{8,26},{9,... | collective-permute-start | bytes 196616 | tf_op jit(solution)/shard_map/ppermute | solution.py:33
  3.2 0.9 %copy-start.4 = (bf16[128,256]{1,0:T(8,128)(2,1)S(1)}, bf16[128,256]{1,0:T(8,128)(2,1)}, u32[]{:S(2)}) copy-start(bf16[128,256]{1,0:T(8,128)(2,1)} %x_ref.1) | copy-start | bytes 196612
  4.1 9.6 %collective-permute-start.4 = (bf16[256,256]{1,0:T(8,128)(2,1)S(1)}, bf16[256,256]{1,0:T(8,128)(2,1)S(1)}, u32[]{:S(2)}, u32[]{:S(2)}) collective-permute-start(bf16[256,256]{1,0:T(8,128)(2,1)S(1)} %pad_maximum_fusion.3), channel_id=1, source_target_pairs={{0,1},{1,0},{2,3},{3,2},{4,5},{5,4},{6,7},{7,6},{8,9},{9,8},{10,11... | collective-permute-start | bytes 393224 | tf_op jit(solution)/shard_map/ppermute | solution.py:33
  5.7 5.3 %collective-permute-start.1 = (bf16[256,128]{1,0:T(8,128)(2,1)S(1)}, bf16[256,128]{1,0:T(8,128)(2,1)S(1)}, u32[]{:S(2)}, u32[]{:S(2)}) collective-permute-start(bf16[256,128]{1,0:T(8,128)(2,1)S(1)} %pad_maximum_fusion.8), channel_id=1, source_target_pairs={{0,18},{1,19},{2,4},{3,5},{4,2},{5,3},{6,20},{7,21},{8,14},{9,15},... | collective-permute-start | bytes 196616 | tf_op jit(solution)/shard_map/ppermute | solution.py:33
  9.1 4.6 %collective-permute-start.3 = (bf16[256,128]{1,0:T(8,128)(2,1)S(1)}, bf16[256,128]{1,0:T(8,128)(2,1)S(1)}, u32[]{:S(2)}, u32[]{:S(2)}) collective-permute-start(bf16[256,128]{1,0:T(8,128)(2,1)S(1)} %pad_maximum_fusion.9), channel_id=1, source_target_pairs={{0,18},{1,19},{2,4},{3,5},{4,2},{5,3},{6,20},{7,21},{8,14},{9,15},... | collective-permute-start | bytes 196616 | tf_op jit(solution)/shard_map/ppermute | solution.py:33
  11.1 5.3 %collective-permute-start.2 = (bf16[512,128]{1,0:T(8,128)(2,1)S(1)}, bf16[512,128]{1,0:T(8,128)(2,1)S(1)}, u32[]{:S(2)}, u32[]{:S(2)}) collective-permute-start(bf16[512,128]{1,0:T(8,128)(2,1)S(1)} %pad_maximum_fusion.2), channel_id=1, source_target_pairs={{0,6},{1,7},{2,8},{3,9},{4,14},{5,15},{6,0},{7,1},{8,2},{9,3},{10,... | collective-permute-start | bytes 393224 | tf_op jit(solution)/shard_map/ppermute | solution.py:33
  13.7 1.9 %copy-start.5 = (s32[1,1,16]{2,1,0:T(1,128)S(1)}, s32[1,1,16]{2,1,0:T(1,128)}, u32[]{:S(2)}) copy-start(s32[1,1,16]{2,1,0:T(1,128)} %param.10) | copy-start | bytes 196
  13.7 4.6 %collective-permute-start.5 = (bf16[512,128]{1,0:T(8,128)(2,1)S(1)}, bf16[512,128]{1,0:T(8,128)(2,1)S(1)}, u32[]{:S(2)}, u32[]{:S(2)}) collective-permute-start(bf16[512,128]{1,0:T(8,128)(2,1)S(1)} %pad_maximum_fusion.4), channel_id=1, source_target_pairs={{0,6},{1,7},{2,8},{3,9},{4,14},{5,15},{6,0},{7,1},{8,2},{9,3},{10,... | collective-permute-start | bytes 393224 | tf_op jit(solution)/shard_map/ppermute | solution.py:33
  16.5 1.9 %collective-permute-start.6 = (bf16[1024,128]{1,0:T(8,128)(2,1)S(1)}, bf16[1024,128]{1,0:T(8,128)(2,1)S(1)}, u32[]{:S(2)}, u32[]{:S(2)}) collective-permute-start(bf16[1024,128]{1,0:T(8,128)(2,1)S(1)} %pad_maximum_fusion.refs_2_), channel_id=1, source_target_pairs={{0,2},{1,3},{2,0},{3,1},{4,6},{5,7},{6,4},{7,5},{8,10},{9,11},{10,... | collective-permute-start | bytes 786440 | tf_op jit(solution)/shard_map/ppermute | solution.py:33
  18.3 2.1 %collective-permute-start.7 = (bf16[1024,128]{1,0:T(8,128)(2,1)S(1)}, bf16[1024,128]{1,0:T(8,128)(2,1)S(1)}, u32[]{:S(2)}, u32[]{:S(2)}) collective-permute-start(bf16[1024,128]{1,0:T(8,128)(2,1)S(1)} %pad_maximum_fusion.1.refs_3_), channel_id=1, source_target_pairs={{0,2},{1,3},{2,0},{3,1},{4,6},{5,7},{6,4},{7,5},{8,10},{9,11},{10,... | collective-permute-start | bytes 786440 | tf_op jit(solution)/shard_map/ppermute | solution.py:33
  18.8 4.6 %collective-permute-start.9 = (bf16[256,128]{1,0:T(8,128)(2,1)S(1)}, bf16[256,128]{1,0:T(8,128)(2,1)S(1)}, u32[]{:S(2)}, u32[]{:S(2)}) collective-permute-start(bf16[256,128]{1,0:T(8,128)(2,1)S(1)} %shard_map.97.total), channel_id=1, source_target_pairs={{0,1},{1,0},{2,3},{3,2},{4,5},{5,4},{6,7},{7,6},{8,9},{9,8},{10,11... | collective-permute-start | bytes 196616 | tf_op jit(solution)/shard_map/ppermute | solution.py:33
  21.1 2.3 %copy-start.1 = (bf16[256,256]{1,0:T(8,128)(2,1)S(1)}, bf16[256,256]{1,0:T(8,128)(2,1)}, u32[]{:S(2)}) copy-start(bf16[256,256]{1,0:T(8,128)(2,1)} %w_neigh.3) | copy-start | bytes 393220
  21.1 2.3 %copy-start.3 = (bf16[256,256]{1,0:T(8,128)(2,1)S(1)}, bf16[256,256]{1,0:T(8,128)(2,1)}, u32[]{:S(2)}) copy-start(bf16[256,256]{1,0:T(8,128)(2,1)} %w_self.1) | copy-start | bytes 393220
  21.1 4.3 %collective-permute-start.8 = (bf16[256,128]{1,0:T(8,128)(2,1)S(1)}, bf16[256,128]{1,0:T(8,128)(2,1)S(1)}, u32[]{:S(2)}, u32[]{:S(2)}) collective-permute-start(bf16[256,128]{1,0:T(8,128)(2,1)S(1)} %shard_map.98.total), channel_id=1, source_target_pairs={{0,1},{1,0},{2,3},{3,2},{4,5},{5,4},{6,7},{7,6},{8,9},{9,8},{10,11... | collective-permute-start | bytes 196616 | tf_op jit(solution)/shard_map/ppermute | solution.py:33
  25.9 1.4 %collective-permute-start.10 = (f32[128,256]{1,0:T(8,128)S(1)}, f32[128,256]{1,0:T(8,128)S(1)}, u32[]{:S(2)}, u32[]{:S(2)}) collective-permute-start(f32[128,256]{1,0:T(8,128)S(1)} %get-tuple-element.67), channel_id=1, source_target_pairs={{0,2},{1,3},{2,0},{3,1},{4,6},{5,7},{6,4},{7,5},{8,10},{9,11},{10,... | collective-permute-start | bytes 393224 | tf_op jit(solution)/shard_map/ppermute | solution.py:33
  26.6 2.6 %collective-permute-start.13 = (f32[128,256]{1,0:T(8,128)S(1)}, f32[128,256]{1,0:T(8,128)S(1)}, u32[]{:S(2)}, u32[]{:S(2)}) collective-permute-start(f32[128,256]{1,0:T(8,128)S(1)} %get-tuple-element.74), channel_id=1, source_target_pairs={{0,2},{1,3},{2,0},{3,1},{4,6},{5,7},{6,4},{7,5},{8,10},{9,11},{10,... | collective-permute-start | bytes 393224 | tf_op jit(solution)/shard_map/ppermute | solution.py:33
  27.3 4.8 %collective-permute-start.11 = (bf16[128,256]{1,0:T(8,128)(2,1)S(1)}, bf16[128,256]{1,0:T(8,128)(2,1)S(1)}, u32[]{:S(2)}, u32[]{:S(2)}) collective-permute-start(bf16[128,256]{1,0:T(8,128)(2,1)S(1)} %add_convert_fusion.5), channel_id=1, source_target_pairs={{0,18},{1,19},{2,8},{3,9},{4,14},{5,15},{6,20},{7,21},{8,2},{9,3},... | collective-permute-start | bytes 196616 | tf_op jit(solution)/shard_map/ppermute | solution.py:33
  29.2 5.0 %collective-permute-start.14 = (bf16[128,256]{1,0:T(8,128)(2,1)S(1)}, bf16[128,256]{1,0:T(8,128)(2,1)S(1)}, u32[]{:S(2)}, u32[]{:S(2)}) collective-permute-start(bf16[128,256]{1,0:T(8,128)(2,1)S(1)} %add_convert_fusion.2), channel_id=1, source_target_pairs={{0,18},{1,19},{2,8},{3,9},{4,14},{5,15},{6,20},{7,21},{8,2},{9,3},... | collective-permute-start | bytes 196616 | tf_op jit(solution)/shard_map/ppermute | solution.py:33
  32.1 4.0 %collective-permute-start.12 = (bf16[128,256]{1,0:T(8,128)(2,1)S(1)}, bf16[128,256]{1,0:T(8,128)(2,1)S(1)}, u32[]{:S(2)}, u32[]{:S(2)}) collective-permute-start(bf16[128,256]{1,0:T(8,128)(2,1)S(1)} %add_convert_fusion.4), channel_id=1, source_target_pairs={{0,6},{1,7},{2,16},{3,17},{4,22},{5,23},{6,0},{7,1},{8,26},{9,27},... | collective-permute-start | bytes 196616 | tf_op jit(solution)/shard_map/ppermute | solution.py:33
  34.2 3.8 %collective-permute-start.15 = (bf16[128,256]{1,0:T(8,128)(2,1)S(1)}, bf16[128,256]{1,0:T(8,128)(2,1)S(1)}, u32[]{:S(2)}, u32[]{:S(2)}) collective-permute-start(bf16[128,256]{1,0:T(8,128)(2,1)S(1)} %add_convert_fusion.1), channel_id=1, source_target_pairs={{0,6},{1,7},{2,16},{3,17},{4,22},{5,23},{6,0},{7,1},{8,26},{9,27},... | collective-permute-start | bytes 196616 | tf_op jit(solution)/shard_map/ppermute | solution.py:33
  36.2 3.8 %collective-permute-start.16 = (bf16[128,256]{1,0:T(8,128)(2,1)S(1)}, bf16[128,256]{1,0:T(8,128)(2,1)S(1)}, u32[]{:S(2)}, u32[]{:S(2)}) collective-permute-start(bf16[128,256]{1,0:T(8,128)(2,1)S(1)} %add_convert_fusion.3), channel_id=1, source_target_pairs={{0,10},{1,11},{2,4},{3,5},{4,2},{5,3},{6,12},{7,13},{8,14},{9,15},... | collective-permute-start | bytes 196616 | tf_op jit(solution)/shard_map/ppermute | solution.py:33
  38.0 3.8 %collective-permute-start.17 = (bf16[128,256]{1,0:T(8,128)(2,1)S(1)}, bf16[128,256]{1,0:T(8,128)(2,1)S(1)}, u32[]{:S(2)}, u32[]{:S(2)}) collective-permute-start(bf16[128,256]{1,0:T(8,128)(2,1)S(1)} %add_convert_fusion), channel_id=1, source_target_pairs={{0,10},{1,11},{2,4},{3,5},{4,2},{5,3},{6,12},{7,13},{8,14},{9,15},... | collective-permute-start | bytes 196616 | tf_op jit(solution)/shard_map/ppermute | solution.py:33
  39.7 2.9 %collective-permute-start.18 = (bf16[256,256]{1,0:T(8,128)(2,1)S(1)}, bf16[256,256]{1,0:T(8,128)(2,1)S(1)}, u32[]{:S(2)}, u32[]{:S(2)}) collective-permute-start(bf16[256,256]{1,0:T(8,128)(2,1)S(1)} %pad_maximum_fusion.5), channel_id=1, source_target_pairs={{0,2},{1,3},{2,0},{3,1},{4,6},{5,7},{6,4},{7,5},{8,10},{9,11},{10,... | collective-permute-start | bytes 393224 | tf_op jit(solution)/shard_map/ppermute | solution.py:33
  40.0 2.6 %collective-permute-start.19 = (bf16[128,256]{1,0:T(8,128)(2,1)S(1)}, bf16[128,256]{1,0:T(8,128)(2,1)S(1)}, u32[]{:S(2)}, u32[]{:S(2)}) collective-permute-start(bf16[128,256]{1,0:T(8,128)(2,1)S(1)} %collective-permute-done.16), channel_id=1, source_target_pairs={{0,2},{1,3},{2,0},{3,1},{4,6},{5,7},{6,4},{7,5},{8,10},{9,11},{10,... | collective-permute-start | bytes 196616 | tf_op jit(solution)/shard_map/ppermute | solution.py:33
  41.8 1.7 %collective-permute-start.20 = (bf16[128,256]{1,0:T(8,128)(2,1)S(1)}, bf16[128,256]{1,0:T(8,128)(2,1)S(1)}, u32[]{:S(2)}, u32[]{:S(2)}) collective-permute-start(bf16[128,256]{1,0:T(8,128)(2,1)S(1)} %collective-permute-done.17), channel_id=1, source_target_pairs={{0,2},{1,3},{2,0},{3,1},{4,6},{5,7},{6,4},{7,5},{8,10},{9,11},{10,... | collective-permute-start | bytes 196616 | tf_op jit(solution)/shard_map/ppermute | solution.py:33

commit v6 on v5

--- a/solution.py
+++ b/solution.py
@@ -150,7 +150,7 @@
     barrier = lax.optimization_barrier
 
     bits = [bit | 1 for bit in bits_below(n_node)[:-1]]
-    hops, turned = bits[1:2] + bits[:1] + bits[2:], bits[:1] + bits[2:] + bits[1:2]
+    hops, turned = bits[:1] + bits[2:] + bits[1:2], bits[1:2] + bits[:1] + bits[2:]
     rep_bits = bits_below(n_rep)
 
     def trade(x, even, odd):
@@ -162,9 +162,9 @@
     got = trade(node_feats, (hops[0], 0), (turned[0], 0))
     feats = call(copied, jax.ShapeDtypeStruct(node_feats.shape, BF16), [VMEM], 0, node_feats.size * 4)(node_feats)
     far = trade(jnp.concatenate([feats, out_grad], axis=0), (0, 1), (0, 1))
-    feats, got, tables = barrier((feats, got, (node, rep, tile_rows, tile_count)))
-    node, rep, tile_rows, tile_count = tables
     row_ids = tile_rows[0, 0].reshape(-1)
+    feats, got, tables = barrier((feats, got, (node, rep, row_ids, tile_count)))
+    node, rep, row_ids, tile_count = tables
     live_count = tile_count[0, 0]
     parity = node
     for shift in reversed(range((n_node.bit_length() - 2).bit_length())):

time: 44.5 us -> 44.3 us (level)
  starting transfers between devices: 26.1 us -> 23.3 us
  waiting for transfers between devices: 10.6 us -> 13.2 us
    ppermute x21, starting transfers between devices: 26.1 us -> 23.3 us  [swap(): return lax.ppermute(x, ('node', 'rep'), pairs)]
    ppermute x21, waiting for transfers between devices: 10.6 us -> 13.2 us  [swap(): return lax.ppermute(x, ('node', 'rep'), pairs)]
    optimization_barrier x1 -> x0, local copies, waits for them, and re-layouts: 0.76 us -> none  [local(): barrier((feats, got, (node, rep, tile_rows, tile_count)))]
    unnamed x12 -> x13, local copies, waits for them, and re-layouts: 0.9 us -> 1.65 us
where the time goes in v6:
time: 44.3 us; the launch traced here: 44.1 us
  starting transfers between devices  23.3 us (53%)
  waiting for transfers between devices  13.2 us (30%)
  Pallas kernels  3.72 us (8%)
  local copies, waits for them, and re-layouts  1.84 us (4%)
  other arithmetic  1.23 us (3%)
  between operations  0.86 us (2%)
    ppermute x21, starting transfers between devices, swap(): return lax.ppermute(x, ('node', 'rep'), pairs)  23.3 us
    ppermute x21, waiting for transfers between devices, swap(): return lax.ppermute(x, ('node', 'rep'), pairs)  13.2 us
    unnamed x13, local copies, waits for them, and re-layouts  1.65 us
    pallas_call x3, Pallas kernels, sums(): call(functools.partial(tile_sums, steps, prebuilt, len(columns), seed is...  1.57 us
  transfers between devices with their start and end apart: 21, of which 11 were waited for; matrix products, arithmetic and copies ran while one was open for 3% of the time, Pallas kernels for 7%

profile of v6, /device:TPU:0, one launch (start us, length us, event | category | flops | bytes accessed | tf_op | source)
XLA Modules:
  0.0 44.1 jit_solution(12050596733389204043)
XLA Ops:
  0.6 0.0 copy-start.2
  0.6 0.0 copy-start
  0.7 3.5 %collective-permute-start = (bf16[128,256]{1,0:T(8,128)(2,1)}, bf16[128,256]{1,0:T(8,128)(2,1)S(1)}, u32[]{:S(2)}, u32[]{:S(2)}) collective-permute-start(bf16[128,256]{1,0:T(8,128)(2,1)} %x_ref.1), channel_id=1, source_target_pairs={{0,18},{1,19},{2,8},{3,9},{4,14},{5,15},{6,20},{7,21},{8,2},{9,3},... | collective-permute-start | bytes 196616 | tf_op jit(solution)/shard_map/ppermute | solution.py:33
  4.2 0.9 %copy-done.4 = bf16[128,256]{1,0:T(8,128)(2,1)S(1)} copy-done((bf16[128,256]{1,0:T(8,128)(2,1)S(1)}, bf16[128,256]{1,0:T(8,128)(2,1)}, u32[]{:S(2)}) %copy-start.4) | copy-done | bytes 65560
  5.1 0.0 copy-done.2
  5.1 1.6 %collective-permute-start.4 = (bf16[256,256]{1,0:T(8,128)(2,1)S(1)}, bf16[256,256]{1,0:T(8,128)(2,1)S(1)}, u32[]{:S(2)}, u32[]{:S(2)}) collective-permute-start(bf16[256,256]{1,0:T(8,128)(2,1)S(1)} %pad_maximum_fusion.3), channel_id=1, source_target_pairs={{0,1},{1,0},{2,3},{3,2},{4,5},{5,4},{6,7},{7,6},{8,9},{9,8},{10,11... | collective-permute-start | bytes 393224 | tf_op jit(solution)/shard_map/ppermute | solution.py:33
  6.7 0.8 %copy.11 = s32[1,1,16,2]{3,2,1,0:T(8,128)S(1)} copy(s32[1,1,16,2]{2,3,1,0:T(2,128)} %param.9) | data formatting | bytes 256 | tf_op args[2]
  7.4 0.1 reshape_squeeze.3.rows
  7.5 0.0 collective-permute-done
  7.6 1.6 %collective-permute-start.1 = (bf16[256,128]{1,0:T(8,128)(2,1)S(1)}, bf16[256,128]{1,0:T(8,128)(2,1)S(1)}, u32[]{:S(2)}, u32[]{:S(2)}) collective-permute-start(bf16[256,128]{1,0:T(8,128)(2,1)S(1)} %pad_maximum_fusion.8), channel_id=1, source_target_pairs={{0,6},{1,7},{2,16},{3,17},{4,22},{5,23},{6,0},{7,1},{8,26},{9,27},... | collective-permute-start | bytes 196616 | tf_op jit(solution)/shard_map/ppermute | solution.py:33
  9.2 0.2 collective-permute-start.3
  9.4 0.1 pad_add_fusion.1
  9.5 0.1 pad_add_fusion.place
  9.5 1.8 %collective-permute-done.1 = bf16[256,128]{1,0:T(8,128)(2,1)S(1)} collective-permute-done((bf16[256,128]{1,0:T(8,128)(2,1)S(1)}, bf16[256,128]{1,0:T(8,128)(2,1)S(1)}, u32[]{:S(2)}, u32[]{:S(2)}) %collective-permute-start.1) | collective-permute-done | bytes 65568 | tf_op jit(solution)/shard_map/ppermute | solution.py:33
  11.3 0.1 broadcast_in_dim.19.flags
  11.4 1.6 %collective-permute-start.2 = (bf16[512,128]{1,0:T(8,128)(2,1)S(1)}, bf16[512,128]{1,0:T(8,128)(2,1)S(1)}, u32[]{:S(2)}, u32[]{:S(2)}) collective-permute-start(bf16[512,128]{1,0:T(8,128)(2,1)S(1)} %pad_maximum_fusion.2), channel_id=1, source_target_pairs={{0,10},{1,11},{2,4},{3,5},{4,2},{5,3},{6,12},{7,13},{8,14},{9,15},... | collective-permute-start | bytes 393224 | tf_op jit(solution)/shard_map/ppermute | solution.py:33
  13.0 0.0 collective-permute-done.3
  13.0 0.0 collective-permute-done.4
  13.1 0.0 copy-start.5
  13.1 1.2 %collective-permute-start.5 = (bf16[512,128]{1,0:T(8,128)(2,1)S(1)}, bf16[512,128]{1,0:T(8,128)(2,1)S(1)}, u32[]{:S(2)}, u32[]{:S(2)}) collective-permute-start(bf16[512,128]{1,0:T(8,128)(2,1)S(1)} %pad_maximum_fusion.4), channel_id=1, source_target_pairs={{0,10},{1,11},{2,4},{3,5},{4,2},{5,3},{6,12},{7,13},{8,14},{9,15},... | collective-permute-start | bytes 393224 | tf_op jit(solution)/shard_map/ppermute | solution.py:33
  14.2 0.0 copy-done
  14.2 0.0 copy-done.5
  14.2 0.8 %shard_map.95 = (bf16[2,512,256]{2,1,0:T(8,128)(2,1)S(1)}, bf16[2,512,256]{2,1,0:T(8,128)(2,1)S(1)}, bf16[4,512,256]{2,1,0:T(8,128)(2,1)S(1)}) custom-call(s32[4]{0:T(128)S(1)} %pad_add_fusion.place, s32[32]{0:T(128)S(1)} %reshape_squeeze.3.rows, s32[16]{0:T(128)S(1)} %bitcast.9, bf16[16,2,128,128]{3,2,1,0:T(8,128)(2,1)S(1)} %bitcast.8), custom_call_target="tpu_custom_call" | custom-call | bytes 6291456 | tf_op jit(solution)/shard_map/pallas_call | solution.py:196
  15.1 0.8 %collective-permute-done.2 = bf16[512,128]{1,0:T(8,128)(2,1)S(1)} collective-permute-done((bf16[512,128]{1,0:T(8,128)(2,1)S(1)}, bf16[512,128]{1,0:T(8,128)(2,1)S(1)}, u32[]{:S(2)}, u32[]{:S(2)}) %collective-permute-start.2) | collective-permute-done | bytes 131104 | tf_op jit(solution)/shard_map/ppermute | solution.py:33
  15.9 1.3 %collective-permute-start.6 = (bf16[1024,128]{1,0:T(8,128)(2,1)S(1)}, bf16[1024,128]{1,0:T(8,128)(2,1)S(1)}, u32[]{:S(2)}, u32[]{:S(2)}) collective-permute-start(bf16[1024,128]{1,0:T(8,128)(2,1)S(1)} %pad_maximum_fusion.refs_2_), channel_id=1, source_target_pairs={{0,2},{1,3},{2,0},{3,1},{4,6},{5,7},{6,4},{7,5},{8,10},{9,11},{10,... | collective-permute-start | bytes 786440 | tf_op jit(solution)/shard_map/ppermute | solution.py:33
  17.2 0.4 shard_map.96.refs_2_
  17.7 0.0 collective-permute-done.5
  17.7 1.2 %collective-permute-start.7 = (bf16[1024,128]{1,0:T(8,128)(2,1)S(1)}, bf16[1024,128]{1,0:T(8,128)(2,1)S(1)}, u32[]{:S(2)}, u32[]{:S(2)}) collective-permute-start(bf16[1024,128]{1,0:T(8,128)(2,1)S(1)} %pad_maximum_fusion.1.refs_3_), channel_id=1, source_target_pairs={{0,2},{1,3},{2,0},{3,1},{4,6},{5,7},{6,4},{7,5},{8,10},{9,11},{10,... | collective-permute-start | bytes 786440 | tf_op jit(solution)/shard_map/ppermute | solution.py:33
  18.9 0.0 collective-permute-done.6.refs_1_
  18.9 0.4 shard_map.97.total
  19.4 1.6 %collective-permute-start.9 = (bf16[256,128]{1,0:T(8,128)(2,1)S(1)}, bf16[256,128]{1,0:T(8,128)(2,1)S(1)}, u32[]{:S(2)}, u32[]{:S(2)}) collective-permute-start(bf16[256,128]{1,0:T(8,128)(2,1)S(1)} %shard_map.97.total), channel_id=1, source_target_pairs={{0,1},{1,0},{2,3},{3,2},{4,5},{5,4},{6,7},{7,6},{8,9},{9,8},{10,11... | collective-permute-start | bytes 196616 | tf_op jit(solution)/shard_map/ppermute | solution.py:33
  21.0 0.0 collective-permute-done.7.refs_4_
  21.0 0.7 %shard_map.98.total = bf16[256,128]{1,0:T(8,128)(2,1)S(1)} custom-call(bf16[2,512,256]{2,1,0:T(8,128)(2,1)S(1)} %get-tuple-element.53.refs_0_, bf16[2,512,256]{2,1,0:T(8,128)(2,1)S(1)} %get-tuple-element.54.refs_1_, bf16[4,512,256]{2,1,0:T(8,128)(2,1)S(1)} %get-tuple-element.55.refs_0_.refs_2_, bf16[1024,128]{1,0:T(8,128)(2,1)S(1)} %pad_maximum_fusion.1.refs_3_, ...), custom_call_target="tpu_custom_call" | custom-call | flops 268435456 | bytes 2097152 | tf_op jit(solution)/shard_map/pallas_call | solution.py:208
  21.7 0.0 copy-start.1
  21.7 0.0 copy-start.3
  21.7 0.7 %collective-permute-start.8 = (bf16[256,128]{1,0:T(8,128)(2,1)S(1)}, bf16[256,128]{1,0:T(8,128)(2,1)S(1)}, u32[]{:S(2)}, u32[]{:S(2)}) collective-permute-start(bf16[256,128]{1,0:T(8,128)(2,1)S(1)} %shard_map.98.total), channel_id=1, source_target_pairs={{0,1},{1,0},{2,3},{3,2},{4,5},{5,4},{6,7},{7,6},{8,9},{9,8},{10,11... | collective-permute-start | bytes 196616 | tf_op jit(solution)/shard_map/ppermute | solution.py:33
  22.4 1.2 %collective-permute-done.9.got = bf16[256,128]{1,0:T(8,128)(2,1)S(1)} collective-permute-done((bf16[256,128]{1,0:T(8,128)(2,1)S(1)}, bf16[256,128]{1,0:T(8,128)(2,1)S(1)}, u32[]{:S(2)}, u32[]{:S(2)}) %collective-permute-start.9) | collective-permute-done | bytes 65568 | tf_op jit(solution)/shard_map/ppermute | solution.py:33
  23.7 0.2 shard_map.99
  23.9 2.1 %collective-permute-done.8.got = bf16[256,128]{1,0:T(8,128)(2,1)S(1)} collective-permute-done((bf16[256,128]{1,0:T(8,128)(2,1)S(1)}, bf16[256,128]{1,0:T(8,128)(2,1)S(1)}, u32[]{:S(2)}, u32[]{:S(2)}) %collective-permute-start.8) | collective-permute-done | bytes 65568 | tf_op jit(solution)/shard_map/ppermute | solution.py:33
  26.0 0.5 %shard_map.100 = (bf16[128,256]{1,0:T(8,128)(2,1)S(1)}, f32[128,256]{1,0:T(8,128)S(1)}, f32[128,256]{1,0:T(8,128)S(1)}, f32[128,256]{1,0:T(8,128)S(1)}, f32[128,256]{1,0:T(8,128)S(1)}) custom-call(s32[2,256]{1,0:T(2,128)S(1)} %broadcast_in_dim.19.flags, bf16[256,128]{1,0:T(8,128)(2,1)S(1)} %shard_map.98.total, ...), custom_call_target="tpu_custom_call" | custom-call | flops 83886080 | bytes 1048576 | tf_op jit(solution)/shard_map/pallas_call | solution.py:243
  26.5 0.1 collective-permute-start.10
  26.6 0.6 %shard_map.101 = bf16[128,256]{1,0:T(8,128)(2,1)} custom-call(bf16[128,256]{1,0:T(8,128)(2,1)S(1)} %get-tuple-element.68.x_ref), custom_call_target="tpu_custom_call" | custom-call | bytes 131072 | tf_op jit(solution)/shard_map/pallas_call | solution.py:251
  27.2 0.5 %collective-permute-start.13 = (f32[128,256]{1,0:T(8,128)S(1)}, f32[128,256]{1,0:T(8,128)S(1)}, u32[]{:S(2)}, u32[]{:S(2)}) collective-permute-start(f32[128,256]{1,0:T(8,128)S(1)} %get-tuple-element.74), channel_id=1, source_target_pairs={{0,2},{1,3},{2,0},{3,1},{4,6},{5,7},{6,4},{7,5},{8,10},{9,11},{10,... | collective-permute-start | bytes 393224 | tf_op jit(solution)/shard_map/ppermute | solution.py:33
  27.7 0.2 collective-permute-done.10
  27.9 0.1 collective-permute-start.11
  28.0 0.7 %collective-permute-done.13 = f32[128,256]{1,0:T(8,128)S(1)} collective-permute-done((f32[128,256]{1,0:T(8,128)S(1)}, f32[128,256]{1,0:T(8,128)S(1)}, u32[]{:S(2)}, u32[]{:S(2)}) %collective-permute-start.13) | collective-permute-done | bytes 131104 | tf_op jit(solution)/shard_map/ppermute | solution.py:33
  28.7 1.1 %collective-permute-start.14 = (bf16[128,256]{1,0:T(8,128)(2,1)S(1)}, bf16[128,256]{1,0:T(8,128)(2,1)S(1)}, u32[]{:S(2)}, u32[]{:S(2)}) collective-permute-start(bf16[128,256]{1,0:T(8,128)(2,1)S(1)} %add_convert_fusion.2), channel_id=1, source_target_pairs={{0,10},{1,11},{2,16},{3,17},{4,22},{5,23},{6,12},{7,13},{8,26},{9,... | collective-permute-start | bytes 196616 | tf_op jit(solution)/shard_map/ppermute | solution.py:33
  29.8 1.9 %collective-permute-done.11 = bf16[128,256]{1,0:T(8,128)(2,1)S(1)} collective-permute-done((bf16[128,256]{1,0:T(8,128)(2,1)S(1)}, bf16[128,256]{1,0:T(8,128)(2,1)S(1)}, u32[]{:S(2)}, u32[]{:S(2)}) %collective-permute-start.11) | collective-permute-done | bytes 65568 | tf_op jit(solution)/shard_map/ppermute | solution.py:33
  31.7 1.8 %collective-permute-start.12 = (bf16[128,256]{1,0:T(8,128)(2,1)S(1)}, bf16[128,256]{1,0:T(8,128)(2,1)S(1)}, u32[]{:S(2)}, u32[]{:S(2)}) collective-permute-start(bf16[128,256]{1,0:T(8,128)(2,1)S(1)} %add_convert_fusion.4), channel_id=1, source_target_pairs={{0,18},{1,19},{2,4},{3,5},{4,2},{5,3},{6,20},{7,21},{8,14},{9,15},... | collective-permute-start | bytes 196616 | tf_op jit(solution)/shard_map/ppermute | solution.py:33
  33.5 0.0 collective-permute-done.14
  33.5 2.0 %collective-permute-start.15 = (bf16[128,256]{1,0:T(8,128)(2,1)S(1)}, bf16[128,256]{1,0:T(8,128)(2,1)S(1)}, u32[]{:S(2)}, u32[]{:S(2)}) collective-permute-start(bf16[128,256]{1,0:T(8,128)(2,1)S(1)} %add_convert_fusion.1), channel_id=1, source_target_pairs={{0,18},{1,19},{2,4},{3,5},{4,2},{5,3},{6,20},{7,21},{8,14},{9,15},... | collective-permute-start | bytes 196616 | tf_op jit(solution)/shard_map/ppermute | solution.py:33
  35.5 1.6 %collective-permute-done.12 = bf16[128,256]{1,0:T(8,128)(2,1)S(1)} collective-permute-done((bf16[128,256]{1,0:T(8,128)(2,1)S(1)}, bf16[128,256]{1,0:T(8,128)(2,1)S(1)}, u32[]{:S(2)}, u32[]{:S(2)}) %collective-permute-start.12) | collective-permute-done | bytes 65568 | tf_op jit(solution)/shard_map/ppermute | solution.py:33
  37.1 1.1 %collective-permute-start.16 = (bf16[128,256]{1,0:T(8,128)(2,1)S(1)}, bf16[128,256]{1,0:T(8,128)(2,1)S(1)}, u32[]{:S(2)}, u32[]{:S(2)}) collective-permute-start(bf16[128,256]{1,0:T(8,128)(2,1)S(1)} %add_convert_fusion.3), channel_id=1, source_target_pairs={{0,6},{1,7},{2,8},{3,9},{4,14},{5,15},{6,0},{7,1},{8,2},{9,3},{10,... | collective-permute-start | bytes 196616 | tf_op jit(solution)/shard_map/ppermute | solution.py:33
  38.2 0.0 collective-permute-done.15
  38.2 1.0 %collective-permute-start.17 = (bf16[128,256]{1,0:T(8,128)(2,1)S(1)}, bf16[128,256]{1,0:T(8,128)(2,1)S(1)}, u32[]{:S(2)}, u32[]{:S(2)}) collective-permute-start(bf16[128,256]{1,0:T(8,128)(2,1)S(1)} %add_convert_fusion), channel_id=1, source_target_pairs={{0,6},{1,7},{2,8},{3,9},{4,14},{5,15},{6,0},{7,1},{8,2},{9,3},{10,... | collective-permute-start | bytes 196616 | tf_op jit(solution)/shard_map/ppermute | solution.py:33
  39.3 0.9 %collective-permute-start.18 = (bf16[256,256]{1,0:T(8,128)(2,1)S(1)}, bf16[256,256]{1,0:T(8,128)(2,1)S(1)}, u32[]{:S(2)}, u32[]{:S(2)}) collective-permute-start(bf16[256,256]{1,0:T(8,128)(2,1)S(1)} %pad_maximum_fusion.5), channel_id=1, source_target_pairs={{0,2},{1,3},{2,0},{3,1},{4,6},{5,7},{6,4},{7,5},{8,10},{9,11},{10,... | collective-permute-start | bytes 393224 | tf_op jit(solution)/shard_map/ppermute | solution.py:33
  40.1 0.7 %collective-permute-done.16 = bf16[128,256]{1,0:T(8,128)(2,1)S(1)} collective-permute-done((bf16[128,256]{1,0:T(8,128)(2,1)S(1)}, bf16[128,256]{1,0:T(8,128)(2,1)S(1)}, u32[]{:S(2)}, u32[]{:S(2)}) %collective-permute-start.16) | collective-permute-done | bytes 65568 | tf_op jit(solution)/shard_map/ppermute | solution.py:33
  40.9 0.1 collective-permute-start.19
  41.0 1.0 %collective-permute-done.17 = bf16[128,256]{1,0:T(8,128)(2,1)S(1)} collective-permute-done((bf16[128,256]{1,0:T(8,128)(2,1)S(1)}, bf16[128,256]{1,0:T(8,128)(2,1)S(1)}, u32[]{:S(2)}, u32[]{:S(2)}) %collective-permute-start.17) | collective-permute-done | bytes 65568 | tf_op jit(solution)/shard_map/ppermute | solution.py:33
  42.0 0.1 collective-permute-start.20
  42.1 0.0 collective-permute-done.18
  42.1 0.0 collective-permute-done.19
  42.1 1.1 %collective-permute-done.20 = bf16[128,256]{1,0:T(8,128)(2,1)S(1)} collective-permute-done((bf16[128,256]{1,0:T(8,128)(2,1)S(1)}, bf16[128,256]{1,0:T(8,128)(2,1)S(1)}, u32[]{:S(2)}, u32[]{:S(2)}) %collective-permute-start.20) | collective-permute-done | bytes 65568 | tf_op jit(solution)/shard_map/ppermute | solution.py:33
  43.2 0.9 %fusion = (f32[256,256]{1,0:T(8,128)}, f32[256,256]{1,0:T(8,128)}) fusion(bf16[256,256]{1,0:T(8,128)(2,1)S(1)} %collective-permute-done.18, pred[256]{0:T(512)(128)(4,1)S(1)} %compare_reduce_fusion, bf16[128,256]{1,0:T(8,128)(2,1)S(1)} %collective-permute-done.20, bf16[128,256]{1,0:T(8,128)(2,1)S(1)} %collective-permute-done.19, ...), kind=kLoop, calls=%fused_computation.4 | loop fusion | flops 1114112 | bytes 1048832 | tf_op jit(solution)/shard_map/jit(_where)/select_n | solution.py:269
  (21 shorter events, 0.3 us)
Async XLA Ops:
  0.6 4.4 %copy-start.2 = (bf16[128,256]{1,0:T(8,128)(2,1)S(1)}, bf16[128,256]{1,0:T(8,128)(2,1)}, u32[]{:S(2)}) copy-start(bf16[128,256]{1,0:T(8,128)(2,1)} %out_grad.1) | copy-start | bytes 196612
  0.6 13.6 %copy-start = (bf16[1,1,16,2,128,128]{5,4,3,2,1,0:T(8,128)(2,1)S(1)}, bf16[1,1,16,2,128,128]{5,4,3,2,1,0:T(8,128)(2,1)}, u32[]{:S(2)}) copy-start(bf16[1,1,16,2,128,128]{5,4,3,2,1,0:T(8,128)(2,1)} %param.8) | copy-start | bytes 3145732
  0.7 6.8 %collective-permute-start = (bf16[128,256]{1,0:T(8,128)(2,1)}, bf16[128,256]{1,0:T(8,128)(2,1)S(1)}, u32[]{:S(2)}, u32[]{:S(2)}) collective-permute-start(bf16[128,256]{1,0:T(8,128)(2,1)} %x_ref.1), channel_id=1, source_target_pairs={{0,18},{1,19},{2,8},{3,9},{4,14},{5,15},{6,20},{7,21},{8,2},{9,3},... | collective-permute-start | bytes 196616 | tf_op jit(solution)/shard_map/ppermute | solution.py:33
  4.2 0.9 %copy-start.4 = (bf16[128,256]{1,0:T(8,128)(2,1)S(1)}, bf16[128,256]{1,0:T(8,128)(2,1)}, u32[]{:S(2)}) copy-start(bf16[128,256]{1,0:T(8,128)(2,1)} %x_ref.1) | copy-start | bytes 196612
  5.1 8.0 %collective-permute-start.4 = (bf16[256,256]{1,0:T(8,128)(2,1)S(1)}, bf16[256,256]{1,0:T(8,128)(2,1)S(1)}, u32[]{:S(2)}, u32[]{:S(2)}) collective-permute-start(bf16[256,256]{1,0:T(8,128)(2,1)S(1)} %pad_maximum_fusion.3), channel_id=1, source_target_pairs={{0,1},{1,0},{2,3},{3,2},{4,5},{5,4},{6,7},{7,6},{8,9},{9,8},{10,11... | collective-permute-start | bytes 393224 | tf_op jit(solution)/shard_map/ppermute | solution.py:33
  7.6 3.8 %collective-permute-start.1 = (bf16[256,128]{1,0:T(8,128)(2,1)S(1)}, bf16[256,128]{1,0:T(8,128)(2,1)S(1)}, u32[]{:S(2)}, u32[]{:S(2)}) collective-permute-start(bf16[256,128]{1,0:T(8,128)(2,1)S(1)} %pad_maximum_fusion.8), channel_id=1, source_target_pairs={{0,6},{1,7},{2,16},{3,17},{4,22},{5,23},{6,0},{7,1},{8,26},{9,27},... | collective-permute-start | bytes 196616 | tf_op jit(solution)/shard_map/ppermute | solution.py:33
  9.2 3.9 %collective-permute-start.3 = (bf16[256,128]{1,0:T(8,128)(2,1)S(1)}, bf16[256,128]{1,0:T(8,128)(2,1)S(1)}, u32[]{:S(2)}, u32[]{:S(2)}) collective-permute-start(bf16[256,128]{1,0:T(8,128)(2,1)S(1)} %pad_maximum_fusion.9), channel_id=1, source_target_pairs={{0,6},{1,7},{2,16},{3,17},{4,22},{5,23},{6,0},{7,1},{8,26},{9,27},... | collective-permute-start | bytes 196616 | tf_op jit(solution)/shard_map/ppermute | solution.py:33
  11.4 4.5 %collective-permute-start.2 = (bf16[512,128]{1,0:T(8,128)(2,1)S(1)}, bf16[512,128]{1,0:T(8,128)(2,1)S(1)}, u32[]{:S(2)}, u32[]{:S(2)}) collective-permute-start(bf16[512,128]{1,0:T(8,128)(2,1)S(1)} %pad_maximum_fusion.2), channel_id=1, source_target_pairs={{0,10},{1,11},{2,4},{3,5},{4,2},{5,3},{6,12},{7,13},{8,14},{9,15},... | collective-permute-start | bytes 393224 | tf_op jit(solution)/shard_map/ppermute | solution.py:33
  13.1 1.2 %copy-start.5 = (s32[1,1,16]{2,1,0:T(1,128)S(1)}, s32[1,1,16]{2,1,0:T(1,128)}, u32[]{:S(2)}) copy-start(s32[1,1,16]{2,1,0:T(1,128)} %param.10) | copy-start | bytes 196
  13.1 4.6 %collective-permute-start.5 = (bf16[512,128]{1,0:T(8,128)(2,1)S(1)}, bf16[512,128]{1,0:T(8,128)(2,1)S(1)}, u32[]{:S(2)}, u32[]{:S(2)}) collective-permute-start(bf16[512,128]{1,0:T(8,128)(2,1)S(1)} %pad_maximum_fusion.4), channel_id=1, source_target_pairs={{0,10},{1,11},{2,4},{3,5},{4,2},{5,3},{6,12},{7,13},{8,14},{9,15},... | collective-permute-start | bytes 393224 | tf_op jit(solution)/shard_map/ppermute | solution.py:33
  15.9 3.0 %collective-permute-start.6 = (bf16[1024,128]{1,0:T(8,128)(2,1)S(1)}, bf16[1024,128]{1,0:T(8,128)(2,1)S(1)}, u32[]{:S(2)}, u32[]{:S(2)}) collective-permute-start(bf16[1024,128]{1,0:T(8,128)(2,1)S(1)} %pad_maximum_fusion.refs_2_), channel_id=1, source_target_pairs={{0,2},{1,3},{2,0},{3,1},{4,6},{5,7},{6,4},{7,5},{8,10},{9,11},{10,... | collective-permute-start | bytes 786440 | tf_op jit(solution)/shard_map/ppermute | solution.py:33
  17.7 3.3 %collective-permute-start.7 = (bf16[1024,128]{1,0:T(8,128)(2,1)S(1)}, bf16[1024,128]{1,0:T(8,128)(2,1)S(1)}, u32[]{:S(2)}, u32[]{:S(2)}) collective-permute-start(bf16[1024,128]{1,0:T(8,128)(2,1)S(1)} %pad_maximum_fusion.1.refs_3_), channel_id=1, source_target_pairs={{0,2},{1,3},{2,0},{3,1},{4,6},{5,7},{6,4},{7,5},{8,10},{9,11},{10,... | collective-permute-start | bytes 786440 | tf_op jit(solution)/shard_map/ppermute | solution.py:33
  19.4 4.3 %collective-permute-start.9 = (bf16[256,128]{1,0:T(8,128)(2,1)S(1)}, bf16[256,128]{1,0:T(8,128)(2,1)S(1)}, u32[]{:S(2)}, u32[]{:S(2)}) collective-permute-start(bf16[256,128]{1,0:T(8,128)(2,1)S(1)} %shard_map.97.total), channel_id=1, source_target_pairs={{0,1},{1,0},{2,3},{3,2},{4,5},{5,4},{6,7},{7,6},{8,9},{9,8},{10,11... | collective-permute-start | bytes 196616 | tf_op jit(solution)/shard_map/ppermute | solution.py:33
  21.7 2.0 %copy-start.1 = (bf16[256,256]{1,0:T(8,128)(2,1)S(1)}, bf16[256,256]{1,0:T(8,128)(2,1)}, u32[]{:S(2)}) copy-start(bf16[256,256]{1,0:T(8,128)(2,1)} %w_neigh.3) | copy-start | bytes 393220
  21.7 2.0 %copy-start.3 = (bf16[256,256]{1,0:T(8,128)(2,1)S(1)}, bf16[256,256]{1,0:T(8,128)(2,1)}, u32[]{:S(2)}) copy-start(bf16[256,256]{1,0:T(8,128)(2,1)} %w_self.1) | copy-start | bytes 393220
  21.7 4.3 %collective-permute-start.8 = (bf16[256,128]{1,0:T(8,128)(2,1)S(1)}, bf16[256,128]{1,0:T(8,128)(2,1)S(1)}, u32[]{:S(2)}, u32[]{:S(2)}) collective-permute-start(bf16[256,128]{1,0:T(8,128)(2,1)S(1)} %shard_map.98.total), channel_id=1, source_target_pairs={{0,1},{1,0},{2,3},{3,2},{4,5},{5,4},{6,7},{7,6},{8,9},{9,8},{10,11... | collective-permute-start | bytes 196616 | tf_op jit(solution)/shard_map/ppermute | solution.py:33
  26.5 1.4 %collective-permute-start.10 = (f32[128,256]{1,0:T(8,128)S(1)}, f32[128,256]{1,0:T(8,128)S(1)}, u32[]{:S(2)}, u32[]{:S(2)}) collective-permute-start(f32[128,256]{1,0:T(8,128)S(1)} %get-tuple-element.67), channel_id=1, source_target_pairs={{0,2},{1,3},{2,0},{3,1},{4,6},{5,7},{6,4},{7,5},{8,10},{9,11},{10,... | collective-permute-start | bytes 393224 | tf_op jit(solution)/shard_map/ppermute | solution.py:33
  27.2 1.5 %collective-permute-start.13 = (f32[128,256]{1,0:T(8,128)S(1)}, f32[128,256]{1,0:T(8,128)S(1)}, u32[]{:S(2)}, u32[]{:S(2)}) collective-permute-start(f32[128,256]{1,0:T(8,128)S(1)} %get-tuple-element.74), channel_id=1, source_target_pairs={{0,2},{1,3},{2,0},{3,1},{4,6},{5,7},{6,4},{7,5},{8,10},{9,11},{10,... | collective-permute-start | bytes 393224 | tf_op jit(solution)/shard_map/ppermute | solution.py:33
  27.9 3.8 %collective-permute-start.11 = (bf16[128,256]{1,0:T(8,128)(2,1)S(1)}, bf16[128,256]{1,0:T(8,128)(2,1)S(1)}, u32[]{:S(2)}, u32[]{:S(2)}) collective-permute-start(bf16[128,256]{1,0:T(8,128)(2,1)S(1)} %add_convert_fusion.5), channel_id=1, source_target_pairs={{0,10},{1,11},{2,16},{3,17},{4,22},{5,23},{6,12},{7,13},{8,26},{9,... | collective-permute-start | bytes 196616 | tf_op jit(solution)/shard_map/ppermute | solution.py:33
  28.7 4.8 %collective-permute-start.14 = (bf16[128,256]{1,0:T(8,128)(2,1)S(1)}, bf16[128,256]{1,0:T(8,128)(2,1)S(1)}, u32[]{:S(2)}, u32[]{:S(2)}) collective-permute-start(bf16[128,256]{1,0:T(8,128)(2,1)S(1)} %add_convert_fusion.2), channel_id=1, source_target_pairs={{0,10},{1,11},{2,16},{3,17},{4,22},{5,23},{6,12},{7,13},{8,26},{9,... | collective-permute-start | bytes 196616 | tf_op jit(solution)/shard_map/ppermute | solution.py:33
  31.7 5.4 %collective-permute-start.12 = (bf16[128,256]{1,0:T(8,128)(2,1)S(1)}, bf16[128,256]{1,0:T(8,128)(2,1)S(1)}, u32[]{:S(2)}, u32[]{:S(2)}) collective-permute-start(bf16[128,256]{1,0:T(8,128)(2,1)S(1)} %add_convert_fusion.4), channel_id=1, source_target_pairs={{0,18},{1,19},{2,4},{3,5},{4,2},{5,3},{6,20},{7,21},{8,14},{9,15},... | collective-permute-start | bytes 196616 | tf_op jit(solution)/shard_map/ppermute | solution.py:33
  33.5 4.7 %collective-permute-start.15 = (bf16[128,256]{1,0:T(8,128)(2,1)S(1)}, bf16[128,256]{1,0:T(8,128)(2,1)S(1)}, u32[]{:S(2)}, u32[]{:S(2)}) collective-permute-start(bf16[128,256]{1,0:T(8,128)(2,1)S(1)} %add_convert_fusion.1), channel_id=1, source_target_pairs={{0,18},{1,19},{2,4},{3,5},{4,2},{5,3},{6,20},{7,21},{8,14},{9,15},... | collective-permute-start | bytes 196616 | tf_op jit(solution)/shard_map/ppermute | solution.py:33
  37.1 3.8 %collective-permute-start.16 = (bf16[128,256]{1,0:T(8,128)(2,1)S(1)}, bf16[128,256]{1,0:T(8,128)(2,1)S(1)}, u32[]{:S(2)}, u32[]{:S(2)}) collective-permute-start(bf16[128,256]{1,0:T(8,128)(2,1)S(1)} %add_convert_fusion.3), channel_id=1, source_target_pairs={{0,6},{1,7},{2,8},{3,9},{4,14},{5,15},{6,0},{7,1},{8,2},{9,3},{10,... | collective-permute-start | bytes 196616 | tf_op jit(solution)/shard_map/ppermute | solution.py:33
  38.2 3.8 %collective-permute-start.17 = (bf16[128,256]{1,0:T(8,128)(2,1)S(1)}, bf16[128,256]{1,0:T(8,128)(2,1)S(1)}, u32[]{:S(2)}, u32[]{:S(2)}) collective-permute-start(bf16[128,256]{1,0:T(8,128)(2,1)S(1)} %add_convert_fusion), channel_id=1, source_target_pairs={{0,6},{1,7},{2,8},{3,9},{4,14},{5,15},{6,0},{7,1},{8,2},{9,3},{10,... | collective-permute-start | bytes 196616 | tf_op jit(solution)/shard_map/ppermute | solution.py:33
  39.3 2.9 %collective-permute-start.18 = (bf16[256,256]{1,0:T(8,128)(2,1)S(1)}, bf16[256,256]{1,0:T(8,128)(2,1)S(1)}, u32[]{:S(2)}, u32[]{:S(2)}) collective-permute-start(bf16[256,256]{1,0:T(8,128)(2,1)S(1)} %pad_maximum_fusion.5), channel_id=1, source_target_pairs={{0,2},{1,3},{2,0},{3,1},{4,6},{5,7},{6,4},{7,5},{8,10},{9,11},{10,... | collective-permute-start | bytes 393224 | tf_op jit(solution)/shard_map/ppermute | solution.py:33
  40.9 1.3 %collective-permute-start.19 = (bf16[128,256]{1,0:T(8,128)(2,1)S(1)}, bf16[128,256]{1,0:T(8,128)(2,1)S(1)}, u32[]{:S(2)}, u32[]{:S(2)}) collective-permute-start(bf16[128,256]{1,0:T(8,128)(2,1)S(1)} %collective-permute-done.16), channel_id=1, source_target_pairs={{0,2},{1,3},{2,0},{3,1},{4,6},{5,7},{6,4},{7,5},{8,10},{9,11},{10,... | collective-permute-start | bytes 196616 | tf_op jit(solution)/shard_map/ppermute | solution.py:33
  42.0 1.3 %collective-permute-start.20 = (bf16[128,256]{1,0:T(8,128)(2,1)S(1)}, bf16[128,256]{1,0:T(8,128)(2,1)S(1)}, u32[]{:S(2)}, u32[]{:S(2)}) collective-permute-start(bf16[128,256]{1,0:T(8,128)(2,1)S(1)} %collective-permute-done.17), channel_id=1, source_target_pairs={{0,2},{1,3},{2,0},{3,1},{4,6},{5,7},{6,4},{7,5},{8,10},{9,11},{10,... | collective-permute-start | bytes 196616 | tf_op jit(solution)/shard_map/ppermute | solution.py:33

commit v7 on v6

--- a/solution.py
+++ b/solution.py
@@ -187,7 +187,7 @@
     for even, odd in zip(hops[1:-1], turned[1:-1], strict=True):
         gots = [trade(part, (even, 0), (odd, 0)) for part in held]
         gots[0], place, flags, row_ids, live_count = barrier((gots[0], place, flags, row_ids, live_count))
-        gots[-1], far = barrier((gots[-1], far))
+        gots[0], far = barrier((gots[0], far))
         held = [jnp.concatenate([part, got], axis=0) for part, got in zip(held, gots, strict=True)]
     tables = [place, row_ids, live_count, tiles]
     table_specs = [SMEM] * 3 + [VMEM]

time: 44.3 us -> 44.3 us (level)
  no operation moved by 1% of the time
where the time goes in v7:
time: 44.3 us; the launch traced here: 44.1 us
  starting transfers between devices  23.3 us (53%)
  waiting for transfers between devices  13.1 us (30%)
  Pallas kernels  3.72 us (8%)
  local copies, waits for them, and re-layouts  1.84 us (4%)
  other arithmetic  1.23 us (3%)
  between operations  0.86 us (2%)
    ppermute x21, starting transfers between devices, swap(): return lax.ppermute(x, ('node', 'rep'), pairs)  23.3 us
    ppermute x21, waiting for transfers between devices, swap(): return lax.ppermute(x, ('node', 'rep'), pairs)  13.1 us
    unnamed x13, local copies, waits for them, and re-layouts  1.65 us
    pallas_call x3, Pallas kernels, sums(): call(functools.partial(tile_sums, steps, prebuilt, len(columns), seed is...  1.57 us
  transfers between devices with their start and end apart: 21, of which 11 were waited for; matrix products, arithmetic and copies ran while one was open for 3% of the time, Pallas kernels for 7%

profile of v7, /device:TPU:0, one launch (start us, length us, event | category | flops | bytes accessed | tf_op | source)
XLA Modules:
  0.0 44.1 jit_solution(16871801550971346256)
XLA Ops:
  0.6 0.0 copy-start.2
  0.6 0.0 copy-start
  0.7 3.5 %collective-permute-start = (bf16[128,256]{1,0:T(8,128)(2,1)}, bf16[128,256]{1,0:T(8,128)(2,1)S(1)}, u32[]{:S(2)}, u32[]{:S(2)}) collective-permute-start(bf16[128,256]{1,0:T(8,128)(2,1)} %x_ref.1), channel_id=1, source_target_pairs={{0,18},{1,19},{2,8},{3,9},{4,14},{5,15},{6,20},{7,21},{8,2},{9,3},... | collective-permute-start | bytes 196616 | tf_op jit(solution)/shard_map/ppermute | solution.py:33
  4.2 0.9 %copy-done.4 = bf16[128,256]{1,0:T(8,128)(2,1)S(1)} copy-done((bf16[128,256]{1,0:T(8,128)(2,1)S(1)}, bf16[128,256]{1,0:T(8,128)(2,1)}, u32[]{:S(2)}) %copy-start.4) | copy-done | bytes 65560
  5.1 0.0 copy-done.2
  5.1 1.6 %collective-permute-start.2 = (bf16[256,256]{1,0:T(8,128)(2,1)S(1)}, bf16[256,256]{1,0:T(8,128)(2,1)S(1)}, u32[]{:S(2)}, u32[]{:S(2)}) collective-permute-start(bf16[256,256]{1,0:T(8,128)(2,1)S(1)} %pad_maximum_fusion.2), channel_id=1, source_target_pairs={{0,1},{1,0},{2,3},{3,2},{4,5},{5,4},{6,7},{7,6},{8,9},{9,8},{10,11... | collective-permute-start | bytes 393224 | tf_op jit(solution)/shard_map/ppermute | solution.py:33
  6.7 0.8 %copy.11 = s32[1,1,16,2]{3,2,1,0:T(8,128)S(1)} copy(s32[1,1,16,2]{2,3,1,0:T(2,128)} %param.9) | data formatting | bytes 256 | tf_op args[2]
  7.4 0.1 reshape_squeeze.3.rows
  7.5 0.0 collective-permute-done
  7.6 1.6 %collective-permute-start.1 = (bf16[256,128]{1,0:T(8,128)(2,1)S(1)}, bf16[256,128]{1,0:T(8,128)(2,1)S(1)}, u32[]{:S(2)}, u32[]{:S(2)}) collective-permute-start(bf16[256,128]{1,0:T(8,128)(2,1)S(1)} %pad_maximum_fusion.8), channel_id=1, source_target_pairs={{0,6},{1,7},{2,16},{3,17},{4,22},{5,23},{6,0},{7,1},{8,26},{9,27},... | collective-permute-start | bytes 196616 | tf_op jit(solution)/shard_map/ppermute | solution.py:33
  9.2 0.2 collective-permute-start.4
  9.4 0.1 pad_add_fusion.1
  9.5 0.1 pad_add_fusion.place
  9.5 1.8 %collective-permute-done.1 = bf16[256,128]{1,0:T(8,128)(2,1)S(1)} collective-permute-done((bf16[256,128]{1,0:T(8,128)(2,1)S(1)}, bf16[256,128]{1,0:T(8,128)(2,1)S(1)}, u32[]{:S(2)}, u32[]{:S(2)}) %collective-permute-start.1) | collective-permute-done | bytes 65568 | tf_op jit(solution)/shard_map/ppermute | solution.py:33
  11.3 0.1 broadcast_in_dim.19.flags
  11.4 0.0 collective-permute-done.2
  11.4 1.6 %collective-permute-start.3 = (bf16[512,128]{1,0:T(8,128)(2,1)S(1)}, bf16[512,128]{1,0:T(8,128)(2,1)S(1)}, u32[]{:S(2)}, u32[]{:S(2)}) collective-permute-start(bf16[512,128]{1,0:T(8,128)(2,1)S(1)} %pad_maximum_fusion.3), channel_id=1, source_target_pairs={{0,10},{1,11},{2,4},{3,5},{4,2},{5,3},{6,12},{7,13},{8,14},{9,15},... | collective-permute-start | bytes 393224 | tf_op jit(solution)/shard_map/ppermute | solution.py:33
  13.0 0.0 collective-permute-done.4
  13.1 0.0 copy-start.5
  13.1 1.2 %collective-permute-start.5 = (bf16[512,128]{1,0:T(8,128)(2,1)S(1)}, bf16[512,128]{1,0:T(8,128)(2,1)S(1)}, u32[]{:S(2)}, u32[]{:S(2)}) collective-permute-start(bf16[512,128]{1,0:T(8,128)(2,1)S(1)} %pad_maximum_fusion.4), channel_id=1, source_target_pairs={{0,10},{1,11},{2,4},{3,5},{4,2},{5,3},{6,12},{7,13},{8,14},{9,15},... | collective-permute-start | bytes 393224 | tf_op jit(solution)/shard_map/ppermute | solution.py:33
  14.2 0.0 copy-done
  14.2 0.8 %shard_map.95 = (bf16[2,512,256]{2,1,0:T(8,128)(2,1)S(1)}, bf16[2,512,256]{2,1,0:T(8,128)(2,1)S(1)}, bf16[4,512,256]{2,1,0:T(8,128)(2,1)S(1)}) custom-call(s32[4]{0:T(128)S(1)} %pad_add_fusion.place, s32[32]{0:T(128)S(1)} %reshape_squeeze.3.rows, s32[16]{0:T(128)S(1)} %bitcast.9, bf16[16,2,128,128]{3,2,1,0:T(8,128)(2,1)S(1)} %bitcast.8), custom_call_target="tpu_custom_call" | custom-call | bytes 6291456 | tf_op jit(solution)/shard_map/pallas_call | solution.py:196
  15.1 0.8 %collective-permute-done.3 = bf16[512,128]{1,0:T(8,128)(2,1)S(1)} collective-permute-done((bf16[512,128]{1,0:T(8,128)(2,1)S(1)}, bf16[512,128]{1,0:T(8,128)(2,1)S(1)}, u32[]{:S(2)}, u32[]{:S(2)}) %collective-permute-start.3) | collective-permute-done | bytes 131104 | tf_op jit(solution)/shard_map/ppermute | solution.py:33
  15.9 1.3 %collective-permute-start.6 = (bf16[1024,128]{1,0:T(8,128)(2,1)S(1)}, bf16[1024,128]{1,0:T(8,128)(2,1)S(1)}, u32[]{:S(2)}, u32[]{:S(2)}) collective-permute-start(bf16[1024,128]{1,0:T(8,128)(2,1)S(1)} %pad_maximum_fusion.refs_2_), channel_id=1, source_target_pairs={{0,2},{1,3},{2,0},{3,1},{4,6},{5,7},{6,4},{7,5},{8,10},{9,11},{10,... | collective-permute-start | bytes 786440 | tf_op jit(solution)/shard_map/ppermute | solution.py:33
  17.2 0.4 shard_map.96.refs_2_
  17.7 0.0 collective-permute-done.5
  17.7 1.2 %collective-permute-start.7 = (bf16[1024,128]{1,0:T(8,128)(2,1)S(1)}, bf16[1024,128]{1,0:T(8,128)(2,1)S(1)}, u32[]{:S(2)}, u32[]{:S(2)}) collective-permute-start(bf16[1024,128]{1,0:T(8,128)(2,1)S(1)} %pad_maximum_fusion.1.refs_3_), channel_id=1, source_target_pairs={{0,2},{1,3},{2,0},{3,1},{4,6},{5,7},{6,4},{7,5},{8,10},{9,11},{10,... | collective-permute-start | bytes 786440 | tf_op jit(solution)/shard_map/ppermute | solution.py:33
  18.9 0.0 collective-permute-done.6.refs_1_
  18.9 0.4 shard_map.97.total
  19.3 1.6 %collective-permute-start.9 = (bf16[256,128]{1,0:T(8,128)(2,1)S(1)}, bf16[256,128]{1,0:T(8,128)(2,1)S(1)}, u32[]{:S(2)}, u32[]{:S(2)}) collective-permute-start(bf16[256,128]{1,0:T(8,128)(2,1)S(1)} %shard_map.97.total), channel_id=1, source_target_pairs={{0,1},{1,0},{2,3},{3,2},{4,5},{5,4},{6,7},{7,6},{8,9},{9,8},{10,11... | collective-permute-start | bytes 196616 | tf_op jit(solution)/shard_map/ppermute | solution.py:33
  21.0 0.0 collective-permute-done.7.refs_4_
  21.0 0.7 %shard_map.98.total = bf16[256,128]{1,0:T(8,128)(2,1)S(1)} custom-call(bf16[2,512,256]{2,1,0:T(8,128)(2,1)S(1)} %get-tuple-element.54.refs_0_, bf16[2,512,256]{2,1,0:T(8,128)(2,1)S(1)} %get-tuple-element.55.refs_1_, bf16[4,512,256]{2,1,0:T(8,128)(2,1)S(1)} %get-tuple-element.56.refs_0_.refs_2_, bf16[1024,128]{1,0:T(8,128)(2,1)S(1)} %pad_maximum_fusion.1.refs_3_, ...), custom_call_target="tpu_custom_call" | custom-call | flops 268435456 | bytes 2097152 | tf_op jit(solution)/shard_map/pallas_call | solution.py:208
  21.7 0.0 copy-start.1
  21.7 0.0 copy-start.3
  21.7 0.7 %collective-permute-start.8 = (bf16[256,128]{1,0:T(8,128)(2,1)S(1)}, bf16[256,128]{1,0:T(8,128)(2,1)S(1)}, u32[]{:S(2)}, u32[]{:S(2)}) collective-permute-start(bf16[256,128]{1,0:T(8,128)(2,1)S(1)} %shard_map.98.total), channel_id=1, source_target_pairs={{0,1},{1,0},{2,3},{3,2},{4,5},{5,4},{6,7},{7,6},{8,9},{9,8},{10,11... | collective-permute-start | bytes 196616 | tf_op jit(solution)/shard_map/ppermute | solution.py:33
  22.4 1.2 %collective-permute-done.9.got = bf16[256,128]{1,0:T(8,128)(2,1)S(1)} collective-permute-done((bf16[256,128]{1,0:T(8,128)(2,1)S(1)}, bf16[256,128]{1,0:T(8,128)(2,1)S(1)}, u32[]{:S(2)}, u32[]{:S(2)}) %collective-permute-start.9) | collective-permute-done | bytes 65568 | tf_op jit(solution)/shard_map/ppermute | solution.py:33
  23.7 0.0 copy-done.3
  23.7 0.2 shard_map.99
  23.9 2.1 %collective-permute-done.8.got = bf16[256,128]{1,0:T(8,128)(2,1)S(1)} collective-permute-done((bf16[256,128]{1,0:T(8,128)(2,1)S(1)}, bf16[256,128]{1,0:T(8,128)(2,1)S(1)}, u32[]{:S(2)}, u32[]{:S(2)}) %collective-permute-start.8) | collective-permute-done | bytes 65568 | tf_op jit(solution)/shard_map/ppermute | solution.py:33
  26.0 0.5 %shard_map.100 = (bf16[128,256]{1,0:T(8,128)(2,1)S(1)}, f32[128,256]{1,0:T(8,128)S(1)}, f32[128,256]{1,0:T(8,128)S(1)}, f32[128,256]{1,0:T(8,128)S(1)}, f32[128,256]{1,0:T(8,128)S(1)}) custom-call(s32[2,256]{1,0:T(2,128)S(1)} %broadcast_in_dim.19.flags, bf16[256,128]{1,0:T(8,128)(2,1)S(1)} %shard_map.98.total, ...), custom_call_target="tpu_custom_call" | custom-call | flops 83886080 | bytes 1048576 | tf_op jit(solution)/shard_map/pallas_call | solution.py:243
  26.5 0.1 collective-permute-start.10
  26.6 0.6 %shard_map.101 = bf16[128,256]{1,0:T(8,128)(2,1)} custom-call(bf16[128,256]{1,0:T(8,128)(2,1)S(1)} %get-tuple-element.68.x_ref), custom_call_target="tpu_custom_call" | custom-call | bytes 131072 | tf_op jit(solution)/shard_map/pallas_call | solution.py:251
  27.2 0.5 %collective-permute-start.13 = (f32[128,256]{1,0:T(8,128)S(1)}, f32[128,256]{1,0:T(8,128)S(1)}, u32[]{:S(2)}, u32[]{:S(2)}) collective-permute-start(f32[128,256]{1,0:T(8,128)S(1)} %get-tuple-element.74), channel_id=1, source_target_pairs={{0,2},{1,3},{2,0},{3,1},{4,6},{5,7},{6,4},{7,5},{8,10},{9,11},{10,... | collective-permute-start | bytes 393224 | tf_op jit(solution)/shard_map/ppermute | solution.py:33
  27.7 0.2 collective-permute-done.10
  27.9 0.1 collective-permute-start.11
  28.0 0.7 %collective-permute-done.13 = f32[128,256]{1,0:T(8,128)S(1)} collective-permute-done((f32[128,256]{1,0:T(8,128)S(1)}, f32[128,256]{1,0:T(8,128)S(1)}, u32[]{:S(2)}, u32[]{:S(2)}) %collective-permute-start.13) | collective-permute-done | bytes 131104 | tf_op jit(solution)/shard_map/ppermute | solution.py:33
  28.7 1.1 %collective-permute-start.14 = (bf16[128,256]{1,0:T(8,128)(2,1)S(1)}, bf16[128,256]{1,0:T(8,128)(2,1)S(1)}, u32[]{:S(2)}, u32[]{:S(2)}) collective-permute-start(bf16[128,256]{1,0:T(8,128)(2,1)S(1)} %add_convert_fusion.2), channel_id=1, source_target_pairs={{0,10},{1,11},{2,16},{3,17},{4,22},{5,23},{6,12},{7,13},{8,26},{9,... | collective-permute-start | bytes 196616 | tf_op jit(solution)/shard_map/ppermute | solution.py:33
  29.8 1.9 %collective-permute-done.11 = bf16[128,256]{1,0:T(8,128)(2,1)S(1)} collective-permute-done((bf16[128,256]{1,0:T(8,128)(2,1)S(1)}, bf16[128,256]{1,0:T(8,128)(2,1)S(1)}, u32[]{:S(2)}, u32[]{:S(2)}) %collective-permute-start.11) | collective-permute-done | bytes 65568 | tf_op jit(solution)/shard_map/ppermute | solution.py:33
  31.7 1.8 %collective-permute-start.12 = (bf16[128,256]{1,0:T(8,128)(2,1)S(1)}, bf16[128,256]{1,0:T(8,128)(2,1)S(1)}, u32[]{:S(2)}, u32[]{:S(2)}) collective-permute-start(bf16[128,256]{1,0:T(8,128)(2,1)S(1)} %add_convert_fusion.4), channel_id=1, source_target_pairs={{0,18},{1,19},{2,4},{3,5},{4,2},{5,3},{6,20},{7,21},{8,14},{9,15},... | collective-permute-start | bytes 196616 | tf_op jit(solution)/shard_map/ppermute | solution.py:33
  33.5 0.0 collective-permute-done.14
  33.5 2.0 %collective-permute-start.15 = (bf16[128,256]{1,0:T(8,128)(2,1)S(1)}, bf16[128,256]{1,0:T(8,128)(2,1)S(1)}, u32[]{:S(2)}, u32[]{:S(2)}) collective-permute-start(bf16[128,256]{1,0:T(8,128)(2,1)S(1)} %add_convert_fusion.1), channel_id=1, source_target_pairs={{0,18},{1,19},{2,4},{3,5},{4,2},{5,3},{6,20},{7,21},{8,14},{9,15},... | collective-permute-start | bytes 196616 | tf_op jit(solution)/shard_map/ppermute | solution.py:33
  35.5 1.6 %collective-permute-done.12 = bf16[128,256]{1,0:T(8,128)(2,1)S(1)} collective-permute-done((bf16[128,256]{1,0:T(8,128)(2,1)S(1)}, bf16[128,256]{1,0:T(8,128)(2,1)S(1)}, u32[]{:S(2)}, u32[]{:S(2)}) %collective-permute-start.12) | collective-permute-done | bytes 65568 | tf_op jit(solution)/shard_map/ppermute | solution.py:33
  37.1 1.1 %collective-permute-start.16 = (bf16[128,256]{1,0:T(8,128)(2,1)S(1)}, bf16[128,256]{1,0:T(8,128)(2,1)S(1)}, u32[]{:S(2)}, u32[]{:S(2)}) collective-permute-start(bf16[128,256]{1,0:T(8,128)(2,1)S(1)} %add_convert_fusion.3), channel_id=1, source_target_pairs={{0,6},{1,7},{2,8},{3,9},{4,14},{5,15},{6,0},{7,1},{8,2},{9,3},{10,... | collective-permute-start | bytes 196616 | tf_op jit(solution)/shard_map/ppermute | solution.py:33
  38.2 0.0 collective-permute-done.15
  38.2 1.0 %collective-permute-start.17 = (bf16[128,256]{1,0:T(8,128)(2,1)S(1)}, bf16[128,256]{1,0:T(8,128)(2,1)S(1)}, u32[]{:S(2)}, u32[]{:S(2)}) collective-permute-start(bf16[128,256]{1,0:T(8,128)(2,1)S(1)} %add_convert_fusion), channel_id=1, source_target_pairs={{0,6},{1,7},{2,8},{3,9},{4,14},{5,15},{6,0},{7,1},{8,2},{9,3},{10,... | collective-permute-start | bytes 196616 | tf_op jit(solution)/shard_map/ppermute | solution.py:33
  39.3 0.9 %collective-permute-start.18 = (bf16[256,256]{1,0:T(8,128)(2,1)S(1)}, bf16[256,256]{1,0:T(8,128)(2,1)S(1)}, u32[]{:S(2)}, u32[]{:S(2)}) collective-permute-start(bf16[256,256]{1,0:T(8,128)(2,1)S(1)} %pad_maximum_fusion.5), channel_id=1, source_target_pairs={{0,2},{1,3},{2,0},{3,1},{4,6},{5,7},{6,4},{7,5},{8,10},{9,11},{10,... | collective-permute-start | bytes 393224 | tf_op jit(solution)/shard_map/ppermute | solution.py:33
  40.1 0.7 %collective-permute-done.16 = bf16[128,256]{1,0:T(8,128)(2,1)S(1)} collective-permute-done((bf16[128,256]{1,0:T(8,128)(2,1)S(1)}, bf16[128,256]{1,0:T(8,128)(2,1)S(1)}, u32[]{:S(2)}, u32[]{:S(2)}) %collective-permute-start.16) | collective-permute-done | bytes 65568 | tf_op jit(solution)/shard_map/ppermute | solution.py:33
  40.9 0.1 collective-permute-start.19
  41.0 1.0 %collective-permute-done.17 = bf16[128,256]{1,0:T(8,128)(2,1)S(1)} collective-permute-done((bf16[128,256]{1,0:T(8,128)(2,1)S(1)}, bf16[128,256]{1,0:T(8,128)(2,1)S(1)}, u32[]{:S(2)}, u32[]{:S(2)}) %collective-permute-start.17) | collective-permute-done | bytes 65568 | tf_op jit(solution)/shard_map/ppermute | solution.py:33
  42.0 0.1 collective-permute-start.20
  42.1 0.0 collective-permute-done.18
  42.1 0.0 collective-permute-done.19
  42.1 1.1 %collective-permute-done.20 = bf16[128,256]{1,0:T(8,128)(2,1)S(1)} collective-permute-done((bf16[128,256]{1,0:T(8,128)(2,1)S(1)}, bf16[128,256]{1,0:T(8,128)(2,1)S(1)}, u32[]{:S(2)}, u32[]{:S(2)}) %collective-permute-start.20) | collective-permute-done | bytes 65568 | tf_op jit(solution)/shard_map/ppermute | solution.py:33
  43.2 0.9 %fusion = (f32[256,256]{1,0:T(8,128)}, f32[256,256]{1,0:T(8,128)}) fusion(bf16[256,256]{1,0:T(8,128)(2,1)S(1)} %collective-permute-done.18, pred[256]{0:T(512)(128)(4,1)S(1)} %compare_reduce_fusion, bf16[128,256]{1,0:T(8,128)(2,1)S(1)} %collective-permute-done.20, bf16[128,256]{1,0:T(8,128)(2,1)S(1)} %collective-permute-done.19, ...), kind=kLoop, calls=%fused_computation.4 | loop fusion | flops 1114112 | bytes 1048832 | tf_op jit(solution)/shard_map/jit(_where)/select_n | solution.py:269
  (21 shorter events, 0.3 us)
Async XLA Ops:
  0.6 4.4 %copy-start.2 = (bf16[128,256]{1,0:T(8,128)(2,1)S(1)}, bf16[128,256]{1,0:T(8,128)(2,1)}, u32[]{:S(2)}) copy-start(bf16[128,256]{1,0:T(8,128)(2,1)} %out_grad.1) | copy-start | bytes 196612
  0.6 13.6 %copy-start = (bf16[1,1,16,2,128,128]{5,4,3,2,1,0:T(8,128)(2,1)S(1)}, bf16[1,1,16,2,128,128]{5,4,3,2,1,0:T(8,128)(2,1)}, u32[]{:S(2)}) copy-start(bf16[1,1,16,2,128,128]{5,4,3,2,1,0:T(8,128)(2,1)} %param.8) | copy-start | bytes 3145732
  0.7 6.8 %collective-permute-start = (bf16[128,256]{1,0:T(8,128)(2,1)}, bf16[128,256]{1,0:T(8,128)(2,1)S(1)}, u32[]{:S(2)}, u32[]{:S(2)}) collective-permute-start(bf16[128,256]{1,0:T(8,128)(2,1)} %x_ref.1), channel_id=1, source_target_pairs={{0,18},{1,19},{2,8},{3,9},{4,14},{5,15},{6,20},{7,21},{8,2},{9,3},... | collective-permute-start | bytes 196616 | tf_op jit(solution)/shard_map/ppermute | solution.py:33
  4.2 0.9 %copy-start.4 = (bf16[128,256]{1,0:T(8,128)(2,1)S(1)}, bf16[128,256]{1,0:T(8,128)(2,1)}, u32[]{:S(2)}) copy-start(bf16[128,256]{1,0:T(8,128)(2,1)} %x_ref.1) | copy-start | bytes 196612
  5.1 6.3 %collective-permute-start.2 = (bf16[256,256]{1,0:T(8,128)(2,1)S(1)}, bf16[256,256]{1,0:T(8,128)(2,1)S(1)}, u32[]{:S(2)}, u32[]{:S(2)}) collective-permute-start(bf16[256,256]{1,0:T(8,128)(2,1)S(1)} %pad_maximum_fusion.2), channel_id=1, source_target_pairs={{0,1},{1,0},{2,3},{3,2},{4,5},{5,4},{6,7},{7,6},{8,9},{9,8},{10,11... | collective-permute-start | bytes 393224 | tf_op jit(solution)/shard_map/ppermute | solution.py:33
  7.6 3.8 %collective-permute-start.1 = (bf16[256,128]{1,0:T(8,128)(2,1)S(1)}, bf16[256,128]{1,0:T(8,128)(2,1)S(1)}, u32[]{:S(2)}, u32[]{:S(2)}) collective-permute-start(bf16[256,128]{1,0:T(8,128)(2,1)S(1)} %pad_maximum_fusion.8), channel_id=1, source_target_pairs={{0,6},{1,7},{2,16},{3,17},{4,22},{5,23},{6,0},{7,1},{8,26},{9,27},... | collective-permute-start | bytes 196616 | tf_op jit(solution)/shard_map/ppermute | solution.py:33
  9.2 3.9 %collective-permute-start.4 = (bf16[256,128]{1,0:T(8,128)(2,1)S(1)}, bf16[256,128]{1,0:T(8,128)(2,1)S(1)}, u32[]{:S(2)}, u32[]{:S(2)}) collective-permute-start(bf16[256,128]{1,0:T(8,128)(2,1)S(1)} %pad_maximum_fusion.9), channel_id=1, source_target_pairs={{0,6},{1,7},{2,16},{3,17},{4,22},{5,23},{6,0},{7,1},{8,26},{9,27},... | collective-permute-start | bytes 196616 | tf_op jit(solution)/shard_map/ppermute | solution.py:33
  11.4 4.5 %collective-permute-start.3 = (bf16[512,128]{1,0:T(8,128)(2,1)S(1)}, bf16[512,128]{1,0:T(8,128)(2,1)S(1)}, u32[]{:S(2)}, u32[]{:S(2)}) collective-permute-start(bf16[512,128]{1,0:T(8,128)(2,1)S(1)} %pad_maximum_fusion.3), channel_id=1, source_target_pairs={{0,10},{1,11},{2,4},{3,5},{4,2},{5,3},{6,12},{7,13},{8,14},{9,15},... | collective-permute-start | bytes 393224 | tf_op jit(solution)/shard_map/ppermute | solution.py:33
  13.1 1.2 %copy-start.5 = (s32[1,1,16]{2,1,0:T(1,128)S(1)}, s32[1,1,16]{2,1,0:T(1,128)}, u32[]{:S(2)}) copy-start(s32[1,1,16]{2,1,0:T(1,128)} %param.10) | copy-start | bytes 196
  13.1 4.6 %collective-permute-start.5 = (bf16[512,128]{1,0:T(8,128)(2,1)S(1)}, bf16[512,128]{1,0:T(8,128)(2,1)S(1)}, u32[]{:S(2)}, u32[]{:S(2)}) collective-permute-start(bf16[512,128]{1,0:T(8,128)(2,1)S(1)} %pad_maximum_fusion.4), channel_id=1, source_target_pairs={{0,10},{1,11},{2,4},{3,5},{4,2},{5,3},{6,12},{7,13},{8,14},{9,15},... | collective-permute-start | bytes 393224 | tf_op jit(solution)/shard_map/ppermute | solution.py:33
  15.9 3.0 %collective-permute-start.6 = (bf16[1024,128]{1,0:T(8,128)(2,1)S(1)}, bf16[1024,128]{1,0:T(8,128)(2,1)S(1)}, u32[]{:S(2)}, u32[]{:S(2)}) collective-permute-start(bf16[1024,128]{1,0:T(8,128)(2,1)S(1)} %pad_maximum_fusion.refs_2_), channel_id=1, source_target_pairs={{0,2},{1,3},{2,0},{3,1},{4,6},{5,7},{6,4},{7,5},{8,10},{9,11},{10,... | collective-permute-start | bytes 786440 | tf_op jit(solution)/shard_map/ppermute | solution.py:33
  17.7 3.3 %collective-permute-start.7 = (bf16[1024,128]{1,0:T(8,128)(2,1)S(1)}, bf16[1024,128]{1,0:T(8,128)(2,1)S(1)}, u32[]{:S(2)}, u32[]{:S(2)}) collective-permute-start(bf16[1024,128]{1,0:T(8,128)(2,1)S(1)} %pad_maximum_fusion.1.refs_3_), channel_id=1, source_target_pairs={{0,2},{1,3},{2,0},{3,1},{4,6},{5,7},{6,4},{7,5},{8,10},{9,11},{10,... | collective-permute-start | bytes 786440 | tf_op jit(solution)/shard_map/ppermute | solution.py:33
  19.3 4.3 %collective-permute-start.9 = (bf16[256,128]{1,0:T(8,128)(2,1)S(1)}, bf16[256,128]{1,0:T(8,128)(2,1)S(1)}, u32[]{:S(2)}, u32[]{:S(2)}) collective-permute-start(bf16[256,128]{1,0:T(8,128)(2,1)S(1)} %shard_map.97.total), channel_id=1, source_target_pairs={{0,1},{1,0},{2,3},{3,2},{4,5},{5,4},{6,7},{7,6},{8,9},{9,8},{10,11... | collective-permute-start | bytes 196616 | tf_op jit(solution)/shard_map/ppermute | solution.py:33
  21.7 2.0 %copy-start.1 = (bf16[256,256]{1,0:T(8,128)(2,1)S(1)}, bf16[256,256]{1,0:T(8,128)(2,1)}, u32[]{:S(2)}) copy-start(bf16[256,256]{1,0:T(8,128)(2,1)} %w_neigh.3) | copy-start | bytes 393220
  21.7 2.0 %copy-start.3 = (bf16[256,256]{1,0:T(8,128)(2,1)S(1)}, bf16[256,256]{1,0:T(8,128)(2,1)}, u32[]{:S(2)}) copy-start(bf16[256,256]{1,0:T(8,128)(2,1)} %w_self.1) | copy-start | bytes 393220
  21.7 4.3 %collective-permute-start.8 = (bf16[256,128]{1,0:T(8,128)(2,1)S(1)}, bf16[256,128]{1,0:T(8,128)(2,1)S(1)}, u32[]{:S(2)}, u32[]{:S(2)}) collective-permute-start(bf16[256,128]{1,0:T(8,128)(2,1)S(1)} %shard_map.98.total), channel_id=1, source_target_pairs={{0,1},{1,0},{2,3},{3,2},{4,5},{5,4},{6,7},{7,6},{8,9},{9,8},{10,11... | collective-permute-start | bytes 196616 | tf_op jit(solution)/shard_map/ppermute | solution.py:33
  26.5 1.4 %collective-permute-start.10 = (f32[128,256]{1,0:T(8,128)S(1)}, f32[128,256]{1,0:T(8,128)S(1)}, u32[]{:S(2)}, u32[]{:S(2)}) collective-permute-start(f32[128,256]{1,0:T(8,128)S(1)} %get-tuple-element.67), channel_id=1, source_target_pairs={{0,2},{1,3},{2,0},{3,1},{4,6},{5,7},{6,4},{7,5},{8,10},{9,11},{10,... | collective-permute-start | bytes 393224 | tf_op jit(solution)/shard_map/ppermute | solution.py:33
  27.2 1.5 %collective-permute-start.13 = (f32[128,256]{1,0:T(8,128)S(1)}, f32[128,256]{1,0:T(8,128)S(1)}, u32[]{:S(2)}, u32[]{:S(2)}) collective-permute-start(f32[128,256]{1,0:T(8,128)S(1)} %get-tuple-element.74), channel_id=1, source_target_pairs={{0,2},{1,3},{2,0},{3,1},{4,6},{5,7},{6,4},{7,5},{8,10},{9,11},{10,... | collective-permute-start | bytes 393224 | tf_op jit(solution)/shard_map/ppermute | solution.py:33
  27.9 3.8 %collective-permute-start.11 = (bf16[128,256]{1,0:T(8,128)(2,1)S(1)}, bf16[128,256]{1,0:T(8,128)(2,1)S(1)}, u32[]{:S(2)}, u32[]{:S(2)}) collective-permute-start(bf16[128,256]{1,0:T(8,128)(2,1)S(1)} %add_convert_fusion.5), channel_id=1, source_target_pairs={{0,10},{1,11},{2,16},{3,17},{4,22},{5,23},{6,12},{7,13},{8,26},{9,... | collective-permute-start | bytes 196616 | tf_op jit(solution)/shard_map/ppermute | solution.py:33
  28.7 4.8 %collective-permute-start.14 = (bf16[128,256]{1,0:T(8,128)(2,1)S(1)}, bf16[128,256]{1,0:T(8,128)(2,1)S(1)}, u32[]{:S(2)}, u32[]{:S(2)}) collective-permute-start(bf16[128,256]{1,0:T(8,128)(2,1)S(1)} %add_convert_fusion.2), channel_id=1, source_target_pairs={{0,10},{1,11},{2,16},{3,17},{4,22},{5,23},{6,12},{7,13},{8,26},{9,... | collective-permute-start | bytes 196616 | tf_op jit(solution)/shard_map/ppermute | solution.py:33
  31.7 5.4 %collective-permute-start.12 = (bf16[128,256]{1,0:T(8,128)(2,1)S(1)}, bf16[128,256]{1,0:T(8,128)(2,1)S(1)}, u32[]{:S(2)}, u32[]{:S(2)}) collective-permute-start(bf16[128,256]{1,0:T(8,128)(2,1)S(1)} %add_convert_fusion.4), channel_id=1, source_target_pairs={{0,18},{1,19},{2,4},{3,5},{4,2},{5,3},{6,20},{7,21},{8,14},{9,15},... | collective-permute-start | bytes 196616 | tf_op jit(solution)/shard_map/ppermute | solution.py:33
  33.5 4.7 %collective-permute-start.15 = (bf16[128,256]{1,0:T(8,128)(2,1)S(1)}, bf16[128,256]{1,0:T(8,128)(2,1)S(1)}, u32[]{:S(2)}, u32[]{:S(2)}) collective-permute-start(bf16[128,256]{1,0:T(8,128)(2,1)S(1)} %add_convert_fusion.1), channel_id=1, source_target_pairs={{0,18},{1,19},{2,4},{3,5},{4,2},{5,3},{6,20},{7,21},{8,14},{9,15},... | collective-permute-start | bytes 196616 | tf_op jit(solution)/shard_map/ppermute | solution.py:33
  37.1 3.8 %collective-permute-start.16 = (bf16[128,256]{1,0:T(8,128)(2,1)S(1)}, bf16[128,256]{1,0:T(8,128)(2,1)S(1)}, u32[]{:S(2)}, u32[]{:S(2)}) collective-permute-start(bf16[128,256]{1,0:T(8,128)(2,1)S(1)} %add_convert_fusion.3), channel_id=1, source_target_pairs={{0,6},{1,7},{2,8},{3,9},{4,14},{5,15},{6,0},{7,1},{8,2},{9,3},{10,... | collective-permute-start | bytes 196616 | tf_op jit(solution)/shard_map/ppermute | solution.py:33
  38.2 3.8 %collective-permute-start.17 = (bf16[128,256]{1,0:T(8,128)(2,1)S(1)}, bf16[128,256]{1,0:T(8,128)(2,1)S(1)}, u32[]{:S(2)}, u32[]{:S(2)}) collective-permute-start(bf16[128,256]{1,0:T(8,128)(2,1)S(1)} %add_convert_fusion), channel_id=1, source_target_pairs={{0,6},{1,7},{2,8},{3,9},{4,14},{5,15},{6,0},{7,1},{8,2},{9,3},{10,... | collective-permute-start | bytes 196616 | tf_op jit(solution)/shard_map/ppermute | solution.py:33
  39.3 2.9 %collective-permute-start.18 = (bf16[256,256]{1,0:T(8,128)(2,1)S(1)}, bf16[256,256]{1,0:T(8,128)(2,1)S(1)}, u32[]{:S(2)}, u32[]{:S(2)}) collective-permute-start(bf16[256,256]{1,0:T(8,128)(2,1)S(1)} %pad_maximum_fusion.5), channel_id=1, source_target_pairs={{0,2},{1,3},{2,0},{3,1},{4,6},{5,7},{6,4},{7,5},{8,10},{9,11},{10,... | collective-permute-start | bytes 393224 | tf_op jit(solution)/shard_map/ppermute | solution.py:33
  40.9 1.3 %collective-permute-start.19 = (bf16[128,256]{1,0:T(8,128)(2,1)S(1)}, bf16[128,256]{1,0:T(8,128)(2,1)S(1)}, u32[]{:S(2)}, u32[]{:S(2)}) collective-permute-start(bf16[128,256]{1,0:T(8,128)(2,1)S(1)} %collective-permute-done.16), channel_id=1, source_target_pairs={{0,2},{1,3},{2,0},{3,1},{4,6},{5,7},{6,4},{7,5},{8,10},{9,11},{10,... | collective-permute-start | bytes 196616 | tf_op jit(solution)/shard_map/ppermute | solution.py:33
  42.0 1.3 %collective-permute-start.20 = (bf16[128,256]{1,0:T(8,128)(2,1)S(1)}, bf16[128,256]{1,0:T(8,128)(2,1)S(1)}, u32[]{:S(2)}, u32[]{:S(2)}) collective-permute-start(bf16[128,256]{1,0:T(8,128)(2,1)S(1)} %collective-permute-done.17), channel_id=1, source_target_pairs={{0,2},{1,3},{2,0},{3,1},{4,6},{5,7},{6,4},{7,5},{8,10},{9,11},{10,... | collective-permute-start | bytes 196616 | tf_op jit(solution)/shard_map/ppermute | solution.py:33

commit v8 on v7

--- a/solution.py
+++ b/solution.py
@@ -252,10 +252,11 @@
 
     steps = [((0, bit), (0, bit)) for bit in rep_bits[:-1]]
     steps += [((even, 0), (odd, 0)) for even, odd in zip(turned, hops, strict=True)]
-    for even, odd in steps[:-1]:
+    for at, (even, odd) in enumerate(steps[:-1]):
         parts = [grad.astype(BF16) for grad in grads]
         gots = [trade(part, even, odd) for part in parts]
-        gots[0], layer_out = barrier((gots[0], layer_out))
+        if at == 1:
+            gots[0], layer_out = barrier((gots[0], layer_out))
         grads = [part.astype(F32) + got.astype(F32) for part, got in zip(parts, gots, strict=True)]
     parts = [grad.astype(BF16) for grad in grads]
     gots = [trade(part, *steps[-1]) for part in parts]

time: 44.3 us -> 44.3 us (level)
  no operation moved by 1% of the time
where the time goes in v8:
time: 44.3 us; the launch traced here: 44.1 us
  starting transfers between devices  23.3 us (53%)
  waiting for transfers between devices  13.1 us (30%)
  Pallas kernels  3.72 us (8%)
  local copies, waits for them, and re-layouts  1.84 us (4%)
  other arithmetic  1.23 us (3%)
  between operations  0.86 us (2%)
    ppermute x21, starting transfers between devices, swap(): return lax.ppermute(x, ('node', 'rep'), pairs)  23.3 us
    ppermute x21, waiting for transfers between devices, swap(): return lax.ppermute(x, ('node', 'rep'), pairs)  13.1 us
    unnamed x13, local copies, waits for them, and re-layouts  1.65 us
    pallas_call x3, Pallas kernels, sums(): call(functools.partial(tile_sums, steps, prebuilt, len(columns), seed is...  1.57 us
  transfers between devices with their start and end apart: 21, of which 11 were waited for; matrix products, arithmetic and copies ran while one was open for 3% of the time, Pallas kernels for 7%

profile of v8, /device:TPU:0, one launch (start us, length us, event | category | flops | bytes accessed | tf_op | source)
XLA Modules:
  0.0 44.1 jit_solution(16871801550971346256)
XLA Ops:
  0.6 0.0 copy-start.2
  0.6 0.0 copy-start
  0.7 3.5 %collective-permute-start = (bf16[128,256]{1,0:T(8,128)(2,1)}, bf16[128,256]{1,0:T(8,128)(2,1)S(1)}, u32[]{:S(2)}, u32[]{:S(2)}) collective-permute-start(bf16[128,256]{1,0:T(8,128)(2,1)} %x_ref.1), channel_id=1, source_target_pairs={{0,18},{1,19},{2,8},{3,9},{4,14},{5,15},{6,20},{7,21},{8,2},{9,3},... | collective-permute-start | bytes 196616 | tf_op jit(solution)/shard_map/ppermute | solution.py:33
  4.2 0.9 %copy-done.4 = bf16[128,256]{1,0:T(8,128)(2,1)S(1)} copy-done((bf16[128,256]{1,0:T(8,128)(2,1)S(1)}, bf16[128,256]{1,0:T(8,128)(2,1)}, u32[]{:S(2)}) %copy-start.4) | copy-done | bytes 65560
  5.1 0.0 copy-done.2
  5.1 1.6 %collective-permute-start.2 = (bf16[256,256]{1,0:T(8,128)(2,1)S(1)}, bf16[256,256]{1,0:T(8,128)(2,1)S(1)}, u32[]{:S(2)}, u32[]{:S(2)}) collective-permute-start(bf16[256,256]{1,0:T(8,128)(2,1)S(1)} %pad_maximum_fusion.2), channel_id=1, source_target_pairs={{0,1},{1,0},{2,3},{3,2},{4,5},{5,4},{6,7},{7,6},{8,9},{9,8},{10,11... | collective-permute-start | bytes 393224 | tf_op jit(solution)/shard_map/ppermute | solution.py:33
  6.7 0.8 %copy.11 = s32[1,1,16,2]{3,2,1,0:T(8,128)S(1)} copy(s32[1,1,16,2]{2,3,1,0:T(2,128)} %param.9) | data formatting | bytes 256 | tf_op args[2]
  7.4 0.1 reshape_squeeze.3.rows
  7.5 0.0 collective-permute-done
  7.6 1.6 %collective-permute-start.1 = (bf16[256,128]{1,0:T(8,128)(2,1)S(1)}, bf16[256,128]{1,0:T(8,128)(2,1)S(1)}, u32[]{:S(2)}, u32[]{:S(2)}) collective-permute-start(bf16[256,128]{1,0:T(8,128)(2,1)S(1)} %pad_maximum_fusion.8), channel_id=1, source_target_pairs={{0,6},{1,7},{2,16},{3,17},{4,22},{5,23},{6,0},{7,1},{8,26},{9,27},... | collective-permute-start | bytes 196616 | tf_op jit(solution)/shard_map/ppermute | solution.py:33
  9.2 0.2 collective-permute-start.4
  9.4 0.1 pad_add_fusion.1
  9.5 0.1 pad_add_fusion.place
  9.5 1.8 %collective-permute-done.1 = bf16[256,128]{1,0:T(8,128)(2,1)S(1)} collective-permute-done((bf16[256,128]{1,0:T(8,128)(2,1)S(1)}, bf16[256,128]{1,0:T(8,128)(2,1)S(1)}, u32[]{:S(2)}, u32[]{:S(2)}) %collective-permute-start.1) | collective-permute-done | bytes 65568 | tf_op jit(solution)/shard_map/ppermute | solution.py:33
  11.3 0.1 broadcast_in_dim.19.flags
  11.4 0.0 collective-permute-done.2
  11.4 1.6 %collective-permute-start.3 = (bf16[512,128]{1,0:T(8,128)(2,1)S(1)}, bf16[512,128]{1,0:T(8,128)(2,1)S(1)}, u32[]{:S(2)}, u32[]{:S(2)}) collective-permute-start(bf16[512,128]{1,0:T(8,128)(2,1)S(1)} %pad_maximum_fusion.3), channel_id=1, source_target_pairs={{0,10},{1,11},{2,4},{3,5},{4,2},{5,3},{6,12},{7,13},{8,14},{9,15},... | collective-permute-start | bytes 393224 | tf_op jit(solution)/shard_map/ppermute | solution.py:33
  13.0 0.0 collective-permute-done.4
  13.1 0.0 copy-start.5
  13.1 1.2 %collective-permute-start.5 = (bf16[512,128]{1,0:T(8,128)(2,1)S(1)}, bf16[512,128]{1,0:T(8,128)(2,1)S(1)}, u32[]{:S(2)}, u32[]{:S(2)}) collective-permute-start(bf16[512,128]{1,0:T(8,128)(2,1)S(1)} %pad_maximum_fusion.4), channel_id=1, source_target_pairs={{0,10},{1,11},{2,4},{3,5},{4,2},{5,3},{6,12},{7,13},{8,14},{9,15},... | collective-permute-start | bytes 393224 | tf_op jit(solution)/shard_map/ppermute | solution.py:33
  14.2 0.0 copy-done
  14.2 0.8 %shard_map.95 = (bf16[2,512,256]{2,1,0:T(8,128)(2,1)S(1)}, bf16[2,512,256]{2,1,0:T(8,128)(2,1)S(1)}, bf16[4,512,256]{2,1,0:T(8,128)(2,1)S(1)}) custom-call(s32[4]{0:T(128)S(1)} %pad_add_fusion.place, s32[32]{0:T(128)S(1)} %reshape_squeeze.3.rows, s32[16]{0:T(128)S(1)} %bitcast.9, bf16[16,2,128,128]{3,2,1,0:T(8,128)(2,1)S(1)} %bitcast.8), custom_call_target="tpu_custom_call" | custom-call | bytes 6291456 | tf_op jit(solution)/shard_map/pallas_call | solution.py:196
  15.1 0.8 %collective-permute-done.3 = bf16[512,128]{1,0:T(8,128)(2,1)S(1)} collective-permute-done((bf16[512,128]{1,0:T(8,128)(2,1)S(1)}, bf16[512,128]{1,0:T(8,128)(2,1)S(1)}, u32[]{:S(2)}, u32[]{:S(2)}) %collective-permute-start.3) | collective-permute-done | bytes 131104 | tf_op jit(solution)/shard_map/ppermute | solution.py:33
  15.9 1.3 %collective-permute-start.6 = (bf16[1024,128]{1,0:T(8,128)(2,1)S(1)}, bf16[1024,128]{1,0:T(8,128)(2,1)S(1)}, u32[]{:S(2)}, u32[]{:S(2)}) collective-permute-start(bf16[1024,128]{1,0:T(8,128)(2,1)S(1)} %pad_maximum_fusion.refs_2_), channel_id=1, source_target_pairs={{0,2},{1,3},{2,0},{3,1},{4,6},{5,7},{6,4},{7,5},{8,10},{9,11},{10,... | collective-permute-start | bytes 786440 | tf_op jit(solution)/shard_map/ppermute | solution.py:33
  17.2 0.4 shard_map.96.refs_2_
  17.7 0.0 collective-permute-done.5
  17.7 1.2 %collective-permute-start.7 = (bf16[1024,128]{1,0:T(8,128)(2,1)S(1)}, bf16[1024,128]{1,0:T(8,128)(2,1)S(1)}, u32[]{:S(2)}, u32[]{:S(2)}) collective-permute-start(bf16[1024,128]{1,0:T(8,128)(2,1)S(1)} %pad_maximum_fusion.1.refs_3_), channel_id=1, source_target_pairs={{0,2},{1,3},{2,0},{3,1},{4,6},{5,7},{6,4},{7,5},{8,10},{9,11},{10,... | collective-permute-start | bytes 786440 | tf_op jit(solution)/shard_map/ppermute | solution.py:33
  18.9 0.0 collective-permute-done.6.refs_1_
  18.9 0.4 shard_map.97.total
  19.3 1.6 %collective-permute-start.9 = (bf16[256,128]{1,0:T(8,128)(2,1)S(1)}, bf16[256,128]{1,0:T(8,128)(2,1)S(1)}, u32[]{:S(2)}, u32[]{:S(2)}) collective-permute-start(bf16[256,128]{1,0:T(8,128)(2,1)S(1)} %shard_map.97.total), channel_id=1, source_target_pairs={{0,1},{1,0},{2,3},{3,2},{4,5},{5,4},{6,7},{7,6},{8,9},{9,8},{10,11... | collective-permute-start | bytes 196616 | tf_op jit(solution)/shard_map/ppermute | solution.py:33
  21.0 0.0 collective-permute-done.7.refs_4_
  21.0 0.7 %shard_map.98.total = bf16[256,128]{1,0:T(8,128)(2,1)S(1)} custom-call(bf16[2,512,256]{2,1,0:T(8,128)(2,1)S(1)} %get-tuple-element.52.refs_0_, bf16[2,512,256]{2,1,0:T(8,128)(2,1)S(1)} %get-tuple-element.53.refs_1_, bf16[4,512,256]{2,1,0:T(8,128)(2,1)S(1)} %get-tuple-element.54.refs_0_.refs_2_, bf16[1024,128]{1,0:T(8,128)(2,1)S(1)} %pad_maximum_fusion.1.refs_3_, ...), custom_call_target="tpu_custom_call" | custom-call | flops 268435456 | bytes 2097152 | tf_op jit(solution)/shard_map/pallas_call | solution.py:208
  21.7 0.0 copy-start.1
  21.7 0.0 copy-start.3
  21.7 0.7 %collective-permute-start.8 = (bf16[256,128]{1,0:T(8,128)(2,1)S(1)}, bf16[256,128]{1,0:T(8,128)(2,1)S(1)}, u32[]{:S(2)}, u32[]{:S(2)}) collective-permute-start(bf16[256,128]{1,0:T(8,128)(2,1)S(1)} %shard_map.98.total), channel_id=1, source_target_pairs={{0,1},{1,0},{2,3},{3,2},{4,5},{5,4},{6,7},{7,6},{8,9},{9,8},{10,11... | collective-permute-start | bytes 196616 | tf_op jit(solution)/shard_map/ppermute | solution.py:33
  22.4 1.2 %collective-permute-done.9.got = bf16[256,128]{1,0:T(8,128)(2,1)S(1)} collective-permute-done((bf16[256,128]{1,0:T(8,128)(2,1)S(1)}, bf16[256,128]{1,0:T(8,128)(2,1)S(1)}, u32[]{:S(2)}, u32[]{:S(2)}) %collective-permute-start.9) | collective-permute-done | bytes 65568 | tf_op jit(solution)/shard_map/ppermute | solution.py:33
  23.7 0.0 copy-done.3
  23.7 0.2 shard_map.99
  23.9 2.1 %collective-permute-done.8.got = bf16[256,128]{1,0:T(8,128)(2,1)S(1)} collective-permute-done((bf16[256,128]{1,0:T(8,128)(2,1)S(1)}, bf16[256,128]{1,0:T(8,128)(2,1)S(1)}, u32[]{:S(2)}, u32[]{:S(2)}) %collective-permute-start.8) | collective-permute-done | bytes 65568 | tf_op jit(solution)/shard_map/ppermute | solution.py:33
  26.0 0.5 %shard_map.100 = (bf16[128,256]{1,0:T(8,128)(2,1)S(1)}, f32[128,256]{1,0:T(8,128)S(1)}, f32[128,256]{1,0:T(8,128)S(1)}, f32[128,256]{1,0:T(8,128)S(1)}, f32[128,256]{1,0:T(8,128)S(1)}) custom-call(s32[2,256]{1,0:T(2,128)S(1)} %broadcast_in_dim.19.flags, bf16[256,128]{1,0:T(8,128)(2,1)S(1)} %shard_map.98.total, ...), custom_call_target="tpu_custom_call" | custom-call | flops 83886080 | bytes 1048576 | tf_op jit(solution)/shard_map/pallas_call | solution.py:243
  26.5 0.1 collective-permute-start.10
  26.6 0.6 %shard_map.101 = bf16[128,256]{1,0:T(8,128)(2,1)} custom-call(bf16[128,256]{1,0:T(8,128)(2,1)S(1)} %get-tuple-element.66.x_ref), custom_call_target="tpu_custom_call" | custom-call | bytes 131072 | tf_op jit(solution)/shard_map/pallas_call | solution.py:251
  27.2 0.5 %collective-permute-start.13 = (f32[128,256]{1,0:T(8,128)S(1)}, f32[128,256]{1,0:T(8,128)S(1)}, u32[]{:S(2)}, u32[]{:S(2)}) collective-permute-start(f32[128,256]{1,0:T(8,128)S(1)} %get-tuple-element.70), channel_id=1, source_target_pairs={{0,2},{1,3},{2,0},{3,1},{4,6},{5,7},{6,4},{7,5},{8,10},{9,11},{10,... | collective-permute-start | bytes 393224 | tf_op jit(solution)/shard_map/ppermute | solution.py:33
  27.7 0.2 collective-permute-done.10
  27.9 0.1 collective-permute-start.11
  28.0 0.7 %collective-permute-done.13 = f32[128,256]{1,0:T(8,128)S(1)} collective-permute-done((f32[128,256]{1,0:T(8,128)S(1)}, f32[128,256]{1,0:T(8,128)S(1)}, u32[]{:S(2)}, u32[]{:S(2)}) %collective-permute-start.13) | collective-permute-done | bytes 131104 | tf_op jit(solution)/shard_map/ppermute | solution.py:33
  28.7 1.1 %collective-permute-start.14 = (bf16[128,256]{1,0:T(8,128)(2,1)S(1)}, bf16[128,256]{1,0:T(8,128)(2,1)S(1)}, u32[]{:S(2)}, u32[]{:S(2)}) collective-permute-start(bf16[128,256]{1,0:T(8,128)(2,1)S(1)} %add_convert_fusion.2), channel_id=1, source_target_pairs={{0,10},{1,11},{2,16},{3,17},{4,22},{5,23},{6,12},{7,13},{8,26},{9,... | collective-permute-start | bytes 196616 | tf_op jit(solution)/shard_map/ppermute | solution.py:33
  29.8 1.9 %collective-permute-done.11 = bf16[128,256]{1,0:T(8,128)(2,1)S(1)} collective-permute-done((bf16[128,256]{1,0:T(8,128)(2,1)S(1)}, bf16[128,256]{1,0:T(8,128)(2,1)S(1)}, u32[]{:S(2)}, u32[]{:S(2)}) %collective-permute-start.11) | collective-permute-done | bytes 65568 | tf_op jit(solution)/shard_map/ppermute | solution.py:33
  31.7 1.8 %collective-permute-start.12 = (bf16[128,256]{1,0:T(8,128)(2,1)S(1)}, bf16[128,256]{1,0:T(8,128)(2,1)S(1)}, u32[]{:S(2)}, u32[]{:S(2)}) collective-permute-start(bf16[128,256]{1,0:T(8,128)(2,1)S(1)} %add_convert_fusion.4), channel_id=1, source_target_pairs={{0,18},{1,19},{2,4},{3,5},{4,2},{5,3},{6,20},{7,21},{8,14},{9,15},... | collective-permute-start | bytes 196616 | tf_op jit(solution)/shard_map/ppermute | solution.py:33
  33.5 0.0 collective-permute-done.14
  33.5 2.0 %collective-permute-start.15 = (bf16[128,256]{1,0:T(8,128)(2,1)S(1)}, bf16[128,256]{1,0:T(8,128)(2,1)S(1)}, u32[]{:S(2)}, u32[]{:S(2)}) collective-permute-start(bf16[128,256]{1,0:T(8,128)(2,1)S(1)} %add_convert_fusion.1), channel_id=1, source_target_pairs={{0,18},{1,19},{2,4},{3,5},{4,2},{5,3},{6,20},{7,21},{8,14},{9,15},... | collective-permute-start | bytes 196616 | tf_op jit(solution)/shard_map/ppermute | solution.py:33
  35.5 1.6 %collective-permute-done.12 = bf16[128,256]{1,0:T(8,128)(2,1)S(1)} collective-permute-done((bf16[128,256]{1,0:T(8,128)(2,1)S(1)}, bf16[128,256]{1,0:T(8,128)(2,1)S(1)}, u32[]{:S(2)}, u32[]{:S(2)}) %collective-permute-start.12) | collective-permute-done | bytes 65568 | tf_op jit(solution)/shard_map/ppermute | solution.py:33
  37.1 1.1 %collective-permute-start.16 = (bf16[128,256]{1,0:T(8,128)(2,1)S(1)}, bf16[128,256]{1,0:T(8,128)(2,1)S(1)}, u32[]{:S(2)}, u32[]{:S(2)}) collective-permute-start(bf16[128,256]{1,0:T(8,128)(2,1)S(1)} %add_convert_fusion.3), channel_id=1, source_target_pairs={{0,6},{1,7},{2,8},{3,9},{4,14},{5,15},{6,0},{7,1},{8,2},{9,3},{10,... | collective-permute-start | bytes 196616 | tf_op jit(solution)/shard_map/ppermute | solution.py:33
  38.2 0.0 collective-permute-done.15
  38.2 1.0 %collective-permute-start.17 = (bf16[128,256]{1,0:T(8,128)(2,1)S(1)}, bf16[128,256]{1,0:T(8,128)(2,1)S(1)}, u32[]{:S(2)}, u32[]{:S(2)}) collective-permute-start(bf16[128,256]{1,0:T(8,128)(2,1)S(1)} %add_convert_fusion), channel_id=1, source_target_pairs={{0,6},{1,7},{2,8},{3,9},{4,14},{5,15},{6,0},{7,1},{8,2},{9,3},{10,... | collective-permute-start | bytes 196616 | tf_op jit(solution)/shard_map/ppermute | solution.py:33
  39.3 0.9 %collective-permute-start.18 = (bf16[256,256]{1,0:T(8,128)(2,1)S(1)}, bf16[256,256]{1,0:T(8,128)(2,1)S(1)}, u32[]{:S(2)}, u32[]{:S(2)}) collective-permute-start(bf16[256,256]{1,0:T(8,128)(2,1)S(1)} %pad_maximum_fusion.5), channel_id=1, source_target_pairs={{0,2},{1,3},{2,0},{3,1},{4,6},{5,7},{6,4},{7,5},{8,10},{9,11},{10,... | collective-permute-start | bytes 393224 | tf_op jit(solution)/shard_map/ppermute | solution.py:33
  40.1 0.7 %collective-permute-done.16 = bf16[128,256]{1,0:T(8,128)(2,1)S(1)} collective-permute-done((bf16[128,256]{1,0:T(8,128)(2,1)S(1)}, bf16[128,256]{1,0:T(8,128)(2,1)S(1)}, u32[]{:S(2)}, u32[]{:S(2)}) %collective-permute-start.16) | collective-permute-done | bytes 65568 | tf_op jit(solution)/shard_map/ppermute | solution.py:33
  40.9 0.1 collective-permute-start.19
  41.0 1.0 %collective-permute-done.17 = bf16[128,256]{1,0:T(8,128)(2,1)S(1)} collective-permute-done((bf16[128,256]{1,0:T(8,128)(2,1)S(1)}, bf16[128,256]{1,0:T(8,128)(2,1)S(1)}, u32[]{:S(2)}, u32[]{:S(2)}) %collective-permute-start.17) | collective-permute-done | bytes 65568 | tf_op jit(solution)/shard_map/ppermute | solution.py:33
  42.0 0.1 collective-permute-start.20
  42.1 0.0 collective-permute-done.18
  42.1 0.0 collective-permute-done.19
  42.1 1.1 %collective-permute-done.20 = bf16[128,256]{1,0:T(8,128)(2,1)S(1)} collective-permute-done((bf16[128,256]{1,0:T(8,128)(2,1)S(1)}, bf16[128,256]{1,0:T(8,128)(2,1)S(1)}, u32[]{:S(2)}, u32[]{:S(2)}) %collective-permute-start.20) | collective-permute-done | bytes 65568 | tf_op jit(solution)/shard_map/ppermute | solution.py:33
  43.2 0.9 %fusion = (f32[256,256]{1,0:T(8,128)}, f32[256,256]{1,0:T(8,128)}) fusion(bf16[256,256]{1,0:T(8,128)(2,1)S(1)} %collective-permute-done.18, pred[256]{0:T(512)(128)(4,1)S(1)} %compare_reduce_fusion, bf16[128,256]{1,0:T(8,128)(2,1)S(1)} %collective-permute-done.20, bf16[128,256]{1,0:T(8,128)(2,1)S(1)} %collective-permute-done.19, ...), kind=kLoop, calls=%fused_computation.4 | loop fusion | flops 1114112 | bytes 1048832 | tf_op jit(solution)/shard_map/jit(_where)/select_n | solution.py:270
  (21 shorter events, 0.3 us)
Async XLA Ops:
  0.6 4.4 %copy-start.2 = (bf16[128,256]{1,0:T(8,128)(2,1)S(1)}, bf16[128,256]{1,0:T(8,128)(2,1)}, u32[]{:S(2)}) copy-start(bf16[128,256]{1,0:T(8,128)(2,1)} %out_grad.1) | copy-start | bytes 196612
  0.6 13.6 %copy-start = (bf16[1,1,16,2,128,128]{5,4,3,2,1,0:T(8,128)(2,1)S(1)}, bf16[1,1,16,2,128,128]{5,4,3,2,1,0:T(8,128)(2,1)}, u32[]{:S(2)}) copy-start(bf16[1,1,16,2,128,128]{5,4,3,2,1,0:T(8,128)(2,1)} %param.8) | copy-start | bytes 3145732
  0.7 6.8 %collective-permute-start = (bf16[128,256]{1,0:T(8,128)(2,1)}, bf16[128,256]{1,0:T(8,128)(2,1)S(1)}, u32[]{:S(2)}, u32[]{:S(2)}) collective-permute-start(bf16[128,256]{1,0:T(8,128)(2,1)} %x_ref.1), channel_id=1, source_target_pairs={{0,18},{1,19},{2,8},{3,9},{4,14},{5,15},{6,20},{7,21},{8,2},{9,3},... | collective-permute-start | bytes 196616 | tf_op jit(solution)/shard_map/ppermute | solution.py:33
  4.2 0.9 %copy-start.4 = (bf16[128,256]{1,0:T(8,128)(2,1)S(1)}, bf16[128,256]{1,0:T(8,128)(2,1)}, u32[]{:S(2)}) copy-start(bf16[128,256]{1,0:T(8,128)(2,1)} %x_ref.1) | copy-start | bytes 196612
  5.1 6.3 %collective-permute-start.2 = (bf16[256,256]{1,0:T(8,128)(2,1)S(1)}, bf16[256,256]{1,0:T(8,128)(2,1)S(1)}, u32[]{:S(2)}, u32[]{:S(2)}) collective-permute-start(bf16[256,256]{1,0:T(8,128)(2,1)S(1)} %pad_maximum_fusion.2), channel_id=1, source_target_pairs={{0,1},{1,0},{2,3},{3,2},{4,5},{5,4},{6,7},{7,6},{8,9},{9,8},{10,11... | collective-permute-start | bytes 393224 | tf_op jit(solution)/shard_map/ppermute | solution.py:33
  7.6 3.8 %collective-permute-start.1 = (bf16[256,128]{1,0:T(8,128)(2,1)S(1)}, bf16[256,128]{1,0:T(8,128)(2,1)S(1)}, u32[]{:S(2)}, u32[]{:S(2)}) collective-permute-start(bf16[256,128]{1,0:T(8,128)(2,1)S(1)} %pad_maximum_fusion.8), channel_id=1, source_target_pairs={{0,6},{1,7},{2,16},{3,17},{4,22},{5,23},{6,0},{7,1},{8,26},{9,27},... | collective-permute-start | bytes 196616 | tf_op jit(solution)/shard_map/ppermute | solution.py:33
  9.2 3.9 %collective-permute-start.4 = (bf16[256,128]{1,0:T(8,128)(2,1)S(1)}, bf16[256,128]{1,0:T(8,128)(2,1)S(1)}, u32[]{:S(2)}, u32[]{:S(2)}) collective-permute-start(bf16[256,128]{1,0:T(8,128)(2,1)S(1)} %pad_maximum_fusion.9), channel_id=1, source_target_pairs={{0,6},{1,7},{2,16},{3,17},{4,22},{5,23},{6,0},{7,1},{8,26},{9,27},... | collective-permute-start | bytes 196616 | tf_op jit(solution)/shard_map/ppermute | solution.py:33
  11.4 4.5 %collective-permute-start.3 = (bf16[512,128]{1,0:T(8,128)(2,1)S(1)}, bf16[512,128]{1,0:T(8,128)(2,1)S(1)}, u32[]{:S(2)}, u32[]{:S(2)}) collective-permute-start(bf16[512,128]{1,0:T(8,128)(2,1)S(1)} %pad_maximum_fusion.3), channel_id=1, source_target_pairs={{0,10},{1,11},{2,4},{3,5},{4,2},{5,3},{6,12},{7,13},{8,14},{9,15},... | collective-permute-start | bytes 393224 | tf_op jit(solution)/shard_map/ppermute | solution.py:33
  13.1 1.2 %copy-start.5 = (s32[1,1,16]{2,1,0:T(1,128)S(1)}, s32[1,1,16]{2,1,0:T(1,128)}, u32[]{:S(2)}) copy-start(s32[1,1,16]{2,1,0:T(1,128)} %param.10) | copy-start | bytes 196
  13.1 4.6 %collective-permute-start.5 = (bf16[512,128]{1,0:T(8,128)(2,1)S(1)}, bf16[512,128]{1,0:T(8,128)(2,1)S(1)}, u32[]{:S(2)}, u32[]{:S(2)}) collective-permute-start(bf16[512,128]{1,0:T(8,128)(2,1)S(1)} %pad_maximum_fusion.4), channel_id=1, source_target_pairs={{0,10},{1,11},{2,4},{3,5},{4,2},{5,3},{6,12},{7,13},{8,14},{9,15},... | collective-permute-start | bytes 393224 | tf_op jit(solution)/shard_map/ppermute | solution.py:33
  15.9 3.0 %collective-permute-start.6 = (bf16[1024,128]{1,0:T(8,128)(2,1)S(1)}, bf16[1024,128]{1,0:T(8,128)(2,1)S(1)}, u32[]{:S(2)}, u32[]{:S(2)}) collective-permute-start(bf16[1024,128]{1,0:T(8,128)(2,1)S(1)} %pad_maximum_fusion.refs_2_), channel_id=1, source_target_pairs={{0,2},{1,3},{2,0},{3,1},{4,6},{5,7},{6,4},{7,5},{8,10},{9,11},{10,... | collective-permute-start | bytes 786440 | tf_op jit(solution)/shard_map/ppermute | solution.py:33
  17.7 3.3 %collective-permute-start.7 = (bf16[1024,128]{1,0:T(8,128)(2,1)S(1)}, bf16[1024,128]{1,0:T(8,128)(2,1)S(1)}, u32[]{:S(2)}, u32[]{:S(2)}) collective-permute-start(bf16[1024,128]{1,0:T(8,128)(2,1)S(1)} %pad_maximum_fusion.1.refs_3_), channel_id=1, source_target_pairs={{0,2},{1,3},{2,0},{3,1},{4,6},{5,7},{6,4},{7,5},{8,10},{9,11},{10,... | collective-permute-start | bytes 786440 | tf_op jit(solution)/shard_map/ppermute | solution.py:33
  19.3 4.3 %collective-permute-start.9 = (bf16[256,128]{1,0:T(8,128)(2,1)S(1)}, bf16[256,128]{1,0:T(8,128)(2,1)S(1)}, u32[]{:S(2)}, u32[]{:S(2)}) collective-permute-start(bf16[256,128]{1,0:T(8,128)(2,1)S(1)} %shard_map.97.total), channel_id=1, source_target_pairs={{0,1},{1,0},{2,3},{3,2},{4,5},{5,4},{6,7},{7,6},{8,9},{9,8},{10,11... | collective-permute-start | bytes 196616 | tf_op jit(solution)/shard_map/ppermute | solution.py:33
  21.7 2.0 %copy-start.1 = (bf16[256,256]{1,0:T(8,128)(2,1)S(1)}, bf16[256,256]{1,0:T(8,128)(2,1)}, u32[]{:S(2)}) copy-start(bf16[256,256]{1,0:T(8,128)(2,1)} %w_neigh.3) | copy-start | bytes 393220
  21.7 2.0 %copy-start.3 = (bf16[256,256]{1,0:T(8,128)(2,1)S(1)}, bf16[256,256]{1,0:T(8,128)(2,1)}, u32[]{:S(2)}) copy-start(bf16[256,256]{1,0:T(8,128)(2,1)} %w_self.1) | copy-start | bytes 393220
  21.7 4.3 %collective-permute-start.8 = (bf16[256,128]{1,0:T(8,128)(2,1)S(1)}, bf16[256,128]{1,0:T(8,128)(2,1)S(1)}, u32[]{:S(2)}, u32[]{:S(2)}) collective-permute-start(bf16[256,128]{1,0:T(8,128)(2,1)S(1)} %shard_map.98.total), channel_id=1, source_target_pairs={{0,1},{1,0},{2,3},{3,2},{4,5},{5,4},{6,7},{7,6},{8,9},{9,8},{10,11... | collective-permute-start | bytes 196616 | tf_op jit(solution)/shard_map/ppermute | solution.py:33
  26.5 1.4 %collective-permute-start.10 = (f32[128,256]{1,0:T(8,128)S(1)}, f32[128,256]{1,0:T(8,128)S(1)}, u32[]{:S(2)}, u32[]{:S(2)}) collective-permute-start(f32[128,256]{1,0:T(8,128)S(1)} %get-tuple-element.65), channel_id=1, source_target_pairs={{0,2},{1,3},{2,0},{3,1},{4,6},{5,7},{6,4},{7,5},{8,10},{9,11},{10,... | collective-permute-start | bytes 393224 | tf_op jit(solution)/shard_map/ppermute | solution.py:33
  27.2 1.5 %collective-permute-start.13 = (f32[128,256]{1,0:T(8,128)S(1)}, f32[128,256]{1,0:T(8,128)S(1)}, u32[]{:S(2)}, u32[]{:S(2)}) collective-permute-start(f32[128,256]{1,0:T(8,128)S(1)} %get-tuple-element.70), channel_id=1, source_target_pairs={{0,2},{1,3},{2,0},{3,1},{4,6},{5,7},{6,4},{7,5},{8,10},{9,11},{10,... | collective-permute-start | bytes 393224 | tf_op jit(solution)/shard_map/ppermute | solution.py:33
  27.9 3.8 %collective-permute-start.11 = (bf16[128,256]{1,0:T(8,128)(2,1)S(1)}, bf16[128,256]{1,0:T(8,128)(2,1)S(1)}, u32[]{:S(2)}, u32[]{:S(2)}) collective-permute-start(bf16[128,256]{1,0:T(8,128)(2,1)S(1)} %add_convert_fusion.5), channel_id=1, source_target_pairs={{0,10},{1,11},{2,16},{3,17},{4,22},{5,23},{6,12},{7,13},{8,26},{9,... | collective-permute-start | bytes 196616 | tf_op jit(solution)/shard_map/ppermute | solution.py:33
  28.7 4.8 %collective-permute-start.14 = (bf16[128,256]{1,0:T(8,128)(2,1)S(1)}, bf16[128,256]{1,0:T(8,128)(2,1)S(1)}, u32[]{:S(2)}, u32[]{:S(2)}) collective-permute-start(bf16[128,256]{1,0:T(8,128)(2,1)S(1)} %add_convert_fusion.2), channel_id=1, source_target_pairs={{0,10},{1,11},{2,16},{3,17},{4,22},{5,23},{6,12},{7,13},{8,26},{9,... | collective-permute-start | bytes 196616 | tf_op jit(solution)/shard_map/ppermute | solution.py:33
  31.7 5.4 %collective-permute-start.12 = (bf16[128,256]{1,0:T(8,128)(2,1)S(1)}, bf16[128,256]{1,0:T(8,128)(2,1)S(1)}, u32[]{:S(2)}, u32[]{:S(2)}) collective-permute-start(bf16[128,256]{1,0:T(8,128)(2,1)S(1)} %add_convert_fusion.4), channel_id=1, source_target_pairs={{0,18},{1,19},{2,4},{3,5},{4,2},{5,3},{6,20},{7,21},{8,14},{9,15},... | collective-permute-start | bytes 196616 | tf_op jit(solution)/shard_map/ppermute | solution.py:33
  33.5 4.7 %collective-permute-start.15 = (bf16[128,256]{1,0:T(8,128)(2,1)S(1)}, bf16[128,256]{1,0:T(8,128)(2,1)S(1)}, u32[]{:S(2)}, u32[]{:S(2)}) collective-permute-start(bf16[128,256]{1,0:T(8,128)(2,1)S(1)} %add_convert_fusion.1), channel_id=1, source_target_pairs={{0,18},{1,19},{2,4},{3,5},{4,2},{5,3},{6,20},{7,21},{8,14},{9,15},... | collective-permute-start | bytes 196616 | tf_op jit(solution)/shard_map/ppermute | solution.py:33
  37.1 3.8 %collective-permute-start.16 = (bf16[128,256]{1,0:T(8,128)(2,1)S(1)}, bf16[128,256]{1,0:T(8,128)(2,1)S(1)}, u32[]{:S(2)}, u32[]{:S(2)}) collective-permute-start(bf16[128,256]{1,0:T(8,128)(2,1)S(1)} %add_convert_fusion.3), channel_id=1, source_target_pairs={{0,6},{1,7},{2,8},{3,9},{4,14},{5,15},{6,0},{7,1},{8,2},{9,3},{10,... | collective-permute-start | bytes 196616 | tf_op jit(solution)/shard_map/ppermute | solution.py:33
  38.2 3.8 %collective-permute-start.17 = (bf16[128,256]{1,0:T(8,128)(2,1)S(1)}, bf16[128,256]{1,0:T(8,128)(2,1)S(1)}, u32[]{:S(2)}, u32[]{:S(2)}) collective-permute-start(bf16[128,256]{1,0:T(8,128)(2,1)S(1)} %add_convert_fusion), channel_id=1, source_target_pairs={{0,6},{1,7},{2,8},{3,9},{4,14},{5,15},{6,0},{7,1},{8,2},{9,3},{10,... | collective-permute-start | bytes 196616 | tf_op jit(solution)/shard_map/ppermute | solution.py:33
  39.3 2.9 %collective-permute-start.18 = (bf16[256,256]{1,0:T(8,128)(2,1)S(1)}, bf16[256,256]{1,0:T(8,128)(2,1)S(1)}, u32[]{:S(2)}, u32[]{:S(2)}) collective-permute-start(bf16[256,256]{1,0:T(8,128)(2,1)S(1)} %pad_maximum_fusion.5), channel_id=1, source_target_pairs={{0,2},{1,3},{2,0},{3,1},{4,6},{5,7},{6,4},{7,5},{8,10},{9,11},{10,... | collective-permute-start | bytes 393224 | tf_op jit(solution)/shard_map/ppermute | solution.py:33
  40.9 1.3 %collective-permute-start.19 = (bf16[128,256]{1,0:T(8,128)(2,1)S(1)}, bf16[128,256]{1,0:T(8,128)(2,1)S(1)}, u32[]{:S(2)}, u32[]{:S(2)}) collective-permute-start(bf16[128,256]{1,0:T(8,128)(2,1)S(1)} %collective-permute-done.16), channel_id=1, source_target_pairs={{0,2},{1,3},{2,0},{3,1},{4,6},{5,7},{6,4},{7,5},{8,10},{9,11},{10,... | collective-permute-start | bytes 196616 | tf_op jit(solution)/shard_map/ppermute | solution.py:33
  42.0 1.3 %collective-permute-start.20 = (bf16[128,256]{1,0:T(8,128)(2,1)S(1)}, bf16[128,256]{1,0:T(8,128)(2,1)S(1)}, u32[]{:S(2)}, u32[]{:S(2)}) collective-permute-start(bf16[128,256]{1,0:T(8,128)(2,1)S(1)} %collective-permute-done.17), channel_id=1, source_target_pairs={{0,2},{1,3},{2,0},{3,1},{4,6},{5,7},{6,4},{7,5},{8,10},{9,11},{10,... | collective-permute-start | bytes 196616 | tf_op jit(solution)/shard_map/ppermute | solution.py:33
